TPU v7x, 32 devices: a whole 2x2x4 slice. The times are simulated.
32 devices in a mesh: seg: 8 (over z, y), grp: 4 (over x, core).
Axes of the slice: x: 2, y: 2, z: 4, core: 2. Of those that a mesh axis runs over, the one named last changes fastest.
Arguments:
- basis: float32 [8, 768, 128], P(None, ('seg', 'grp')), may hold values from -6 to 6
- coords: float32 [768, 3, 128], P(('seg', 'grp')), may hold values from 0 to 4
- areas: float32 [768, 128], P(('seg', 'grp')), may hold values from 0.5 to 2
- p2m: bfloat16 [768, 121, 128], P(('seg', 'grp')), may hold values from -0.5 to 0.5
- l2p: bfloat16 [768, 128, 121], P(('seg', 'grp')), may hold values from -0.5 to 0.5
- m2l: bfloat16 [316, 121, 121], replicated, may hold values from -0.0390625 to 0.0390625
- counts: int32 [32], P(('seg', 'grp')), may hold values from 8 to 24
- near_list: int32 [768, 27], P(('seg', 'grp')), may hold values from 0 to 287
- far_list: int32 [768, 189], P(('seg', 'grp')), may hold values from 0 to 287
- far_offset: int32 [768, 189], P(('seg', 'grp')), may hold values from 0 to 315
Outputs:
- new_vector: float32 [768, 128], P(('seg', 'grp'))
- hessenberg: float32 [9], replicated
Inputs may be any that keep to these rules, and one draw needn't show every extreme that they name: `near_list`: window indices follow the rule of the steps; entries may name empty slots or leaves beyond the ends of the curve, which contribute nothing. A device's live leaves are its first counts slots.
All inputs are finite; a program needn't handle non-finite values.
Results may differ from a plain program's by a relative error of at most 0.0012.
Values sent between devices are 32-bit elements; how exact they have to be, the bound alone decides.
No kernel may reach another device: no remote copies, remote signals or barrier semaphores. Data moves between devices by JAX's collectives and lax.ppermute only.
A program may use at most 64 MiB of HBM per device.

v0:
```python
import jax
import jax.numpy as jnp
from jax import lax
from jax.sharding import PartitionSpec as P

four_pi = 12.566370614359172
epsilon = 1e-06
highest = lax.Precision.HIGHEST


def with_halo(cells, sides, width):
    for axis, dim in sides:
        count = lax.axis_size(axis)
        ends = count - 1
        head = lax.slice_in_dim(cells, 0, width, axis=dim)
        tail = lax.slice_in_dim(cells, cells.shape[dim] - width, cells.shape[dim], axis=dim)
        cells = jnp.concatenate(
            [
                lax.ppermute(tail, axis, [(i, (i + 1) % count) for i in range(ends)]),
                cells,
                lax.ppermute(head, axis, [((i + 1) % count, i) for i in range(ends)]),
            ],
            axis=dim,
        )
    return cells


def near_field(coords, wide_panels, near_list):
    leaf_count = coords.shape[0]
    panels = coords.shape[2]

    def near_step(running, column):
        source = jnp.take(wide_panels, column, axis=0)
        square = jnp.zeros((leaf_count, panels, panels), jnp.float32)
        for component in range(3):
            spread = coords[:, component, :, None] - source[:, component, None, :]
            square = square + spread * spread
        source_area = source[:, 3, None, :]
        kernel = source_area / (four_pi * jnp.sqrt(square + source_area))
        return (running + jnp.sum(kernel * source[:, 4, None, :], axis=2), None)

    result, _ = lax.scan(near_step, jnp.zeros((leaf_count, panels), jnp.float32), near_list.T)
    return result


def far_field(wide_poles, m2l, far_list, far_offset):
    offsets = m2l.shape[0]
    gathered = jnp.take(wide_poles, far_list, axis=0)
    offset_hot = (
        far_offset[:, :, None] == lax.broadcasted_iota(jnp.int32, (1, 1, offsets), 2)
    ).astype(jnp.float32)
    summed = jnp.einsum("tfo,tfk->tok", offset_hot, gathered, precision=highest)
    return jnp.einsum("tok,oik->ti", summed, m2l.astype(jnp.float32), precision=highest)


def on_device(basis, coords, areas, p2m, l2p, m2l, counts, near_list, far_list, far_offset):
    leaf_count, panels = areas.shape
    krylov = basis.shape[0]
    slots = lax.broadcasted_iota(jnp.int32, (leaf_count, 1), 0)
    live_mask = (slots < counts[0]).astype(jnp.float32)
    current = basis[krylov - 1] * live_mask
    rounded = current.astype(jnp.bfloat16)
    multipoles = jnp.einsum("lkp,lp->lk", p2m, rounded, preferred_element_type=jnp.float32)
    packed = jnp.concatenate([coords, areas[:, None, :], current[:, None, :]], axis=1)
    group_panels, group_poles = (
        lax.all_gather(packed, "grp", axis=0, tiled=True),
        lax.all_gather(multipoles, "grp", axis=0, tiled=True),
    )
    wide_panels, wide_poles = (
        with_halo(group_panels, (("seg", 0),), group_panels.shape[0]),
        with_halo(group_poles, (("seg", 0),), group_panels.shape[0]),
    )
    nearby = near_field(coords, wide_panels, near_list)
    local = far_field(wide_poles, m2l, far_list, far_offset).astype(jnp.bfloat16)
    distant = jnp.einsum("lpk,lk->lp", l2p, local, preferred_element_type=jnp.float32)
    image = (0.5 * current + nearby + distant) * live_mask
    masked = basis * live_mask[None]
    products = jnp.einsum("jlp,lp->j", masked, image, precision=highest)
    live_panels = jnp.sum(live_mask) * panels
    gram = jnp.einsum("ilp,jlp->ij", masked, masked, precision=highest)
    summed, population, gram_sum, energy = lax.psum(
        (products, live_panels, gram, jnp.sum(image * image)), ("seg", "grp")
    )
    coefficients = summed / population
    residue = image - jnp.einsum("j,jlp->lp", coefficients, masked, precision=highest)
    curvature = jnp.dot(
        coefficients, jnp.dot(gram_sum, coefficients, precision=highest), precision=highest
    )
    squares = energy - 2.0 * jnp.dot(coefficients, summed, precision=highest) + curvature
    scale = jnp.sqrt(squares / population + epsilon)
    return (residue / scale, jnp.concatenate([coefficients, scale[None]]))


def solution(mesh):
    placed = (
        P(None, ("seg", "grp"), None),
        P(("seg", "grp"), None, None),
        P(("seg", "grp"), None),
        P(("seg", "grp"), None, None),
        P(("seg", "grp"), None, None),
        P(),
        P(("seg", "grp")),
        P(("seg", "grp"), None),
        P(("seg", "grp"), None),
        P(("seg", "grp"), None),
    )
    return jax.shard_map(
        on_device,
        mesh=mesh,
        in_specs=placed,
        out_specs=(P(("seg", "grp"), None), P()),
        check_vma=False,
    )
```

profile of v0, /device:TPU:0, one launch (start us, length us, event | category | flops | bytes accessed | tf_op | source)
XLA Modules:
  0.0 204.8 jit_solution(10559210306540188368)
XLA Ops:
  3.8 6.2 %all_gather.7 = f32[96,121]{1,0:T(8,128)S(1)} all-gather(f32[24,121]{1,0:T(8,128)S(1)} %bitcast.98), channel_id=1, replica_groups=mesh['seg'=8,'grp'=4] {'grp'}, dimensions={0}, use_global_device_ids=true | all-gather | bytes 58080 | tf_op jit(solution)/shard_map/all_gather | solution.py:67
  10.0 3.9 %collective-permute-start.2 = (f32[96,121]{1,0:T(8,128)S(1)}, f32[96,121]{1,0:T(8,128)S(1)}, u32[]{:S(2)}, u32[]{:S(2)}) collective-permute-start(f32[96,121]{1,0:T(8,128)S(1)} %all_gather.7), channel_id=1, source_target_pairs={{0,4},{4,8},{8,12},{12,16},{16,20},{20,24},{24,28},{1,5},{5,9},{9,... | collective-permute-start | bytes 139400 | tf_op jit(solution)/shard_map/ppermute | solution.py:19
  16.8 6.2 %all_gather.6 = f32[96,5,128]{2,0,1:T(8,128)} all-gather(f32[24,5,128]{2,0,1:T(8,128)S(1)} %pad_maximum_fusion.2), channel_id=1, replica_groups=mesh['seg'=8,'grp'=4] {'grp'}, dimensions={0}, use_global_device_ids=true | all-gather | bytes 307200 | tf_op jit(solution)/shard_map/all_gather | solution.py:66
  23.0 5.2 %collective-permute-start = (f32[96,5,128]{2,0,1:T(8,128)}, f32[96,5,128]{2,0,1:T(8,128)}, u32[]{:S(2)}, u32[]{:S(2)}) collective-permute-start(f32[96,5,128]{2,0,1:T(8,128)} %all_gather.6), channel_id=1, source_target_pairs={{0,4},{4,8},{8,12},{12,16},{16,20},{20,24},{24,28},{1,5},{5,9},{9,... | collective-permute-start | bytes 737288 | tf_op jit(solution)/shard_map/ppermute | solution.py:19
  34.0 7.4 %gather_fusion.1 = f32[4536,121]{1,0:T(8,128)S(1)} fusion(f32[288,121]{1,0:T(8,128)S(1)} %pad_maximum_fusion.1, s32[5120]{0:T(1024)S(1)} %pad_clamp_fusion.1), kind=kCustom, calls=%fused_computation.1 | custom fusion | bytes 4408992 | tf_op jit(solution)/shard_map/jit(_take)/gather | solution.py:48
  43.0 10.6 %fusion.3 = f32[24,316,121]{2,1,0:T(8,128)S(1)} fusion(s32[24,189]{1,0:T(8,128)S(1)} %copy-done.2, f32[24,189,121]{2,1,0:T(8,128)} %reshape.102, pred[24,189]{1,0:T(8,128)(4,1)S(1)} %compare_and_fusion.1), kind=kOutput, calls=%fused_computation.17 | convolution fusion | flops 2083244160 | bytes 5888760 | tf_op jit(solution)/shard_map/tfo,tfk->tok/dot_general | solution.py:52
  53.6 16.4 %fusion.19 = bf16[24,121,1]{1,0,2:T(8,128)(2,1)S(1)} fusion(bf16[316,121,121]{2,0,1:T(8,128)(2,1)} %param.17, f32[24,316,121]{2,1,0:T(8,128)S(1)} %fusion.3), kind=kOutput, calls=%fused_computation.25 | convolution fusion | flops 1332450944 | bytes 12929576 | tf_op jit(solution)/shard_map/tok,oik->ti/dot_general | solution.py:53
  72.1 82.8 %while.11 = (s32[]{:T(128)}, f32[24,128]{1,0:T(8,128)S(1)}, s32[27,24]{1,0:T(8,128)S(1)}, f32[288,5,128]{2,1,0:T(8,128)S(1)}, f32[24,3,128]{2,0,1:T(8,128)S(1)}, /*index=5*/s32[]{:T(128)}, s32[]{:T(128)}) while((s32[]{:T(128)}, f32[24,128]{1,0:T(8,128)S(1)}, s32[27,24]{1,0:T(8,128)S(1)}, f32[288,5,128]{2,1,0:T(8,128)S(1)}, ...), condition=%wide.region_2.3_spmd.clone, body=%wide.region_0.2_spmd.clone.sunk | while | flops 5131483 | bytes 594543 | solution.py:42
  72.9 2.2 %multiply_reduce_fusion.4 = f32[24,128]{1,0:T(8,128)S(1)} fusion(f32[24,128]{1,0:T(8,128)S(1)} %bitcast.90, f32[24,128]{1,0:T(8,128)S(1)} %bitcast.91, f32[24,128]{1,0:T(8,128)S(1)} %get-tuple-element.125, f32[24,128]{1,0:T(8,128)S(1)} %bitcast.92, f32[24,128]{1,0:T(8,128)S(1)} %get-tuple-element.127, f32[24,128]{1,0:T(8,128)S(1)} %bitcast.93, ...), kind=kLoop, calls=%fused_computation.2.clone.1 | loop fusion | flops 5108736 | bytes 110592 | tf_op jit(solution)/shard_map/while/body/eval_jaxpr/reduce_sum | solution.py:40
  76.0 2.2 %multiply_reduce_fusion.4 = f32[24,128]{1,0:T(8,128)S(1)} fusion(f32[24,128]{1,0:T(8,128)S(1)} %bitcast.90, f32[24,128]{1,0:T(8,128)S(1)} %bitcast.91, f32[24,128]{1,0:T(8,128)S(1)} %get-tuple-element.125, f32[24,128]{1,0:T(8,128)S(1)} %bitcast.92, f32[24,128]{1,0:T(8,128)S(1)} %get-tuple-element.127, f32[24,128]{1,0:T(8,128)S(1)} %bitcast.93, ...), kind=kLoop, calls=%fused_computation.2.clone.1 | loop fusion | flops 5108736 | bytes 110592 | tf_op jit(solution)/shard_map/while/body/eval_jaxpr/reduce_sum | solution.py:40
  79.1 2.2 %multiply_reduce_fusion.4 = f32[24,128]{1,0:T(8,128)S(1)} fusion(f32[24,128]{1,0:T(8,128)S(1)} %bitcast.90, f32[24,128]{1,0:T(8,128)S(1)} %bitcast.91, f32[24,128]{1,0:T(8,128)S(1)} %get-tuple-element.125, f32[24,128]{1,0:T(8,128)S(1)} %bitcast.92, f32[24,128]{1,0:T(8,128)S(1)} %get-tuple-element.127, f32[24,128]{1,0:T(8,128)S(1)} %bitcast.93, ...), kind=kLoop, calls=%fused_computation.2.clone.1 | loop fusion | flops 5108736 | bytes 110592 | tf_op jit(solution)/shard_map/while/body/eval_jaxpr/reduce_sum | solution.py:40
  82.1 2.2 %multiply_reduce_fusion.4 = f32[24,128]{1,0:T(8,128)S(1)} fusion(f32[24,128]{1,0:T(8,128)S(1)} %bitcast.90, f32[24,128]{1,0:T(8,128)S(1)} %bitcast.91, f32[24,128]{1,0:T(8,128)S(1)} %get-tuple-element.125, f32[24,128]{1,0:T(8,128)S(1)} %bitcast.92, f32[24,128]{1,0:T(8,128)S(1)} %get-tuple-element.127, f32[24,128]{1,0:T(8,128)S(1)} %bitcast.93, ...), kind=kLoop, calls=%fused_computation.2.clone.1 | loop fusion | flops 5108736 | bytes 110592 | tf_op jit(solution)/shard_map/while/body/eval_jaxpr/reduce_sum | solution.py:40
  85.2 2.2 %multiply_reduce_fusion.4 = f32[24,128]{1,0:T(8,128)S(1)} fusion(f32[24,128]{1,0:T(8,128)S(1)} %bitcast.90, f32[24,128]{1,0:T(8,128)S(1)} %bitcast.91, f32[24,128]{1,0:T(8,128)S(1)} %get-tuple-element.125, f32[24,128]{1,0:T(8,128)S(1)} %bitcast.92, f32[24,128]{1,0:T(8,128)S(1)} %get-tuple-element.127, f32[24,128]{1,0:T(8,128)S(1)} %bitcast.93, ...), kind=kLoop, calls=%fused_computation.2.clone.1 | loop fusion | flops 5108736 | bytes 110592 | tf_op jit(solution)/shard_map/while/body/eval_jaxpr/reduce_sum | solution.py:40
  88.3 2.2 %multiply_reduce_fusion.4 = f32[24,128]{1,0:T(8,128)S(1)} fusion(f32[24,128]{1,0:T(8,128)S(1)} %bitcast.90, f32[24,128]{1,0:T(8,128)S(1)} %bitcast.91, f32[24,128]{1,0:T(8,128)S(1)} %get-tuple-element.125, f32[24,128]{1,0:T(8,128)S(1)} %bitcast.92, f32[24,128]{1,0:T(8,128)S(1)} %get-tuple-element.127, f32[24,128]{1,0:T(8,128)S(1)} %bitcast.93, ...), kind=kLoop, calls=%fused_computation.2.clone.1 | loop fusion | flops 5108736 | bytes 110592 | tf_op jit(solution)/shard_map/while/body/eval_jaxpr/reduce_sum | solution.py:40
  91.3 2.2 %multiply_reduce_fusion.4 = f32[24,128]{1,0:T(8,128)S(1)} fusion(f32[24,128]{1,0:T(8,128)S(1)} %bitcast.90, f32[24,128]{1,0:T(8,128)S(1)} %bitcast.91, f32[24,128]{1,0:T(8,128)S(1)} %get-tuple-element.125, f32[24,128]{1,0:T(8,128)S(1)} %bitcast.92, f32[24,128]{1,0:T(8,128)S(1)} %get-tuple-element.127, f32[24,128]{1,0:T(8,128)S(1)} %bitcast.93, ...), kind=kLoop, calls=%fused_computation.2.clone.1 | loop fusion | flops 5108736 | bytes 110592 | tf_op jit(solution)/shard_map/while/body/eval_jaxpr/reduce_sum | solution.py:40
  94.4 2.2 %multiply_reduce_fusion.4 = f32[24,128]{1,0:T(8,128)S(1)} fusion(f32[24,128]{1,0:T(8,128)S(1)} %bitcast.90, f32[24,128]{1,0:T(8,128)S(1)} %bitcast.91, f32[24,128]{1,0:T(8,128)S(1)} %get-tuple-element.125, f32[24,128]{1,0:T(8,128)S(1)} %bitcast.92, f32[24,128]{1,0:T(8,128)S(1)} %get-tuple-element.127, f32[24,128]{1,0:T(8,128)S(1)} %bitcast.93, ...), kind=kLoop, calls=%fused_computation.2.clone.1 | loop fusion | flops 5108736 | bytes 110592 | tf_op jit(solution)/shard_map/while/body/eval_jaxpr/reduce_sum | solution.py:40
  97.5 2.2 %multiply_reduce_fusion.4 = f32[24,128]{1,0:T(8,128)S(1)} fusion(f32[24,128]{1,0:T(8,128)S(1)} %bitcast.90, f32[24,128]{1,0:T(8,128)S(1)} %bitcast.91, f32[24,128]{1,0:T(8,128)S(1)} %get-tuple-element.125, f32[24,128]{1,0:T(8,128)S(1)} %bitcast.92, f32[24,128]{1,0:T(8,128)S(1)} %get-tuple-element.127, f32[24,128]{1,0:T(8,128)S(1)} %bitcast.93, ...), kind=kLoop, calls=%fused_computation.2.clone.1 | loop fusion | flops 5108736 | bytes 110592 | tf_op jit(solution)/shard_map/while/body/eval_jaxpr/reduce_sum | solution.py:40
  100.5 2.2 %multiply_reduce_fusion.4 = f32[24,128]{1,0:T(8,128)S(1)} fusion(f32[24,128]{1,0:T(8,128)S(1)} %bitcast.90, f32[24,128]{1,0:T(8,128)S(1)} %bitcast.91, f32[24,128]{1,0:T(8,128)S(1)} %get-tuple-element.125, f32[24,128]{1,0:T(8,128)S(1)} %bitcast.92, f32[24,128]{1,0:T(8,128)S(1)} %get-tuple-element.127, f32[24,128]{1,0:T(8,128)S(1)} %bitcast.93, ...), kind=kLoop, calls=%fused_computation.2.clone.1 | loop fusion | flops 5108736 | bytes 110592 | tf_op jit(solution)/shard_map/while/body/eval_jaxpr/reduce_sum | solution.py:40
  103.6 2.2 %multiply_reduce_fusion.4 = f32[24,128]{1,0:T(8,128)S(1)} fusion(f32[24,128]{1,0:T(8,128)S(1)} %bitcast.90, f32[24,128]{1,0:T(8,128)S(1)} %bitcast.91, f32[24,128]{1,0:T(8,128)S(1)} %get-tuple-element.125, f32[24,128]{1,0:T(8,128)S(1)} %bitcast.92, f32[24,128]{1,0:T(8,128)S(1)} %get-tuple-element.127, f32[24,128]{1,0:T(8,128)S(1)} %bitcast.93, ...), kind=kLoop, calls=%fused_computation.2.clone.1 | loop fusion | flops 5108736 | bytes 110592 | tf_op jit(solution)/shard_map/while/body/eval_jaxpr/reduce_sum | solution.py:40
  106.7 2.2 %multiply_reduce_fusion.4 = f32[24,128]{1,0:T(8,128)S(1)} fusion(f32[24,128]{1,0:T(8,128)S(1)} %bitcast.90, f32[24,128]{1,0:T(8,128)S(1)} %bitcast.91, f32[24,128]{1,0:T(8,128)S(1)} %get-tuple-element.125, f32[24,128]{1,0:T(8,128)S(1)} %bitcast.92, f32[24,128]{1,0:T(8,128)S(1)} %get-tuple-element.127, f32[24,128]{1,0:T(8,128)S(1)} %bitcast.93, ...), kind=kLoop, calls=%fused_computation.2.clone.1 | loop fusion | flops 5108736 | bytes 110592 | tf_op jit(solution)/shard_map/while/body/eval_jaxpr/reduce_sum | solution.py:40
  109.7 2.2 %multiply_reduce_fusion.4 = f32[24,128]{1,0:T(8,128)S(1)} fusion(f32[24,128]{1,0:T(8,128)S(1)} %bitcast.90, f32[24,128]{1,0:T(8,128)S(1)} %bitcast.91, f32[24,128]{1,0:T(8,128)S(1)} %get-tuple-element.125, f32[24,128]{1,0:T(8,128)S(1)} %bitcast.92, f32[24,128]{1,0:T(8,128)S(1)} %get-tuple-element.127, f32[24,128]{1,0:T(8,128)S(1)} %bitcast.93, ...), kind=kLoop, calls=%fused_computation.2.clone.1 | loop fusion | flops 5108736 | bytes 110592 | tf_op jit(solution)/shard_map/while/body/eval_jaxpr/reduce_sum | solution.py:40
  112.8 2.2 %multiply_reduce_fusion.4 = f32[24,128]{1,0:T(8,128)S(1)} fusion(f32[24,128]{1,0:T(8,128)S(1)} %bitcast.90, f32[24,128]{1,0:T(8,128)S(1)} %bitcast.91, f32[24,128]{1,0:T(8,128)S(1)} %get-tuple-element.125, f32[24,128]{1,0:T(8,128)S(1)} %bitcast.92, f32[24,128]{1,0:T(8,128)S(1)} %get-tuple-element.127, f32[24,128]{1,0:T(8,128)S(1)} %bitcast.93, ...), kind=kLoop, calls=%fused_computation.2.clone.1 | loop fusion | flops 5108736 | bytes 110592 | tf_op jit(solution)/shard_map/while/body/eval_jaxpr/reduce_sum | solution.py:40
  115.9 2.2 %multiply_reduce_fusion.4 = f32[24,128]{1,0:T(8,128)S(1)} fusion(f32[24,128]{1,0:T(8,128)S(1)} %bitcast.90, f32[24,128]{1,0:T(8,128)S(1)} %bitcast.91, f32[24,128]{1,0:T(8,128)S(1)} %get-tuple-element.125, f32[24,128]{1,0:T(8,128)S(1)} %bitcast.92, f32[24,128]{1,0:T(8,128)S(1)} %get-tuple-element.127, f32[24,128]{1,0:T(8,128)S(1)} %bitcast.93, ...), kind=kLoop, calls=%fused_computation.2.clone.1 | loop fusion | flops 5108736 | bytes 110592 | tf_op jit(solution)/shard_map/while/body/eval_jaxpr/reduce_sum | solution.py:40
  118.9 2.2 %multiply_reduce_fusion.4 = f32[24,128]{1,0:T(8,128)S(1)} fusion(f32[24,128]{1,0:T(8,128)S(1)} %bitcast.90, f32[24,128]{1,0:T(8,128)S(1)} %bitcast.91, f32[24,128]{1,0:T(8,128)S(1)} %get-tuple-element.125, f32[24,128]{1,0:T(8,128)S(1)} %bitcast.92, f32[24,128]{1,0:T(8,128)S(1)} %get-tuple-element.127, f32[24,128]{1,0:T(8,128)S(1)} %bitcast.93, ...), kind=kLoop, calls=%fused_computation.2.clone.1 | loop fusion | flops 5108736 | bytes 110592 | tf_op jit(solution)/shard_map/while/body/eval_jaxpr/reduce_sum | solution.py:40
  122.0 2.2 %multiply_reduce_fusion.4 = f32[24,128]{1,0:T(8,128)S(1)} fusion(f32[24,128]{1,0:T(8,128)S(1)} %bitcast.90, f32[24,128]{1,0:T(8,128)S(1)} %bitcast.91, f32[24,128]{1,0:T(8,128)S(1)} %get-tuple-element.125, f32[24,128]{1,0:T(8,128)S(1)} %bitcast.92, f32[24,128]{1,0:T(8,128)S(1)} %get-tuple-element.127, f32[24,128]{1,0:T(8,128)S(1)} %bitcast.93, ...), kind=kLoop, calls=%fused_computation.2.clone.1 | loop fusion | flops 5108736 | bytes 110592 | tf_op jit(solution)/shard_map/while/body/eval_jaxpr/reduce_sum | solution.py:40
  125.1 2.2 %multiply_reduce_fusion.4 = f32[24,128]{1,0:T(8,128)S(1)} fusion(f32[24,128]{1,0:T(8,128)S(1)} %bitcast.90, f32[24,128]{1,0:T(8,128)S(1)} %bitcast.91, f32[24,128]{1,0:T(8,128)S(1)} %get-tuple-element.125, f32[24,128]{1,0:T(8,128)S(1)} %bitcast.92, f32[24,128]{1,0:T(8,128)S(1)} %get-tuple-element.127, f32[24,128]{1,0:T(8,128)S(1)} %bitcast.93, ...), kind=kLoop, calls=%fused_computation.2.clone.1 | loop fusion | flops 5108736 | bytes 110592 | tf_op jit(solution)/shard_map/while/body/eval_jaxpr/reduce_sum | solution.py:40
  128.1 2.2 %multiply_reduce_fusion.4 = f32[24,128]{1,0:T(8,128)S(1)} fusion(f32[24,128]{1,0:T(8,128)S(1)} %bitcast.90, f32[24,128]{1,0:T(8,128)S(1)} %bitcast.91, f32[24,128]{1,0:T(8,128)S(1)} %get-tuple-element.125, f32[24,128]{1,0:T(8,128)S(1)} %bitcast.92, f32[24,128]{1,0:T(8,128)S(1)} %get-tuple-element.127, f32[24,128]{1,0:T(8,128)S(1)} %bitcast.93, ...), kind=kLoop, calls=%fused_computation.2.clone.1 | loop fusion | flops 5108736 | bytes 110592 | tf_op jit(solution)/shard_map/while/body/eval_jaxpr/reduce_sum | solution.py:40
  131.2 2.2 %multiply_reduce_fusion.4 = f32[24,128]{1,0:T(8,128)S(1)} fusion(f32[24,128]{1,0:T(8,128)S(1)} %bitcast.90, f32[24,128]{1,0:T(8,128)S(1)} %bitcast.91, f32[24,128]{1,0:T(8,128)S(1)} %get-tuple-element.125, f32[24,128]{1,0:T(8,128)S(1)} %bitcast.92, f32[24,128]{1,0:T(8,128)S(1)} %get-tuple-element.127, f32[24,128]{1,0:T(8,128)S(1)} %bitcast.93, ...), kind=kLoop, calls=%fused_computation.2.clone.1 | loop fusion | flops 5108736 | bytes 110592 | tf_op jit(solution)/shard_map/while/body/eval_jaxpr/reduce_sum | solution.py:40
  134.2 2.2 %multiply_reduce_fusion.4 = f32[24,128]{1,0:T(8,128)S(1)} fusion(f32[24,128]{1,0:T(8,128)S(1)} %bitcast.90, f32[24,128]{1,0:T(8,128)S(1)} %bitcast.91, f32[24,128]{1,0:T(8,128)S(1)} %get-tuple-element.125, f32[24,128]{1,0:T(8,128)S(1)} %bitcast.92, f32[24,128]{1,0:T(8,128)S(1)} %get-tuple-element.127, f32[24,128]{1,0:T(8,128)S(1)} %bitcast.93, ...), kind=kLoop, calls=%fused_computation.2.clone.1 | loop fusion | flops 5108736 | bytes 110592 | tf_op jit(solution)/shard_map/while/body/eval_jaxpr/reduce_sum | solution.py:40
  146.5 2.2 %multiply_reduce_fusion.4 = f32[24,128]{1,0:T(8,128)S(1)} fusion(f32[24,128]{1,0:T(8,128)S(1)} %bitcast.90, f32[24,128]{1,0:T(8,128)S(1)} %bitcast.91, f32[24,128]{1,0:T(8,128)S(1)} %get-tuple-element.125, f32[24,128]{1,0:T(8,128)S(1)} %bitcast.92, f32[24,128]{1,0:T(8,128)S(1)} %get-tuple-element.127, f32[24,128]{1,0:T(8,128)S(1)} %bitcast.93, ...), kind=kLoop, calls=%fused_computation.2.clone.1 | loop fusion | flops 5108736 | bytes 110592 | tf_op jit(solution)/shard_map/while/body/eval_jaxpr/reduce_sum | solution.py:40
  149.6 2.2 %multiply_reduce_fusion.4 = f32[24,128]{1,0:T(8,128)S(1)} fusion(f32[24,128]{1,0:T(8,128)S(1)} %bitcast.90, f32[24,128]{1,0:T(8,128)S(1)} %bitcast.91, f32[24,128]{1,0:T(8,128)S(1)} %get-tuple-element.125, f32[24,128]{1,0:T(8,128)S(1)} %bitcast.92, f32[24,128]{1,0:T(8,128)S(1)} %get-tuple-element.127, f32[24,128]{1,0:T(8,128)S(1)} %bitcast.93, ...), kind=kLoop, calls=%fused_computation.2.clone.1 | loop fusion | flops 5108736 | bytes 110592 | tf_op jit(solution)/shard_map/while/body/eval_jaxpr/reduce_sum | solution.py:40
  156.6 42.1 %all-reduce = (f32[8]{0:T(128)S(1)}, f32[]{:T(128)}, f32[]{:T(128)}, f32[8,8]{1,0:T(8,128)S(1)}) all-reduce(f32[8]{0:T(128)S(1)} %convolution_bitcast_fusion.2, f32[]{:T(128)S(6)} %mul.76, f32[]{:T(128)} %get-tuple-element.74, f32[8,8]{1,0:T(8,128)S(1)} %convolution_bitcast_fusion), channel_id=1, replica_groups=mesh['seg'=8,'grp'=4] {'seg','grp'}, use_global_device_ids=true, to_apply=%region_3.4 | all-reduce | flops 74 | bytes 592 | tf_op jit(solution)/shard_map/psum | solution.py:81
  (260 shorter events, 48.4 us)
Async XLA Ops:
  0.6 69.4 %copy-start = (bf16[24,128,121]{1,0,2:T(8,128)(2,1)S(1)}, bf16[24,128,121]{1,0,2:T(8,128)(2,1)}, u32[]{:S(2)}) copy-start(bf16[24,128,121]{1,0,2:T(8,128)(2,1)} %param.16) | copy-start | bytes 2230276
  0.6 31.8 %copy-start.3 = (s32[24,27]{1,0:T(8,128)S(1)}, s32[24,27]{1,0:T(8,128)}, u32[]{:S(2)}) copy-start(s32[24,27]{1,0:T(8,128)} %param.19) | copy-start | bytes 7780
  10.0 23.9 %collective-permute-start.2 = (f32[96,121]{1,0:T(8,128)S(1)}, f32[96,121]{1,0:T(8,128)S(1)}, u32[]{:S(2)}, u32[]{:S(2)}) collective-permute-start(f32[96,121]{1,0:T(8,128)S(1)} %all_gather.7), channel_id=1, source_target_pairs={{0,4},{4,8},{8,12},{12,16},{16,20},{20,24},{24,28},{1,5},{5,9},{9,... | collective-permute-start | bytes 139400 | tf_op jit(solution)/shard_map/ppermute | solution.py:19
  13.9 20.0 %collective-permute-start.3 = (f32[96,121]{1,0:T(8,128)S(1)}, f32[96,121]{1,0:T(8,128)S(1)}, u32[]{:S(2)}, u32[]{:S(2)}) collective-permute-start(f32[96,121]{1,0:T(8,128)S(1)} %all_gather.7), channel_id=1, source_target_pairs={{4,0},{8,4},{12,8},{16,12},{20,16},{24,20},{28,24},{5,1},{9,5},{13... | collective-permute-start | bytes 139400 | tf_op jit(solution)/shard_map/ppermute | solution.py:21
  23.0 47.4 %collective-permute-start = (f32[96,5,128]{2,0,1:T(8,128)}, f32[96,5,128]{2,0,1:T(8,128)}, u32[]{:S(2)}, u32[]{:S(2)}) collective-permute-start(f32[96,5,128]{2,0,1:T(8,128)} %all_gather.6), channel_id=1, source_target_pairs={{0,4},{4,8},{8,12},{12,16},{16,20},{20,24},{24,28},{1,5},{5,9},{9,... | collective-permute-start | bytes 737288 | tf_op jit(solution)/shard_map/ppermute | solution.py:19
  28.2 42.2 %collective-permute-start.1 = (f32[96,5,128]{2,0,1:T(8,128)}, f32[96,5,128]{2,0,1:T(8,128)}, u32[]{:S(2)}, u32[]{:S(2)}) collective-permute-start(f32[96,5,128]{2,0,1:T(8,128)} %all_gather.6), channel_id=1, source_target_pairs={{4,0},{8,4},{12,8},{16,12},{20,16},{24,20},{28,24},{5,1},{9,5},{13... | collective-permute-start | bytes 737288 | tf_op jit(solution)/shard_map/ppermute | solution.py:21
  41.4 1.6 copy-start.2
  70.4 1.7 copy-start.1
where the time goes:
time: 206 us; the launch traced here: 205 us
  other arithmetic  74.2 us (36%)
  blocking collectives  54.5 us (26%)
  matrix products  30.5 us (15%)
  local copies, waits for them, and re-layouts  26.7 us (13%)
  starting transfers between devices  11.7 us (6%)
  between operations  4.88 us (2%)
  loops' own time  2.33 us (1%)
    reduce_sum x27, other arithmetic, near_step(): return (running + jnp.sum(kernel * source[:, 4, None, :], axis=2), None)  59.9 us
    psum x1, blocking collectives, on_device(): lax.psum((products, live_panels, gram, jnp.sum(image * image)), ('seg', '...  42.1 us
    dot_general x1, matrix products, far_field(): jnp.einsum('tok,oik->ti', summed, m2l.astype(jnp.float32), precision=high...  16.4 us
    gather x27, local copies, waits for them, and re-layouts, near_step(): source = jnp.take(wide_panels, column, axis=0)  15.6 us
    dot_general x1, matrix products, far_field(): summed = jnp.einsum('tfo,tfk->tok', offset_hot, gathered, precision=highest)  10.6 us
    ppermute x2, starting transfers between devices, with_halo(): lax.ppermute(tail, axis, [(i, (i + 1) % count) for i in range(ends)])  9.14 us
    gather x2, local copies, waits for them, and re-layouts, far_field(): gathered = jnp.take(wide_poles, far_list, axis=0)  9 us
    all_gather x1, blocking collectives, on_device(): lax.all_gather(packed, 'grp', axis=0, tiled=True)  6.2 us
  transfers between devices with their start and end apart: 4, of which 0 were waited for; matrix products, arithmetic and copies ran while one was open for 20% of the time, Pallas kernels for 0%

commit v1 on v0

v1 whole, which is shorter than its diff:
```python
import functools

import jax
import jax.numpy as jnp
from jax import lax
from jax.experimental import pallas as pl
from jax.experimental.pallas import tpu as pltpu
from jax.sharding import PartitionSpec as P

four_pi = 12.566370614359172
epsilon = 1e-06
bf16 = jnp.bfloat16
f32 = jnp.float32
WIDTH = 32
LIMIT = 56 * 1024 * 1024

across = (((1,), (1,)), ((), ()))


def vmem(count):
    return [pl.BlockSpec(memory_space=pltpu.VMEM)] * count


def smem(count):
    return [pl.BlockSpec(memory_space=pltpu.SMEM)] * count


def live_rows(counts, shape):
    return (lax.broadcasted_iota(jnp.int32, shape, 0) < counts[0]).astype(f32)


def prep_kernel(counts, basis, coords, areas, p2m, block):
    krylov, leaves, panels = basis.shape
    terms = p2m.shape[1]
    current = basis[krylov - 1] * live_rows(counts, (leaves, panels))
    rounded = current.astype(bf16)
    row = lax.broadcasted_iota(jnp.int32, (leaves, terms), 0)
    poles = jnp.zeros((leaves, terms), f32)
    for leaf in range(leaves):
        moved = lax.dot_general(rounded, p2m[leaf], across, preferred_element_type=f32)
        poles = jnp.where(row == leaf, moved, poles)
    for c in range(3):
        block[c] = coords[:, c, :]
    block[3] = areas[...]
    block[4] = areas[...] * current * (1.0 / four_pi)
    block[5] = jnp.zeros((leaves, panels), f32)
    block[5, :, 0:terms] = poles


def plan_kernel(counts, basis, slots, classes, hits, gram, wide):
    krylov, leaves, panels = basis.shape
    total = hits.shape[0] // leaves
    window = hits.shape[1]
    panes = wide.shape[0]
    lanes = wide.shape[2]
    entries = slots.shape[1]

    def body(leaf, carry):
        offset = classes[pl.ds(leaf, 1), :]
        slot = slots[pl.ds(leaf, 1), :]
        by_class = lax.broadcasted_iota(jnp.int32, (total, entries), 0) == offset
        by_slot = lax.broadcasted_iota(jnp.int32, (window, entries), 0) == slot
        found = lax.dot_general(
            by_class.astype(f32).astype(bf16),
            by_slot.astype(f32).astype(bf16),
            across,
            preferred_element_type=f32,
        )
        for pane in range(panes):
            part = found[:, pane * lanes : (pane + 1) * lanes]
            wide[pane, pl.ds(leaf, total, stride=leaves), :] = part
        return carry

    lax.fori_loop(0, leaves, body, 0)

    rows = 16 * leaves

    def shrink(step, carry):
        at = pl.ds(pl.multiple_of(step * rows, rows), rows)
        for pane in range(panes):
            hits[at, pane * lanes : (pane + 1) * lanes] = wide[pane, at, :].astype(bf16)
        return carry

    lax.fori_loop(0, hits.shape[0] // rows, shrink, 0)

    live = live_rows(counts, (leaves, panels))
    masked = [basis[j] * live for j in range(krylov)]
    lane = lax.broadcasted_iota(jnp.int32, (krylov, panels), 1)
    tile = jnp.zeros((krylov, panels), f32)
    for j in range(krylov):
        rows_j = [jnp.sum(masked[i] * masked[j], axis=0, keepdims=True) for i in range(krylov)]
        column = jnp.sum(jnp.concatenate(rows_j, axis=0), axis=1, keepdims=True)
        tile = jnp.where(lane == krylov + j, column, tile)
    population = (jnp.minimum(counts[0], leaves) * panels).astype(f32)
    gram[...] = jnp.where(lane == 2, population, tile)


def thirds(value):
    first = value.astype(bf16).astype(f32)
    second = (value - first).astype(bf16).astype(f32)
    return first, second, value - first - second


pairs = ((0, 0), (0, 1), (1, 0), (1, 1), (0, 2), (2, 0))


def main_kernel(
    counts, near, here, there, hits_hbm, m2l_hbm, l2p, basis, gram,
    image_out, tile_out,
    hits, m2l, source32, source16, target32, charge, poles32, poles16, nearby, sems,
):
    krylov, leaves, panels = basis.shape
    blocks = here.shape[0]
    terms = l2p.shape[2]
    offsets = m2l.shape[0]
    copies = [
        pltpu.make_async_copy(hits_hbm, hits, sems.at[0]),
        pltpu.make_async_copy(m2l_hbm, m2l, sems.at[1]),
    ]
    for copy in copies:
        copy.start()

    ones = jnp.ones((leaves, panels), f32)
    zeros = jnp.zeros((leaves, panels), f32)

    def place(ref, base, rows):
        for k in range(WIDTH):
            value = rows[k] if k < len(rows) else zeros
            ref[pl.ds(base * WIDTH + k, leaves, stride=WIDTH), :] = value

    poles32[...] = jnp.zeros_like(poles32)
    for b in range(2 * blocks):
        got = here if b < blocks else there
        at = b % blocks
        point = [got[at, c] for c in range(3)]
        area = got[at, 3]
        area = jnp.where(area > 0.0, area, 1.0)
        split = [thirds(p) for p in point]
        square = point[0] * point[0] + point[1] * point[1] + point[2] * point[2]
        rows = [split[c][q] for c in range(3) for (_, q) in pairs]
        place(source32, b * leaves, rows + list(thirds(square + area)) + [ones] * 3)
        if b == 0:
            rows = [split[c][p] * (-2.0) for c in range(3) for (p, _) in pairs]
            place(target32, 0, rows + [ones] * 3 + list(thirds(square)))
        charge[pl.ds(b * leaves, leaves), :] = got[at, 4]
        poles32[pl.ds(b * leaves, leaves), :] = got[at, 5]
    source16[...] = source32[...].astype(bf16)
    pole = poles32[...]
    pole_high = pole.astype(bf16)
    poles16[:, 0:panels] = pole_high
    poles16[:, panels : 2 * panels] = (pole - pole_high.astype(f32)).astype(bf16)

    entries = near.shape[1]
    row_ones = jnp.ones((8, panels), f32)

    def near_body(leaf, carry):
        at = pl.multiple_of(leaf * WIDTH, WIDTH)
        target = target32[pl.ds(at, WIDTH), :].T.astype(bf16)
        total = jnp.zeros((panels, panels), f32)
        for start in range(0, entries, 2):
            ids = [near[leaf, e] for e in range(start, min(start + 2, entries))]
            source = [source16[pl.ds(pl.multiple_of(s * WIDTH, WIDTH), WIDTH), :] for s in ids]
            source = jnp.concatenate(source, axis=1) if len(ids) > 1 else source[0]
            inverse = lax.rsqrt(jnp.dot(target, source, preferred_element_type=f32))
            for e, s in enumerate(ids):
                total += inverse[:, e * panels : (e + 1) * panels] * charge[pl.ds(s, 1), :]
        summed = lax.dot_general(
            row_ones, total, across, preferred_element_type=f32, precision=lax.Precision.HIGHEST
        )
        nearby[pl.ds(leaf, 1), :] = summed[0:1]
        return carry

    lax.fori_loop(0, leaves, near_body, 0)
    for copy in copies:
        copy.wait()

    chunk = 16
    steps = hits.shape[0] // leaves // chunk

    def far_body(step, local):
        at = pl.multiple_of(step * chunk * leaves, chunk * leaves)
        both = jnp.dot(
            hits[pl.ds(at, chunk * leaves), :], poles16[...], preferred_element_type=f32
        )
        summed = both[:, 0:panels] + both[:, panels : 2 * panels]
        for i in range(chunk):
            part = summed[i * leaves : (i + 1) * leaves, 0:terms]
            high = part.astype(bf16).astype(f32)
            stacked = jnp.concatenate([high, part - high], axis=0).astype(bf16)
            table = m2l[jnp.minimum(step * chunk + i, offsets - 1)]
            local += lax.dot_general(stacked, table, across, preferred_element_type=f32)
        return local

    local = lax.fori_loop(0, steps, far_body, jnp.zeros((2 * leaves, terms), f32))
    local16 = (local[0:leaves] + local[leaves:]).astype(bf16)
    row = lax.broadcasted_iota(jnp.int32, (leaves, panels), 0)
    distant = jnp.zeros((leaves, panels), f32)
    for leaf in range(leaves):
        moved = lax.dot_general(local16, l2p[leaf], across, preferred_element_type=f32)
        distant = jnp.where(row == leaf, moved, distant)

    live = live_rows(counts, (leaves, panels))
    current = basis[krylov - 1] * live
    image = (0.5 * current + nearby[...] + distant) * live
    image_out[...] = image
    rows = [jnp.sum(basis[j] * live * image, axis=0, keepdims=True) for j in range(krylov)]
    product = jnp.sum(jnp.concatenate(rows, axis=0), axis=1, keepdims=True)
    energy = jnp.sum(jnp.sum(image * image, axis=0, keepdims=True), axis=1, keepdims=True)
    lane = lax.broadcasted_iota(jnp.int32, (krylov, panels), 1)
    tile_out[...] = jnp.where(lane == 0, product, jnp.where(lane == 1, energy, gram[...]))


def final_kernel(counts, basis, image, tile, vector, column):
    krylov, leaves, panels = basis.shape
    sums = tile[...]
    population = sums[0:1, 2:3]
    energy = sums[0:1, 1:2]
    products = sums[:, 0:1]
    coefficients = products / population
    row = lax.broadcasted_iota(jnp.int32, (krylov, panels), 0)
    lane = lax.broadcasted_iota(jnp.int32, (krylov, panels), 1)
    in_gram = (lane >= krylov) & (lane < 2 * krylov)
    applied = jnp.sum(jnp.where(in_gram, coefficients * sums, 0.0), axis=0, keepdims=True)
    across_lanes = jnp.sum(jnp.where(lane == krylov + row, coefficients, 0.0), axis=0, keepdims=True)
    curvature = jnp.sum(applied * across_lanes, axis=1, keepdims=True)
    crossed = jnp.sum(coefficients * products, axis=0, keepdims=True)
    squares = energy - 2.0 * crossed + curvature
    scale = jnp.sqrt(squares / population + epsilon)
    live = live_rows(counts, (leaves, panels))
    residue = image[...]
    for j in range(krylov):
        residue = residue - coefficients[j : j + 1, 0:1] * (basis[j] * live)
    vector[...] = residue / scale
    placed = jnp.sum(jnp.where(lane == row, coefficients, 0.0), axis=0, keepdims=True)
    column[...] = jnp.where(lane[0:1] == krylov, scale, placed)


def swap(value, axis, bit):
    count = lax.axis_size(axis)
    return lax.ppermute(value, axis, [(i, i ^ bit) for i in range(count)])


def hop(value, axis):
    count = lax.axis_size(axis)
    moves = [(i, i + 2 if i % 2 == 0 else i - 2) for i in range(count)]
    return lax.ppermute(value, axis, [(i, k) for i, k in moves if 0 <= k < count])


def on_device(basis, coords, areas, p2m, l2p, m2l, counts, near_list, far_list, far_offset):
    krylov, leaves, panels = basis.shape
    terms = p2m.shape[1]
    offsets = m2l.shape[0]
    groups = lax.axis_size("grp")
    params = pltpu.CompilerParams(vmem_limit_bytes=LIMIT)
    me = lax.axis_index("grp")
    even = lax.axis_index("seg") % 2 == 0

    block = pl.pallas_call(
        prep_kernel,
        out_shape=jax.ShapeDtypeStruct((6, leaves, panels), f32),
        in_specs=smem(1) + vmem(4),
        out_specs=pl.BlockSpec(memory_space=pltpu.VMEM),
        compiler_params=params,
        name="prep",
    )(counts, basis, coords, areas, p2m)

    half = groups // 2

    def slot_of(window):
        segment = window // (groups * leaves)
        group = (window // leaves) % groups
        order = jnp.where(segment == 1, 0, jnp.where((segment == 2) == even, 1, 2))
        relative = group ^ me
        return ((relative % 2) * 3 * half + order * half + relative // 2) * leaves + window % leaves

    near_slots = slot_of(near_list)
    pad = -far_list.shape[1] % 128
    slots = jnp.pad(slot_of(far_list), ((0, 0), (0, pad)), constant_values=-1)
    classes = jnp.pad(far_offset, ((0, 0), (0, pad)), constant_values=-1)
    window = 3 * groups * leaves
    wide = window + -window % 128
    total = offsets + -offsets % 16
    hits, gram = pl.pallas_call(
        plan_kernel,
        out_shape=(
            jax.ShapeDtypeStruct((total * leaves, wide), bf16),
            jax.ShapeDtypeStruct((krylov, panels), f32),
        ),
        in_specs=smem(1) + vmem(3),
        out_specs=tuple(vmem(2)),
        scratch_shapes=[pltpu.VMEM((wide // 128, total * leaves, 128), f32)],
        compiler_params=params,
        name="plan",
    )(counts, basis, slots, classes)

    def spread(value):
        whole = [value]
        bit = 2
        while bit < groups:
            whole = whole + [swap(v, "grp", bit) for v in whole]
            bit *= 2
        return whole

    beside = swap(block, "seg", 1)
    own = spread(block)
    beyond = hop(beside, "seg")
    here = jnp.stack(own + spread(beside) + spread(beyond))
    there = swap(here, "grp", 1)

    image, tile = pl.pallas_call(
        main_kernel,
        out_shape=(
            jax.ShapeDtypeStruct((leaves, panels), f32),
            jax.ShapeDtypeStruct((krylov, panels), f32),
        ),
        in_specs=smem(2) + vmem(2) + [pl.BlockSpec(memory_space=pl.ANY)] * 2 + vmem(3),
        out_specs=tuple(vmem(2)),
        scratch_shapes=[
            pltpu.VMEM((total * leaves, wide), bf16),
            pltpu.VMEM(m2l.shape, bf16),
            pltpu.VMEM((window * WIDTH, panels), f32),
            pltpu.VMEM((window * WIDTH, panels), bf16),
            pltpu.VMEM((leaves * WIDTH, panels), f32),
            pltpu.VMEM((window, panels), f32),
            pltpu.VMEM((wide, panels), f32),
            pltpu.VMEM((wide, 2 * panels), bf16),
            pltpu.VMEM((leaves, panels), f32),
            pltpu.SemaphoreType.DMA((2,)),
        ],
        compiler_params=params,
        name="main",
    )(counts, near_slots, here, there, hits, m2l, l2p, basis, gram)

    for axis in ("grp", "seg"):
        bit = 1
        while bit < lax.axis_size(axis):
            tile = tile + swap(tile, axis, bit)
            bit *= 2

    vector, column = pl.pallas_call(
        final_kernel,
        out_shape=(
            jax.ShapeDtypeStruct((leaves, panels), f32),
            jax.ShapeDtypeStruct((1, panels), f32),
        ),
        in_specs=smem(1) + vmem(3),
        out_specs=tuple(vmem(2)),
        compiler_params=params,
        name="final",
    )(counts, basis, image, tile)
    return vector, column[0, : krylov + 1]


def solution(mesh):
    placed = (
        P(None, ("seg", "grp"), None),
        P(("seg", "grp"), None, None),
        P(("seg", "grp"), None),
        P(("seg", "grp"), None, None),
        P(("seg", "grp"), None, None),
        P(),
        P(("seg", "grp")),
        P(("seg", "grp"), None),
        P(("seg", "grp"), None),
        P(("seg", "grp"), None),
    )
    return jax.shard_map(
        on_device,
        mesh=mesh,
        in_specs=placed,
        out_specs=(P(("seg", "grp"), None), P()),
        check_vma=False,
    )
```

time: 206 us -> 120 us (0.58)
  other arithmetic: 74.2 us -> 2.8 us
  Pallas kernels: 0 us -> 57.5 us
  blocking collectives: 54.5 us -> 0 us
  matrix products: 30.5 us -> 0 us
  waiting for transfers between devices: 0.01 us -> 11.2 us
  starting transfers between devices: 11.7 us -> 21 us
  between operations: 4.88 us -> 1.34 us
  loops' own time: 2.33 us -> 0 us
    reduce_sum x29 -> x0, other arithmetic: 61.9 us -> none  [the longest x27 59.9 us: near_step(): return (running + jnp.sum(kernel * source[:, 4, None, :], axis=2), None)]
    pallas_call x0 -> x4, Pallas kernels: none -> 57.5 us  [the longest x1 41.5 us: on_device(): pl.pallas_call(main_kernel, out_shape=(jax.ShapeDtypeStruct((leaves, pane...]
    psum x1 -> x0, blocking collectives: 42.1 us -> none  [on_device(): lax.psum((products, live_panels, gram, jnp.sum(image * image)), ('seg', '...]
    dot_general x8 -> x0, matrix products: 30.5 us -> none  [the longest x1 16.4 us: far_field(): jnp.einsum('tok,oik->ti', summed, m2l.astype(jnp.float32), precision=high...]
    gather x29 -> x0, local copies, waits for them, and re-layouts: 24.6 us -> none  [the longest x27 15.6 us: near_step(): source = jnp.take(wide_panels, column, axis=0)]
    unnamed x10 -> x15, local copies, waits for them, and re-layouts: 0.57 us -> 22 us
    all_gather x2 -> x0, blocking collectives: 12.4 us -> none  [the longest x1 6.2 us: on_device(): lax.all_gather(packed, 'grp', axis=0, tiled=True)]
    ppermute x4 -> x11, waiting for transfers between devices: 0.01 us -> 11.2 us  [the longest x10 10.9 us: swap(): return lax.ppermute(value, axis, [(i, i ^ bit) for i in range(count)])]
  transfers between devices with their start and end apart: 4 -> 11, of which waited for: 0 -> 9; matrix products, arithmetic and copies ran while one was open for 20% -> 18% of each run, Pallas kernels for 0% -> 10%
where the time goes in v1:
time: 120 us; the launch traced here: 119 us
  Pallas kernels  57.5 us (48%)
  local copies, waits for them, and re-layouts  25 us (21%)
  starting transfers between devices  21 us (18%)
  waiting for transfers between devices  11.2 us (9%)
  other arithmetic  2.8 us (2%)
  between operations  1.34 us (1%)
    pallas_call x1, Pallas kernels, on_device(): pl.pallas_call(main_kernel, out_shape=(jax.ShapeDtypeStruct((leaves, pane...  41.5 us
    unnamed x15, local copies, waits for them, and re-layouts  22 us
    ppermute x10, starting transfers between devices, swap(): return lax.ppermute(value, axis, [(i, i ^ bit) for i in range(count)])  17 us
    pallas_call x1, Pallas kernels, on_device(): pl.pallas_call(plan_kernel, out_shape=(jax.ShapeDtypeStruct((total * leav...  11.7 us
    ppermute x10, waiting for transfers between devices, swap(): return lax.ppermute(value, axis, [(i, i ^ bit) for i in range(count)])  10.9 us
    ppermute x1, starting transfers between devices, hop(): lax.ppermute(value, axis, [(i, k) for i, k in moves if 0 <= k < count])  3.98 us
  transfers between devices with their start and end apart: 11, of which 9 were waited for; matrix products, arithmetic and copies ran while one was open for 18% of the time, Pallas kernels for 10%

profile of v1, /device:TPU:0, one launch (start us, length us, event | category | flops | bytes accessed | tf_op | source)
XLA Modules:
  0.0 118.9 jit_solution(9046655565216820857)
XLA Ops:
  1.3 1.4 %copy.12.coords = f32[24,3,128]{2,1,0:T(4,128)} copy(f32[24,3,128]{2,0,1:T(8,128)} %param.11) | data formatting | bytes 73728 | tf_op args[1]
  2.7 2.2 %copy.13.p2m = bf16[24,121,128]{2,1,0:T(8,128)(2,1)} copy(bf16[24,121,128]{2,0,1:T(8,128)(2,1)} %param.13) | data formatting | bytes 1486848 | tf_op args[3]
  4.9 2.4 %prep.1 = f32[6,24,128]{2,1,0:T(8,128)} custom-call(s32[1]{0:T(128)S(6)} %copy.21.counts, f32[8,24,128]{2,1,0:T(8,128)} %basis.7, f32[24,3,128]{2,1,0:T(4,128)} %copy.12.coords, f32[24,128]{1,0:T(8,128)} %areas.1, bf16[24,121,128]{2,1,0:T(8,128)(2,1)} %copy.13.p2m), custom_call_target="tpu_custom_call" | custom-call | tf_op jit(solution)/shard_map/prep/pallas_call | solution.py:258
  7.3 3.0 %collective-permute-start.1 = (f32[6,24,128]{2,1,0:T(8,128)}, f32[6,24,128]{2,1,0:T(8,128)S(1)}, u32[]{:S(2)}, u32[]{:S(2)}) collective-permute-start(f32[6,24,128]{2,1,0:T(8,128)} %prep.1), channel_id=1, source_target_pairs={{0,4},{4,0},{8,12},{12,8},{16,20},{20,16},{24,28},{28,24},{1,5},{5... | collective-permute-start | bytes 221192 | tf_op jit(solution)/shard_map/ppermute | solution.py:240
  10.2 1.5 %collective-permute-start = (f32[6,24,128]{2,1,0:T(8,128)}, f32[6,24,128]{2,1,0:T(8,128)S(1)}, u32[]{:S(2)}, u32[]{:S(2)}) collective-permute-start(f32[6,24,128]{2,1,0:T(8,128)} %prep.1), channel_id=1, source_target_pairs={{0,2},{1,3},{2,0},{3,1},{4,6},{5,7},{6,4},{7,5},{8,10},{9,11},{10,... | collective-permute-start | bytes 221192 | tf_op jit(solution)/shard_map/ppermute | solution.py:240
  11.7 0.9 bitcast_dynamic-update-slice_fusion.5
  12.8 4.0 %collective-permute-start.3 = (f32[6,24,128]{2,1,0:T(8,128)S(1)}, f32[6,24,128]{2,1,0:T(8,128)S(1)}, u32[]{:S(2)}, u32[]{:S(2)}) collective-permute-start(f32[6,24,128]{2,1,0:T(8,128)S(1)} %collective-permute-done.1), channel_id=1, source_target_pairs={{0,8},{8,16},{12,4},{16,24},{20,12},{28,20},{1,9},{9,17},{13,5},{1... | collective-permute-start | bytes 221192 | tf_op jit(solution)/shard_map/ppermute | solution.py:246
  16.8 1.6 %collective-permute-start.2 = (f32[6,24,128]{2,1,0:T(8,128)S(1)}, f32[6,24,128]{2,1,0:T(8,128)S(1)}, u32[]{:S(2)}, u32[]{:S(2)}) collective-permute-start(f32[6,24,128]{2,1,0:T(8,128)S(1)} %collective-permute-done.1), channel_id=1, source_target_pairs={{0,2},{1,3},{2,0},{3,1},{4,6},{5,7},{6,4},{7,5},{8,10},{9,11},{10,... | collective-permute-start | bytes 221192 | tf_op jit(solution)/shard_map/ppermute | solution.py:240
  18.7 1.5 %collective-permute-start.4 = (f32[6,24,128]{2,1,0:T(8,128)S(1)}, f32[6,24,128]{2,1,0:T(8,128)S(1)}, u32[]{:S(2)}, u32[]{:S(2)}) collective-permute-start(f32[6,24,128]{2,1,0:T(8,128)S(1)} %collective-permute-done.3), channel_id=1, source_target_pairs={{0,2},{1,3},{2,0},{3,1},{4,6},{5,7},{6,4},{7,5},{8,10},{9,11},{10,... | collective-permute-start | bytes 221192 | tf_op jit(solution)/shard_map/ppermute | solution.py:240
  20.2 1.0 collective-permute-done.2
  21.2 1.9 %collective-permute-done.4 = f32[6,24,128]{2,1,0:T(8,128)S(1)} collective-permute-done((f32[6,24,128]{2,1,0:T(8,128)S(1)}, f32[6,24,128]{2,1,0:T(8,128)S(1)}, u32[]{:S(2)}, u32[]{:S(2)}) %collective-permute-start.4) | collective-permute-done | bytes 73760 | tf_op jit(solution)/shard_map/ppermute | solution.py:240
  23.2 0.9 fusion.6
  24.0 0.6 pad.7.slots
  24.6 1.3 %pad.8.classes = s32[24,256]{1,0:T(8,128)} pad(s32[24,189]{1,0:T(8,128)} %param.19, s32[]{:T(128)} %constant.106.clone.1), padding=0_0x0_67 | pad | bytes 42724 | tf_op jit(solution)/shard_map/jit(_pad)/pad | solution.py:279
  26.0 2.4 %copy.15.l2p = bf16[24,128,121]{2,1,0:T(8,128)(2,1)} copy(bf16[24,128,121]{1,0,2:T(8,128)(2,1)} %param.14) | data formatting | bytes 1486848 | tf_op args[4]
  28.4 14.2 %copy.14.m2l_hbm = bf16[316,121,121]{2,1,0:T(8,128)(2,1)} copy(bf16[316,121,121]{2,0,1:T(8,128)(2,1)} %param.15) | data formatting | bytes 18506224 | tf_op args[5]
  42.6 11.7 %plan.1 = (bf16[7680,384]{1,0:T(8,128)(2,1)}, f32[8,128]{1,0:T(8,128)}) custom-call(s32[1]{0:T(128)S(6)} %copy.21.counts, f32[8,24,128]{2,1,0:T(8,128)} %basis.7, s32[24,256]{1,0:T(8,128)} %pad.7.slots, s32[24,256]{1,0:T(8,128)} %pad.8.classes), custom_call_target="tpu_custom_call" | custom-call | tf_op jit(solution)/shard_map/plan/pallas_call | solution.py:283
  54.4 0.6 fusion.18.near
  55.0 0.8 copy-done.1
  55.8 41.5 %main.1 = (f32[24,128]{1,0:T(8,128)}, f32[8,128]{1,0:T(8,128)}) custom-call(s32[1]{0:T(128)S(6)} %copy.21.counts, s32[24,27]{1,0:T(8,128)} %fusion.18.near, f32[6,6,24,128]{3,2,1,0:T(8,128)} %copy-done, f32[6,6,24,128]{3,2,1,0:T(8,128)} %copy-done.1, bf16[7680,384]{1,0:T(8,128)(2,1)} %get-tuple-element.8.hits_hbm, bf16[316,121,121]{2,1,0:T(8,128)(2,1)} %copy.14.m2l_hbm, ...), custom_call_target="tpu_custom_call" | custom-call | tf_op jit(solution)/shard_map/main/pallas_call | solution.py:310
  97.8 1.0 collective-permute-done.6
  98.8 0.7 add.88
  99.5 1.5 %collective-permute-start.7 = (f32[8,128]{1,0:T(8,128)S(1)}, f32[8,128]{1,0:T(8,128)S(1)}, u32[]{:S(2)}, u32[]{:S(2)}) collective-permute-start(f32[8,128]{1,0:T(8,128)S(1)} %add.88), channel_id=1, source_target_pairs={{0,2},{1,3},{2,0},{3,1},{4,6},{5,7},{6,4},{7,5},{8,10},{9,11},{10,... | collective-permute-start | bytes 12296 | tf_op jit(solution)/shard_map/ppermute | solution.py:240
  101.0 2.1 %collective-permute-done.7 = f32[8,128]{1,0:T(8,128)S(1)} collective-permute-done((f32[8,128]{1,0:T(8,128)S(1)}, f32[8,128]{1,0:T(8,128)S(1)}, u32[]{:S(2)}, u32[]{:S(2)}) %collective-permute-start.7) | collective-permute-done | bytes 4128 | tf_op jit(solution)/shard_map/ppermute | solution.py:240
  103.1 2.3 %collective-permute-start.8 = (f32[8,128]{1,0:T(8,128)S(1)}, f32[8,128]{1,0:T(8,128)S(1)}, u32[]{:S(2)}, u32[]{:S(2)}) collective-permute-start(f32[8,128]{1,0:T(8,128)S(1)} %add.89), channel_id=1, source_target_pairs={{0,4},{4,0},{8,12},{12,8},{16,20},{20,16},{24,28},{28,24},{1,5},{5... | collective-permute-start | bytes 12296 | tf_op jit(solution)/shard_map/ppermute | solution.py:240
  105.5 1.6 %collective-permute-done.8 = f32[8,128]{1,0:T(8,128)S(1)} collective-permute-done((f32[8,128]{1,0:T(8,128)S(1)}, f32[8,128]{1,0:T(8,128)S(1)}, u32[]{:S(2)}, u32[]{:S(2)}) %collective-permute-start.8) | collective-permute-done | bytes 4128 | tf_op jit(solution)/shard_map/ppermute | solution.py:240
  107.0 2.1 %collective-permute-start.9 = (f32[8,128]{1,0:T(8,128)S(1)}, f32[8,128]{1,0:T(8,128)S(1)}, u32[]{:S(2)}, u32[]{:S(2)}) collective-permute-start(f32[8,128]{1,0:T(8,128)S(1)} %add.90), channel_id=1, source_target_pairs={{0,8},{4,12},{8,0},{12,4},{16,24},{20,28},{24,16},{28,20},{1,9},{5... | collective-permute-start | bytes 12296 | tf_op jit(solution)/shard_map/ppermute | solution.py:240
  109.1 1.6 %collective-permute-done.9 = f32[8,128]{1,0:T(8,128)S(1)} collective-permute-done((f32[8,128]{1,0:T(8,128)S(1)}, f32[8,128]{1,0:T(8,128)S(1)}, u32[]{:S(2)}, u32[]{:S(2)}) %collective-permute-start.9) | collective-permute-done | bytes 4128 | tf_op jit(solution)/shard_map/ppermute | solution.py:240
  110.7 3.0 %collective-permute-start.10 = (f32[8,128]{1,0:T(8,128)S(1)}, f32[8,128]{1,0:T(8,128)S(1)}, u32[]{:S(2)}, u32[]{:S(2)}) collective-permute-start(f32[8,128]{1,0:T(8,128)S(1)} %add.91), channel_id=1, source_target_pairs={{0,16},{4,20},{8,24},{12,28},{16,0},{20,4},{24,8},{28,12},{1,17},{... | collective-permute-start | bytes 12296 | tf_op jit(solution)/shard_map/ppermute | solution.py:240
  113.7 1.6 %collective-permute-done.10 = f32[8,128]{1,0:T(8,128)S(1)} collective-permute-done((f32[8,128]{1,0:T(8,128)S(1)}, f32[8,128]{1,0:T(8,128)S(1)}, u32[]{:S(2)}, u32[]{:S(2)}) %collective-permute-start.10) | collective-permute-done | bytes 4128 | tf_op jit(solution)/shard_map/ppermute | solution.py:240
  115.9 1.9 %final.1 = (f32[24,128]{1,0:T(8,128)}, f32[1,128]{1,0:T(1,128)}) custom-call(s32[1]{0:T(128)S(6)} %copy.21.counts, f32[8,24,128]{2,1,0:T(8,128)} %basis.7, f32[24,128]{1,0:T(8,128)} %get-tuple-element.10.image, f32[8,128]{1,0:T(8,128)} %add.92.tile), custom_call_target="tpu_custom_call" | custom-call | tf_op jit(solution)/shard_map/final/pallas_call | solution.py:340
  117.8 1.1 slice_bitcast_fusion
  (20 shorter events, 1.7 us)
Async XLA Ops:
  7.3 5.5 %collective-permute-start.1 = (f32[6,24,128]{2,1,0:T(8,128)}, f32[6,24,128]{2,1,0:T(8,128)S(1)}, u32[]{:S(2)}, u32[]{:S(2)}) collective-permute-start(f32[6,24,128]{2,1,0:T(8,128)} %prep.1), channel_id=1, source_target_pairs={{0,4},{4,0},{8,12},{12,8},{16,20},{20,16},{24,28},{28,24},{1,5},{5... | collective-permute-start | bytes 221192 | tf_op jit(solution)/shard_map/ppermute | solution.py:240
  10.2 8.1 %collective-permute-start = (f32[6,24,128]{2,1,0:T(8,128)}, f32[6,24,128]{2,1,0:T(8,128)S(1)}, u32[]{:S(2)}, u32[]{:S(2)}) collective-permute-start(f32[6,24,128]{2,1,0:T(8,128)} %prep.1), channel_id=1, source_target_pairs={{0,2},{1,3},{2,0},{3,1},{4,6},{5,7},{6,4},{7,5},{8,10},{9,11},{10,... | collective-permute-start | bytes 221192 | tf_op jit(solution)/shard_map/ppermute | solution.py:240
  12.8 5.9 %collective-permute-start.3 = (f32[6,24,128]{2,1,0:T(8,128)S(1)}, f32[6,24,128]{2,1,0:T(8,128)S(1)}, u32[]{:S(2)}, u32[]{:S(2)}) collective-permute-start(f32[6,24,128]{2,1,0:T(8,128)S(1)} %collective-permute-done.1), channel_id=1, source_target_pairs={{0,8},{8,16},{12,4},{16,24},{20,12},{28,20},{1,9},{9,17},{13,5},{1... | collective-permute-start | bytes 221192 | tf_op jit(solution)/shard_map/ppermute | solution.py:246
  16.8 4.4 %collective-permute-start.2 = (f32[6,24,128]{2,1,0:T(8,128)S(1)}, f32[6,24,128]{2,1,0:T(8,128)S(1)}, u32[]{:S(2)}, u32[]{:S(2)}) collective-permute-start(f32[6,24,128]{2,1,0:T(8,128)S(1)} %collective-permute-done.1), channel_id=1, source_target_pairs={{0,2},{1,3},{2,0},{3,1},{4,6},{5,7},{6,4},{7,5},{8,10},{9,11},{10,... | collective-permute-start | bytes 221192 | tf_op jit(solution)/shard_map/ppermute | solution.py:240
  18.7 4.4 %collective-permute-start.4 = (f32[6,24,128]{2,1,0:T(8,128)S(1)}, f32[6,24,128]{2,1,0:T(8,128)S(1)}, u32[]{:S(2)}, u32[]{:S(2)}) collective-permute-start(f32[6,24,128]{2,1,0:T(8,128)S(1)} %collective-permute-done.3), channel_id=1, source_target_pairs={{0,2},{1,3},{2,0},{3,1},{4,6},{5,7},{6,4},{7,5},{8,10},{9,11},{10,... | collective-permute-start | bytes 221192 | tf_op jit(solution)/shard_map/ppermute | solution.py:240
  23.1 19.6 %copy-start = (f32[6,6,24,128]{3,2,1,0:T(8,128)}, f32[6,6,24,128]{3,2,1,0:T(8,128)S(1)}, u32[]{:S(2)}) copy-start(f32[6,6,24,128]{3,2,1,0:T(8,128)S(1)} %bitcast_dynamic-update-slice_fusion.here) | copy-start | bytes 1327108
  23.1 31.9 %collective-permute-start.5 = (f32[6,6,24,128]{3,2,1,0:T(8,128)S(1)}, f32[6,6,24,128]{3,2,1,0:T(8,128)S(1)}, u32[]{:S(2)}, u32[]{:S(2)}) collective-permute-start(f32[6,6,24,128]{3,2,1,0:T(8,128)S(1)} %bitcast_dynamic-update-slice_fusion.here), channel_id=1, source_target_pairs={{0,1},{1,0},{2,3},{3,2},{4,5},{5,4},{6,7},{7,6},{8,9},{9,8},{10,11... | collective-permute-start | bytes 1327112 | tf_op jit(solution)/shard_map/ppermute | solution.py:240
  28.4 25.9 %copy-start.2 = (s32[24,27]{1,0:T(8,128)S(1)}, s32[24,27]{1,0:T(8,128)}, u32[]{:S(2)}) copy-start(s32[24,27]{1,0:T(8,128)} %param.17) | copy-start | bytes 7780
  55.0 0.8 copy-start.1
  97.3 1.5 %collective-permute-start.6 = (f32[8,128]{1,0:T(8,128)}, f32[8,128]{1,0:T(8,128)S(1)}, u32[]{:S(2)}, u32[]{:S(2)}) collective-permute-start(f32[8,128]{1,0:T(8,128)} %get-tuple-element.11), channel_id=1, source_target_pairs={{0,1},{1,0},{2,3},{3,2},{4,5},{5,4},{6,7},{7,6},{8,9},{9,8},{10,11... | collective-permute-start | bytes 12296 | tf_op jit(solution)/shard_map/ppermute | solution.py:240
  99.5 3.6 %collective-permute-start.7 = (f32[8,128]{1,0:T(8,128)S(1)}, f32[8,128]{1,0:T(8,128)S(1)}, u32[]{:S(2)}, u32[]{:S(2)}) collective-permute-start(f32[8,128]{1,0:T(8,128)S(1)} %add.88), channel_id=1, source_target_pairs={{0,2},{1,3},{2,0},{3,1},{4,6},{5,7},{6,4},{7,5},{8,10},{9,11},{10,... | collective-permute-start | bytes 12296 | tf_op jit(solution)/shard_map/ppermute | solution.py:240
  103.1 3.9 %collective-permute-start.8 = (f32[8,128]{1,0:T(8,128)S(1)}, f32[8,128]{1,0:T(8,128)S(1)}, u32[]{:S(2)}, u32[]{:S(2)}) collective-permute-start(f32[8,128]{1,0:T(8,128)S(1)} %add.89), channel_id=1, source_target_pairs={{0,4},{4,0},{8,12},{12,8},{16,20},{20,16},{24,28},{28,24},{1,5},{5... | collective-permute-start | bytes 12296 | tf_op jit(solution)/shard_map/ppermute | solution.py:240
  107.0 3.7 %collective-permute-start.9 = (f32[8,128]{1,0:T(8,128)S(1)}, f32[8,128]{1,0:T(8,128)S(1)}, u32[]{:S(2)}, u32[]{:S(2)}) collective-permute-start(f32[8,128]{1,0:T(8,128)S(1)} %add.90), channel_id=1, source_target_pairs={{0,8},{4,12},{8,0},{12,4},{16,24},{20,28},{24,16},{28,20},{1,9},{5... | collective-permute-start | bytes 12296 | tf_op jit(solution)/shard_map/ppermute | solution.py:240
  110.7 4.6 %collective-permute-start.10 = (f32[8,128]{1,0:T(8,128)S(1)}, f32[8,128]{1,0:T(8,128)S(1)}, u32[]{:S(2)}, u32[]{:S(2)}) collective-permute-start(f32[8,128]{1,0:T(8,128)S(1)} %add.91), channel_id=1, source_target_pairs={{0,16},{4,20},{8,24},{12,28},{16,0},{20,4},{24,8},{28,12},{1,17},{... | collective-permute-start | bytes 12296 | tf_op jit(solution)/shard_map/ppermute | solution.py:240

commit v2 on v1

v2 whole, which is shorter than its diff:
```python
import functools

import jax
import jax.numpy as jnp
from jax import lax
from jax.experimental import pallas as pl
from jax.experimental.pallas import tpu as pltpu
from jax.sharding import PartitionSpec as P

four_pi = 12.566370614359172
epsilon = 1e-06
bf16 = jnp.bfloat16
f32 = jnp.float32
WIDTH = 32
LIMIT = 56 * 1024 * 1024

across = (((1,), (1,)), ((), ()))


def vmem(count):
    return [pl.BlockSpec(memory_space=pltpu.VMEM)] * count


def smem(count):
    return [pl.BlockSpec(memory_space=pltpu.SMEM)] * count


def live_rows(counts, shape):
    return (lax.broadcasted_iota(jnp.int32, shape, 0) < counts[0]).astype(f32)


def prep_kernel(counts, basis, coords, areas, p2m, block):
    leaves, panels = areas.shape
    terms = p2m.shape[0]
    current = basis[basis.shape[0] - 1] * live_rows(counts, (leaves, panels))
    rounded = current.astype(bf16).astype(f32)
    lane = lax.broadcasted_iota(jnp.int32, (leaves, panels), 1)
    poles = jnp.zeros((leaves, panels), f32)
    for k in range(terms):
        moved = jnp.sum(p2m[k].astype(f32) * rounded, axis=1, keepdims=True)
        poles = jnp.where(lane == k, moved, poles)
    for c in range(3):
        block[c] = coords[c]
    block[3] = areas[...]
    block[4] = areas[...] * current * (1.0 / four_pi)
    block[5] = poles


def plan_kernel(groups, counts, place, basis, near, far, offset, near_slots, slots, classes, gram):
    krylov, leaves, panels = basis.shape
    half = groups // 2
    span = groups * leaves
    me = place[0]
    order_low = place[1]

    def slot_of(window):
        low = (window < span).astype(jnp.int32)
        high = (window >= 2 * span).astype(jnp.int32)
        order = low * order_low + high * (3 - order_low)
        inner = window - span * (1 - low + high)
        group = jnp.zeros_like(window)
        for g in range(1, groups):
            group += (inner >= g * leaves).astype(jnp.int32)
        relative = group ^ me
        core = relative & 1
        column = core * (3 * half) + order * half + lax.shift_right_logical(relative, 1)
        return column * leaves + inner - group * leaves

    near_slots[...] = slot_of(near[...])
    count = far.shape[1]
    slots[...] = jnp.full(slots.shape, -1, jnp.int32)
    slots[:, 0:count] = slot_of(far[...])
    classes[...] = jnp.full(classes.shape, -1, jnp.int32)
    classes[:, 0:count] = offset[...]

    live = live_rows(counts, (leaves, panels))
    masked = [basis[j] * live for j in range(krylov)]
    lane = lax.broadcasted_iota(jnp.int32, (krylov, panels), 1)
    tile = jnp.zeros((krylov, panels), f32)
    for j in range(krylov):
        rows_j = [jnp.sum(masked[i] * masked[j], axis=0, keepdims=True) for i in range(krylov)]
        column = jnp.sum(jnp.concatenate(rows_j, axis=0), axis=1, keepdims=True)
        tile = jnp.where(lane == krylov + j, column, tile)
    population = (jnp.minimum(counts[0], leaves) * panels).astype(f32)
    gram[...] = jnp.where(lane == 2, population, tile)


def thirds(value):
    first = value.astype(bf16).astype(f32)
    second = (value - first).astype(bf16).astype(f32)
    return first, second, value - first - second


pairs = ((0, 0), (0, 1), (1, 0), (1, 1), (0, 2), (2, 0))


def main_kernel(
    counts, near, here, there, slots, classes, m2l_hbm, l2p, basis, gram,
    image_out, tile_out,
    m2l, source32, source16, target32, target16, charge, poles32, sums, totals, found, sem,
):
    krylov, leaves, panels = basis.shape
    blocks = here.shape[0]
    terms = l2p.shape[0]
    offsets = m2l.shape[1]
    padded = found.shape[1]
    entries = slots.shape[1]
    copy = pltpu.make_async_copy(m2l_hbm, m2l, sem)
    copy.start()

    ones = jnp.ones((leaves, panels), f32)
    zeros = jnp.zeros((leaves, panels), f32)

    def place(ref, base, rows):
        for k in range(WIDTH):
            value = rows[k] if k < len(rows) else zeros
            ref[pl.ds(base * WIDTH + k, leaves, stride=WIDTH), :] = value

    poles32[...] = jnp.zeros_like(poles32)
    for b in range(2 * blocks):
        got = here if b < blocks else there
        at = b % blocks
        point = [got[at, c] for c in range(3)]
        area = got[at, 3]
        area = jnp.where(area > 0.0, area, 1.0)
        split = [thirds(p) for p in point]
        square = point[0] * point[0] + point[1] * point[1] + point[2] * point[2]
        rows = [split[c][q] for c in range(3) for (_, q) in pairs]
        place(source32, b * leaves, rows + list(thirds(square + area)) + [ones] * 3)
        if b == 0:
            rows = [split[c][p] * (-2.0) for c in range(3) for (p, _) in pairs]
            place(target32, 0, rows + [ones] * 3 + list(thirds(square)))
        charge[pl.ds(b * leaves, leaves), :] = got[at, 4]
        poles32[pl.ds(b * leaves, leaves), :] = got[at, 5]
    source16[...] = source32[...].astype(bf16)
    for leaf in range(leaves):
        target16[leaf] = target32[leaf * WIDTH : (leaf + 1) * WIDTH, :].T.astype(bf16)

    neighbours = near.shape[1]

    def near_body(leaf):
        total = jnp.zeros((panels, panels), f32)
        for start in range(0, neighbours, 2):
            ids = [near[leaf, e] for e in range(start, min(start + 2, neighbours))]
            source = [source16[pl.ds(pl.multiple_of(s * WIDTH, WIDTH), WIDTH), :] for s in ids]
            source = jnp.concatenate(source, axis=1) if len(ids) > 1 else source[0]
            inverse = lax.rsqrt(jnp.dot(target16[leaf], source, preferred_element_type=f32))
            for e, s in enumerate(ids):
                total += inverse[:, e * panels : (e + 1) * panels] * charge[pl.ds(s, 1), :]
        totals[leaf] = total

    repeat(leaves, 4, near_body)
    nearby = jnp.concatenate(
        [jnp.sum(totals[leaf].T, axis=0, keepdims=True) for leaf in range(leaves)], axis=0
    )

    pole = poles32[...].T
    high = pole.astype(bf16)
    poles16 = jnp.concatenate([high, (pole - high.astype(f32)).astype(bf16)], axis=0)
    window = poles16.shape[1]

    def class_body(leaf):
        slot = slots[pl.ds(leaf, 1), :]
        offset = classes[pl.ds(leaf, 1), :]
        by_slot = lax.broadcasted_iota(jnp.int32, (window, entries), 0) == slot
        by_class = lax.broadcasted_iota(jnp.int32, (padded, entries), 0) == offset
        taken = jnp.dot(poles16, by_slot.astype(f32).astype(bf16), preferred_element_type=f32)
        both = lax.dot_general(
            by_class.astype(f32).astype(bf16),
            taken.astype(bf16),
            across,
            preferred_element_type=f32,
        )
        found[leaf] = both[:, 0:panels] + both[:, panels : 2 * panels]

    repeat(leaves, 4, class_body)
    copy.wait()

    group = 8
    filler = jnp.zeros((terms * group, panels - terms), bf16)

    def translate(table, at):
        part = found[:, pl.ds(at, group), :].reshape(leaves * group, panels)
        first = part.astype(bf16)
        second = (part - first.astype(f32)).astype(bf16)
        table = jnp.concatenate([table.reshape(terms * group, terms), filler], axis=1)
        return lax.dot_general(
            jnp.concatenate([table, table], axis=1),
            jnp.concatenate([first, second], axis=1),
            across,
            preferred_element_type=f32,
        )

    full = offsets // group
    rest = offsets % group
    sums[...] = jnp.zeros_like(sums)
    if rest:
        tail = m2l[:, full * group : offsets, :].astype(f32)
        tail = jnp.concatenate([tail, jnp.zeros((terms, group - rest, terms), f32)], axis=1)
        sums[...] = translate(tail.reshape(terms * group, terms).astype(bf16), full * group)
    batch = next(n for n in range(min(13, full), 0, -1) if full % n == 0)

    def far_body(step, carry):
        value = None
        for i in range(batch):
            at = pl.multiple_of((step * batch + i) * group, group)
            one = translate(m2l[:, pl.ds(at, group), :], at)
            value = one if value is None else value + one
        sums[...] += value
        return carry

    lax.fori_loop(0, full // batch, far_body, 0)
    spread = leaves * group
    row = lax.broadcasted_iota(jnp.int32, (terms * group, spread), 0) & (group - 1)
    lane = lax.broadcasted_iota(jnp.int32, (terms * group, spread), 1) & (group - 1)
    kept = jnp.where(row == lane, sums[...], 0.0)
    kept = jnp.sum(kept.reshape(terms, group, spread), axis=1)
    owner = lax.broadcasted_iota(jnp.int32, (leaves, spread), 0) * group
    lane = lax.broadcasted_iota(jnp.int32, (leaves, spread), 1)
    pick = ((lane >= owner) & (lane < owner + group)).astype(f32).astype(bf16)
    local = jnp.zeros((leaves, terms), f32)
    for part in thirds(kept):
        local += lax.dot_general(pick, part.astype(bf16), across, preferred_element_type=f32)
    local = local.astype(bf16).astype(f32)
    distant = zeros
    for k in range(terms):
        distant += l2p[k].astype(f32) * local[:, k : k + 1]

    live = live_rows(counts, (leaves, panels))
    current = basis[krylov - 1] * live
    image = (0.5 * current + nearby + distant) * live
    image_out[...] = image
    rows = [jnp.sum(basis[j] * live * image, axis=0, keepdims=True) for j in range(krylov)]
    product = jnp.sum(jnp.concatenate(rows, axis=0), axis=1, keepdims=True)
    energy = jnp.sum(jnp.sum(image * image, axis=0, keepdims=True), axis=1, keepdims=True)
    lane = lax.broadcasted_iota(jnp.int32, (krylov, panels), 1)
    tile_out[...] = jnp.where(lane == 0, product, jnp.where(lane == 1, energy, gram[...]))


def repeat(count, most, body):
    batch = next(n for n in range(most, 0, -1) if count % n == 0)

    def several(step, carry):
        for i in range(batch):
            body(step * batch + i)
        return carry

    lax.fori_loop(0, count // batch, several, 0)


def final_kernel(counts, basis, image, tile, vector, column):
    krylov, leaves, panels = basis.shape
    sums = tile[...]
    population = sums[0:1, 2:3]
    energy = sums[0:1, 1:2]
    products = sums[:, 0:1]
    coefficients = products / population
    row = lax.broadcasted_iota(jnp.int32, (krylov, panels), 0)
    lane = lax.broadcasted_iota(jnp.int32, (krylov, panels), 1)
    in_gram = (lane >= krylov) & (lane < 2 * krylov)
    applied = jnp.sum(jnp.where(in_gram, coefficients * sums, 0.0), axis=0, keepdims=True)
    across_lanes = jnp.sum(jnp.where(lane == krylov + row, coefficients, 0.0), axis=0, keepdims=True)
    curvature = jnp.sum(applied * across_lanes, axis=1, keepdims=True)
    crossed = jnp.sum(coefficients * products, axis=0, keepdims=True)
    squares = energy - 2.0 * crossed + curvature
    scale = jnp.sqrt(squares / population + epsilon)
    live = live_rows(counts, (leaves, panels))
    residue = image[...]
    for j in range(krylov):
        residue = residue - coefficients[j : j + 1, 0:1] * (basis[j] * live)
    vector[...] = residue / scale
    placed = jnp.sum(jnp.where(lane == row, coefficients, 0.0), axis=0, keepdims=True)
    column[...] = jnp.where(lane[0:1] == krylov, scale, placed)


def swap(value, axis, bit):
    count = lax.axis_size(axis)
    return lax.ppermute(value, axis, [(i, i ^ bit) for i in range(count)])


def hop(value, axis):
    count = lax.axis_size(axis)
    moves = [(i, i + 2 if i % 2 == 0 else i - 2) for i in range(count)]
    return lax.ppermute(value, axis, [(i, k) for i, k in moves if 0 <= k < count])


def on_device(basis, coords, areas, p2m, l2p, m2l, counts, near_list, far_list, far_offset):
    krylov, leaves, panels = basis.shape
    coords = jnp.transpose(coords, (1, 0, 2))
    p2m = jnp.transpose(p2m, (1, 0, 2))
    l2p = jnp.transpose(l2p, (2, 0, 1))
    m2l = jnp.transpose(m2l, (1, 0, 2))
    terms, offsets = m2l.shape[:2]
    groups = lax.axis_size("grp")
    params = pltpu.CompilerParams(vmem_limit_bytes=LIMIT)
    even = 1 - lax.axis_index("seg") % 2
    position = jnp.stack([lax.axis_index("grp"), 1 + even]).astype(jnp.int32)

    block = pl.pallas_call(
        prep_kernel,
        out_shape=jax.ShapeDtypeStruct((6, leaves, panels), f32),
        in_specs=smem(1) + vmem(4),
        out_specs=pl.BlockSpec(memory_space=pltpu.VMEM),
        compiler_params=params,
        name="prep",
    )(counts, basis, coords, areas, p2m)

    window = 3 * groups * leaves
    wide = window + -window % 128
    entries = far_list.shape[1] + -far_list.shape[1] % 128
    padded = offsets + -offsets % 16
    near_slots, slots, classes, gram = pl.pallas_call(
        functools.partial(plan_kernel, groups),
        out_shape=(
            jax.ShapeDtypeStruct(near_list.shape, jnp.int32),
            jax.ShapeDtypeStruct((leaves, entries), jnp.int32),
            jax.ShapeDtypeStruct((leaves, entries), jnp.int32),
            jax.ShapeDtypeStruct((krylov, panels), f32),
        ),
        in_specs=smem(2) + vmem(4),
        out_specs=tuple(vmem(4)),
        compiler_params=params,
        name="plan",
    )(counts, position, basis, near_list, far_list, far_offset)

    def spread(value):
        whole = [value]
        bit = 2
        while bit < groups:
            whole = whole + [swap(v, "grp", bit) for v in whole]
            bit *= 2
        return whole

    beside = swap(block, "seg", 1)
    own = spread(block)
    beyond = hop(beside, "seg")
    here = jnp.stack(own + spread(beside) + spread(beyond))
    there = swap(here, "grp", 1)

    image, tile = pl.pallas_call(
        main_kernel,
        out_shape=(
            jax.ShapeDtypeStruct((leaves, panels), f32),
            jax.ShapeDtypeStruct((krylov, panels), f32),
        ),
        in_specs=smem(2) + vmem(4) + [pl.BlockSpec(memory_space=pl.ANY)] + vmem(3),
        out_specs=tuple(vmem(2)),
        scratch_shapes=[
            pltpu.VMEM(m2l.shape, bf16),
            pltpu.VMEM((window * WIDTH, panels), f32),
            pltpu.VMEM((window * WIDTH, panels), bf16),
            pltpu.VMEM((leaves * WIDTH, panels), f32),
            pltpu.VMEM((leaves, panels, WIDTH), bf16),
            pltpu.VMEM((window, panels), f32),
            pltpu.VMEM((wide, panels), f32),
            pltpu.VMEM((terms * 8, leaves * 8), f32),
            pltpu.VMEM((leaves, panels, panels), f32),
            pltpu.VMEM((leaves, padded, panels), f32),
            pltpu.SemaphoreType.DMA,
        ],
        compiler_params=params,
        name="main",
    )(counts, near_slots, here, there, slots, classes, m2l, l2p, basis, gram)

    for axis in ("grp", "seg"):
        bit = 1
        while bit < lax.axis_size(axis):
            tile = tile + swap(tile, axis, bit)
            bit *= 2

    vector, column = pl.pallas_call(
        final_kernel,
        out_shape=(
            jax.ShapeDtypeStruct((leaves, panels), f32),
            jax.ShapeDtypeStruct((1, panels), f32),
        ),
        in_specs=smem(1) + vmem(3),
        out_specs=tuple(vmem(2)),
        compiler_params=params,
        name="final",
    )(counts, basis, image, tile)
    return vector, column[0, : krylov + 1]


def solution(mesh):
    placed = (
        P(None, ("seg", "grp"), None),
        P(("seg", "grp"), None, None),
        P(("seg", "grp"), None),
        P(("seg", "grp"), None, None),
        P(("seg", "grp"), None, None),
        P(),
        P(("seg", "grp")),
        P(("seg", "grp"), None),
        P(("seg", "grp"), None),
        P(("seg", "grp"), None),
    )
    return jax.shard_map(
        on_device,
        mesh=mesh,
        in_specs=placed,
        out_specs=(P(("seg", "grp"), None), P()),
        check_vma=False,
    )
```

time: 120 us -> 76.7 us (0.64)
  local copies, waits for them, and re-layouts: 25 us -> 2.84 us
  Pallas kernels: 57.5 us -> 35.9 us
  waiting for transfers between devices: 11.2 us -> 14.8 us
  starting transfers between devices: 21 us -> 19.5 us
    unnamed x15 -> x9, local copies, waits for them, and re-layouts: 22 us -> 1.7 us
    pallas_call x1, Pallas kernels: 41.5 us -> 30.1 us  [on_device(): pl.pallas_call(main_kernel, out_shape=(jax.ShapeDtypeStruct((leaves, pane...]
    pallas_call x1, Pallas kernels: 11.7 us -> 1.66 us  [on_device(): pl.pallas_call(functools.partial(plan_kernel, groups), out_shape=(jax.Sha...]
    ppermute x10, waiting for transfers between devices: 10.9 us -> 12.9 us  [swap(): return lax.ppermute(value, axis, [(i, i ^ bit) for i in range(count)])]
    pad x2 -> x0, local copies, waits for them, and re-layouts: 1.97 us -> none  [the longest x1 1.35 us: on_device(): classes = jnp.pad(far_offset, ((0, 0), (0, pad)), constant_values=-1)]
    ppermute x1, waiting for transfers between devices: 0.38 us -> 1.92 us  [hop(): lax.ppermute(value, axis, [(i, k) for i, k in moves if 0 <= k < count])]
    add x2 -> x0, other arithmetic: 1.52 us -> none  [slot_of(): (relative % 2 * 3 * half + order * half + relative // 2) * leaves]
    ppermute x10, starting transfers between devices: 17 us -> 15.6 us  [swap(): return lax.ppermute(value, axis, [(i, i ^ bit) for i in range(count)])]
  transfers between devices with their start and end apart: 11 -> 11, of which waited for: 9 -> 8; matrix products, arithmetic and copies ran while one was open for 18% -> 2% of each run, Pallas kernels for 10% -> 2%
where the time goes in v2:
time: 76.7 us; the launch traced here: 76.3 us
  Pallas kernels  35.9 us (47%)
  starting transfers between devices  19.5 us (25%)
  waiting for transfers between devices  14.8 us (19%)
  local copies, waits for them, and re-layouts  2.84 us (4%)
  other arithmetic  1.9 us (2%)
  between operations  1.38 us (2%)
    pallas_call x1, Pallas kernels, on_device(): pl.pallas_call(main_kernel, out_shape=(jax.ShapeDtypeStruct((leaves, pane...  30.1 us
    ppermute x10, starting transfers between devices, swap(): return lax.ppermute(value, axis, [(i, i ^ bit) for i in range(count)])  15.6 us
    ppermute x10, waiting for transfers between devices, swap(): return lax.ppermute(value, axis, [(i, i ^ bit) for i in range(count)])  12.9 us
    ppermute x1, starting transfers between devices, hop(): lax.ppermute(value, axis, [(i, k) for i, k in moves if 0 <= k < count])  3.94 us
    pallas_call x1, Pallas kernels, on_device(): pl.pallas_call(prep_kernel, out_shape=jax.ShapeDtypeStruct((6, leaves, pa...  2.3 us
    ppermute x1, waiting for transfers between devices, hop(): lax.ppermute(value, axis, [(i, k) for i, k in moves if 0 <= k < count])  1.92 us
    pallas_call x1, Pallas kernels, on_device(): pl.pallas_call(final_kernel, out_shape=(jax.ShapeDtypeStruct((leaves, pan...  1.86 us
    unnamed x9, local copies, waits for them, and re-layouts  1.7 us
  transfers between devices with their start and end apart: 11, of which 8 were waited for; matrix products, arithmetic and copies ran while one was open for 2% of the time, Pallas kernels for 2%

profile of v2, /device:TPU:0, one launch (start us, length us, event | category | flops | bytes accessed | tf_op | source)
XLA Modules:
  0.0 76.3 jit_solution(616538322071109665)
XLA Ops:
  1.3 2.3 %prep.1 = f32[6,24,128]{2,1,0:T(8,128)} custom-call(s32[1]{0:T(128)S(6)} %copy.17.counts, f32[8,24,128]{2,1,0:T(8,128)} %basis.7, f32[3,24,128]{2,1,0:T(8,128)} %bitcast.23, f32[24,128]{1,0:T(8,128)} %areas.1, bf16[121,24,128]{2,1,0:T(8,128)(2,1)} %bitcast.21), custom_call_target="tpu_custom_call" | custom-call | tf_op jit(solution)/shard_map/prep/pallas_call | solution.py:299
  3.6 2.9 %collective-permute-start = (f32[6,24,128]{2,1,0:T(8,128)}, f32[6,24,128]{2,1,0:T(8,128)S(1)}, u32[]{:S(2)}, u32[]{:S(2)}) collective-permute-start(f32[6,24,128]{2,1,0:T(8,128)} %prep.1), channel_id=1, source_target_pairs={{0,2},{1,3},{2,0},{3,1},{4,6},{5,7},{6,4},{7,5},{8,10},{9,11},{10,... | collective-permute-start | bytes 221192 | tf_op jit(solution)/shard_map/ppermute | solution.py:278
  6.5 1.5 %collective-permute-start.1 = (f32[6,24,128]{2,1,0:T(8,128)}, f32[6,24,128]{2,1,0:T(8,128)S(1)}, u32[]{:S(2)}, u32[]{:S(2)}) collective-permute-start(f32[6,24,128]{2,1,0:T(8,128)} %prep.1), channel_id=1, source_target_pairs={{0,4},{4,0},{8,12},{12,8},{16,20},{20,16},{24,28},{28,24},{1,5},{5... | collective-permute-start | bytes 221192 | tf_op jit(solution)/shard_map/ppermute | solution.py:278
  8.0 0.9 %bitcast_dynamic-update-slice_fusion.5 = f32[6,6,24,128]{3,2,1,0:T(8,128)S(1)} fusion(f32[6,24,128]{2,1,0:T(8,128)} %prep.1), kind=kLoop, calls=%fused_computation.5 | loop fusion | bytes 147456
  9.0 2.1 %collective-permute-done.1 = f32[6,24,128]{2,1,0:T(8,128)S(1)} collective-permute-done((f32[6,24,128]{2,1,0:T(8,128)}, f32[6,24,128]{2,1,0:T(8,128)S(1)}, u32[]{:S(2)}, u32[]{:S(2)}) %collective-permute-start.1) | collective-permute-done | bytes 73760 | tf_op jit(solution)/shard_map/ppermute | solution.py:278
  11.1 0.1 collective-permute-start.2
  11.1 3.9 %collective-permute-start.3 = (f32[6,24,128]{2,1,0:T(8,128)S(1)}, f32[6,24,128]{2,1,0:T(8,128)S(1)}, u32[]{:S(2)}, u32[]{:S(2)}) collective-permute-start(f32[6,24,128]{2,1,0:T(8,128)S(1)} %collective-permute-done.1), channel_id=1, source_target_pairs={{0,8},{8,16},{12,4},{16,24},{20,12},{28,20},{1,9},{9,17},{13,5},{1... | collective-permute-start | bytes 221192 | tf_op jit(solution)/shard_map/ppermute | solution.py:284
  15.1 0.0 collective-permute-done
  15.1 1.9 %collective-permute-done.3 = f32[6,24,128]{2,1,0:T(8,128)S(1)} collective-permute-done((f32[6,24,128]{2,1,0:T(8,128)S(1)}, f32[6,24,128]{2,1,0:T(8,128)S(1)}, u32[]{:S(2)}, u32[]{:S(2)}) %collective-permute-start.3) | collective-permute-done | bytes 73760 | tf_op jit(solution)/shard_map/ppermute | solution.py:284
  17.1 1.5 %collective-permute-start.4 = (f32[6,24,128]{2,1,0:T(8,128)S(1)}, f32[6,24,128]{2,1,0:T(8,128)S(1)}, u32[]{:S(2)}, u32[]{:S(2)}) collective-permute-start(f32[6,24,128]{2,1,0:T(8,128)S(1)} %collective-permute-done.3), channel_id=1, source_target_pairs={{0,2},{1,3},{2,0},{3,1},{4,6},{5,7},{6,4},{7,5},{8,10},{9,11},{10,... | collective-permute-start | bytes 221192 | tf_op jit(solution)/shard_map/ppermute | solution.py:278
  18.6 0.0 collective-permute-done.2
  18.6 2.8 %collective-permute-done.4 = f32[6,24,128]{2,1,0:T(8,128)S(1)} collective-permute-done((f32[6,24,128]{2,1,0:T(8,128)S(1)}, f32[6,24,128]{2,1,0:T(8,128)S(1)}, u32[]{:S(2)}, u32[]{:S(2)}) %collective-permute-start.4) | collective-permute-done | bytes 73760 | tf_op jit(solution)/shard_map/ppermute | solution.py:278
  21.4 0.1 collective-permute-start.5
  21.5 0.6 pad_add_fusion.place
  22.1 1.7 %plan.1 = (s32[24,27]{1,0:T(8,128)}, s32[24,256]{1,0:T(8,128)}, s32[24,256]{1,0:T(8,128)}, f32[8,128]{1,0:T(8,128)}) custom-call(s32[1]{0:T(128)S(6)} %copy.17.counts, s32[2]{0:T(128)} %pad_add_fusion.place, f32[8,24,128]{2,1,0:T(8,128)} %basis.7, s32[24,27]{1,0:T(8,128)} %near.1, s32[24,189]{1,0:T(8,128)} %far.1, s32[24,189]{1,0:T(8,128)} %offset.1), custom_call_target="tpu_custom_call" | custom-call | tf_op jit(solution)/shard_map/plan/pallas_call | solution.py:312
  23.8 0.0 collective-permute-done.5.there
  23.8 0.7 copy-done.1
  24.6 30.1 %main.1 = (f32[24,128]{1,0:T(8,128)}, f32[8,128]{1,0:T(8,128)}) custom-call(s32[1]{0:T(128)S(6)} %copy.17.counts, s32[24,27]{1,0:T(8,128)} %get-tuple-element.10.near, f32[6,6,24,128]{3,2,1,0:T(8,128)} %copy-done, f32[6,6,24,128]{3,2,1,0:T(8,128)} %copy-done.1, s32[24,256]{1,0:T(8,128)} %get-tuple-element.11.slots, s32[24,256]{1,0:T(8,128)} %get-tuple-element.12.classes, ...), custom_call_target="tpu_custom_call" | custom-call | tf_op jit(solution)/shard_map/main/pallas_call | solution.py:340
  54.7 0.5 collective-permute-start.6
  55.2 1.0 %collective-permute-done.6 = f32[8,128]{1,0:T(8,128)S(1)} collective-permute-done((f32[8,128]{1,0:T(8,128)}, f32[8,128]{1,0:T(8,128)S(1)}, u32[]{:S(2)}, u32[]{:S(2)}) %collective-permute-start.6) | collective-permute-done | bytes 4128 | tf_op jit(solution)/shard_map/ppermute | solution.py:278
  56.3 0.7 add.25
  56.9 1.5 %collective-permute-start.7 = (f32[8,128]{1,0:T(8,128)S(1)}, f32[8,128]{1,0:T(8,128)S(1)}, u32[]{:S(2)}, u32[]{:S(2)}) collective-permute-start(f32[8,128]{1,0:T(8,128)S(1)} %add.25), channel_id=1, source_target_pairs={{0,2},{1,3},{2,0},{3,1},{4,6},{5,7},{6,4},{7,5},{8,10},{9,11},{10,... | collective-permute-start | bytes 12296 | tf_op jit(solution)/shard_map/ppermute | solution.py:278
  58.4 2.1 %collective-permute-done.7 = f32[8,128]{1,0:T(8,128)S(1)} collective-permute-done((f32[8,128]{1,0:T(8,128)S(1)}, f32[8,128]{1,0:T(8,128)S(1)}, u32[]{:S(2)}, u32[]{:S(2)}) %collective-permute-start.7) | collective-permute-done | bytes 4128 | tf_op jit(solution)/shard_map/ppermute | solution.py:278
  60.6 2.3 %collective-permute-start.8 = (f32[8,128]{1,0:T(8,128)S(1)}, f32[8,128]{1,0:T(8,128)S(1)}, u32[]{:S(2)}, u32[]{:S(2)}) collective-permute-start(f32[8,128]{1,0:T(8,128)S(1)} %add.26), channel_id=1, source_target_pairs={{0,4},{4,0},{8,12},{12,8},{16,20},{20,16},{24,28},{28,24},{1,5},{5... | collective-permute-start | bytes 12296 | tf_op jit(solution)/shard_map/ppermute | solution.py:278
  62.9 1.6 %collective-permute-done.8 = f32[8,128]{1,0:T(8,128)S(1)} collective-permute-done((f32[8,128]{1,0:T(8,128)S(1)}, f32[8,128]{1,0:T(8,128)S(1)}, u32[]{:S(2)}, u32[]{:S(2)}) %collective-permute-start.8) | collective-permute-done | bytes 4128 | tf_op jit(solution)/shard_map/ppermute | solution.py:278
  64.5 2.1 %collective-permute-start.9 = (f32[8,128]{1,0:T(8,128)S(1)}, f32[8,128]{1,0:T(8,128)S(1)}, u32[]{:S(2)}, u32[]{:S(2)}) collective-permute-start(f32[8,128]{1,0:T(8,128)S(1)} %add.27), channel_id=1, source_target_pairs={{0,8},{4,12},{8,0},{12,4},{16,24},{20,28},{24,16},{28,20},{1,9},{5... | collective-permute-start | bytes 12296 | tf_op jit(solution)/shard_map/ppermute | solution.py:278
  66.5 1.6 %collective-permute-done.9 = f32[8,128]{1,0:T(8,128)S(1)} collective-permute-done((f32[8,128]{1,0:T(8,128)S(1)}, f32[8,128]{1,0:T(8,128)S(1)}, u32[]{:S(2)}, u32[]{:S(2)}) %collective-permute-start.9) | collective-permute-done | bytes 4128 | tf_op jit(solution)/shard_map/ppermute | solution.py:278
  68.1 3.0 %collective-permute-start.10 = (f32[8,128]{1,0:T(8,128)S(1)}, f32[8,128]{1,0:T(8,128)S(1)}, u32[]{:S(2)}, u32[]{:S(2)}) collective-permute-start(f32[8,128]{1,0:T(8,128)S(1)} %add.28), channel_id=1, source_target_pairs={{0,16},{4,20},{8,24},{12,28},{16,0},{20,4},{24,8},{28,12},{1,17},{... | collective-permute-start | bytes 12296 | tf_op jit(solution)/shard_map/ppermute | solution.py:278
  71.2 1.6 %collective-permute-done.10 = f32[8,128]{1,0:T(8,128)S(1)} collective-permute-done((f32[8,128]{1,0:T(8,128)S(1)}, f32[8,128]{1,0:T(8,128)S(1)}, u32[]{:S(2)}, u32[]{:S(2)}) %collective-permute-start.10) | collective-permute-done | bytes 4128 | tf_op jit(solution)/shard_map/ppermute | solution.py:278
  72.8 0.6 add.29.tile
  73.3 1.9 %final.1 = (f32[24,128]{1,0:T(8,128)}, f32[1,128]{1,0:T(1,128)}) custom-call(s32[1]{0:T(128)S(6)} %copy.17.counts, f32[8,24,128]{2,1,0:T(8,128)} %basis.7, f32[24,128]{1,0:T(8,128)} %get-tuple-element.14.image, f32[8,128]{1,0:T(8,128)} %add.29.tile), custom_call_target="tpu_custom_call" | custom-call | tf_op jit(solution)/shard_map/final/pallas_call | solution.py:371
  75.2 1.1 %slice_bitcast_fusion = f32[9]{0:T(128)} fusion(f32[1,128]{1,0:T(1,128)} %get-tuple-element.17), kind=kLoop, calls=%fused_computation.7 | loop fusion | bytes 72 | tf_op jit(solution)/shard_map/squeeze | solution.py:382
  (11 shorter events, 0.1 us)
Async XLA Ops:
  3.6 11.5 %collective-permute-start = (f32[6,24,128]{2,1,0:T(8,128)}, f32[6,24,128]{2,1,0:T(8,128)S(1)}, u32[]{:S(2)}, u32[]{:S(2)}) collective-permute-start(f32[6,24,128]{2,1,0:T(8,128)} %prep.1), channel_id=1, source_target_pairs={{0,2},{1,3},{2,0},{3,1},{4,6},{5,7},{6,4},{7,5},{8,10},{9,11},{10,... | collective-permute-start | bytes 221192 | tf_op jit(solution)/shard_map/ppermute | solution.py:278
  6.5 4.6 %collective-permute-start.1 = (f32[6,24,128]{2,1,0:T(8,128)}, f32[6,24,128]{2,1,0:T(8,128)S(1)}, u32[]{:S(2)}, u32[]{:S(2)}) collective-permute-start(f32[6,24,128]{2,1,0:T(8,128)} %prep.1), channel_id=1, source_target_pairs={{0,4},{4,0},{8,12},{12,8},{16,20},{20,16},{24,28},{28,24},{1,5},{5... | collective-permute-start | bytes 221192 | tf_op jit(solution)/shard_map/ppermute | solution.py:278
  11.1 7.5 %collective-permute-start.2 = (f32[6,24,128]{2,1,0:T(8,128)S(1)}, f32[6,24,128]{2,1,0:T(8,128)S(1)}, u32[]{:S(2)}, u32[]{:S(2)}) collective-permute-start(f32[6,24,128]{2,1,0:T(8,128)S(1)} %collective-permute-done.1), channel_id=1, source_target_pairs={{0,2},{1,3},{2,0},{3,1},{4,6},{5,7},{6,4},{7,5},{8,10},{9,11},{10,... | collective-permute-start | bytes 221192 | tf_op jit(solution)/shard_map/ppermute | solution.py:278
  11.1 5.9 %collective-permute-start.3 = (f32[6,24,128]{2,1,0:T(8,128)S(1)}, f32[6,24,128]{2,1,0:T(8,128)S(1)}, u32[]{:S(2)}, u32[]{:S(2)}) collective-permute-start(f32[6,24,128]{2,1,0:T(8,128)S(1)} %collective-permute-done.1), channel_id=1, source_target_pairs={{0,8},{8,16},{12,4},{16,24},{20,12},{28,20},{1,9},{9,17},{13,5},{1... | collective-permute-start | bytes 221192 | tf_op jit(solution)/shard_map/ppermute | solution.py:284
  17.1 4.4 %collective-permute-start.4 = (f32[6,24,128]{2,1,0:T(8,128)S(1)}, f32[6,24,128]{2,1,0:T(8,128)S(1)}, u32[]{:S(2)}, u32[]{:S(2)}) collective-permute-start(f32[6,24,128]{2,1,0:T(8,128)S(1)} %collective-permute-done.3), channel_id=1, source_target_pairs={{0,2},{1,3},{2,0},{3,1},{4,6},{5,7},{6,4},{7,5},{8,10},{9,11},{10,... | collective-permute-start | bytes 221192 | tf_op jit(solution)/shard_map/ppermute | solution.py:278
  21.4 2.4 %copy-start = (f32[6,6,24,128]{3,2,1,0:T(8,128)}, f32[6,6,24,128]{3,2,1,0:T(8,128)S(1)}, u32[]{:S(2)}) copy-start(f32[6,6,24,128]{3,2,1,0:T(8,128)S(1)} %bitcast_dynamic-update-slice_fusion.here) | copy-start | bytes 1327108
  21.4 2.4 %collective-permute-start.5 = (f32[6,6,24,128]{3,2,1,0:T(8,128)S(1)}, f32[6,6,24,128]{3,2,1,0:T(8,128)S(1)}, u32[]{:S(2)}, u32[]{:S(2)}) collective-permute-start(f32[6,6,24,128]{3,2,1,0:T(8,128)S(1)} %bitcast_dynamic-update-slice_fusion.here), channel_id=1, source_target_pairs={{0,1},{1,0},{2,3},{3,2},{4,5},{5,4},{6,7},{7,6},{8,9},{9,8},{10,11... | collective-permute-start | bytes 1327112 | tf_op jit(solution)/shard_map/ppermute | solution.py:278
  23.8 0.8 copy-start.1
  54.7 1.6 %collective-permute-start.6 = (f32[8,128]{1,0:T(8,128)}, f32[8,128]{1,0:T(8,128)S(1)}, u32[]{:S(2)}, u32[]{:S(2)}) collective-permute-start(f32[8,128]{1,0:T(8,128)} %get-tuple-element.15), channel_id=1, source_target_pairs={{0,1},{1,0},{2,3},{3,2},{4,5},{5,4},{6,7},{7,6},{8,9},{9,8},{10,11... | collective-permute-start | bytes 12296 | tf_op jit(solution)/shard_map/ppermute | solution.py:278
  56.9 3.6 %collective-permute-start.7 = (f32[8,128]{1,0:T(8,128)S(1)}, f32[8,128]{1,0:T(8,128)S(1)}, u32[]{:S(2)}, u32[]{:S(2)}) collective-permute-start(f32[8,128]{1,0:T(8,128)S(1)} %add.25), channel_id=1, source_target_pairs={{0,2},{1,3},{2,0},{3,1},{4,6},{5,7},{6,4},{7,5},{8,10},{9,11},{10,... | collective-permute-start | bytes 12296 | tf_op jit(solution)/shard_map/ppermute | solution.py:278
  60.6 3.9 %collective-permute-start.8 = (f32[8,128]{1,0:T(8,128)S(1)}, f32[8,128]{1,0:T(8,128)S(1)}, u32[]{:S(2)}, u32[]{:S(2)}) collective-permute-start(f32[8,128]{1,0:T(8,128)S(1)} %add.26), channel_id=1, source_target_pairs={{0,4},{4,0},{8,12},{12,8},{16,20},{20,16},{24,28},{28,24},{1,5},{5... | collective-permute-start | bytes 12296 | tf_op jit(solution)/shard_map/ppermute | solution.py:278
  64.5 3.7 %collective-permute-start.9 = (f32[8,128]{1,0:T(8,128)S(1)}, f32[8,128]{1,0:T(8,128)S(1)}, u32[]{:S(2)}, u32[]{:S(2)}) collective-permute-start(f32[8,128]{1,0:T(8,128)S(1)} %add.27), channel_id=1, source_target_pairs={{0,8},{4,12},{8,0},{12,4},{16,24},{20,28},{24,16},{28,20},{1,9},{5... | collective-permute-start | bytes 12296 | tf_op jit(solution)/shard_map/ppermute | solution.py:278
  68.1 4.6 %collective-permute-start.10 = (f32[8,128]{1,0:T(8,128)S(1)}, f32[8,128]{1,0:T(8,128)S(1)}, u32[]{:S(2)}, u32[]{:S(2)}) collective-permute-start(f32[8,128]{1,0:T(8,128)S(1)} %add.28), channel_id=1, source_target_pairs={{0,16},{4,20},{8,24},{12,28},{16,0},{20,4},{24,8},{28,12},{1,17},{... | collective-permute-start | bytes 12296 | tf_op jit(solution)/shard_map/ppermute | solution.py:278

commit v3 on v2

--- a/solution.py
+++ b/solution.py
@@ -11,7 +11,8 @@
 epsilon = 1e-06
 bf16 = jnp.bfloat16
 f32 = jnp.float32
-WIDTH = 32
+WIDTH = 16
+CENTRE = 2.0
 LIMIT = 56 * 1024 * 1024
 
 across = (((1,), (1,)), ((), ()))
@@ -46,33 +47,49 @@
     block[5] = poles
 
 
-def plan_kernel(groups, counts, place, basis, near, far, offset, near_slots, slots, classes, gram):
-    krylov, leaves, panels = basis.shape
+def slot_of(window, groups, leaves, me, order_low):
     half = groups // 2
     span = groups * leaves
-    me = place[0]
-    order_low = place[1]
-
-    def slot_of(window):
-        low = (window < span).astype(jnp.int32)
-        high = (window >= 2 * span).astype(jnp.int32)
-        order = low * order_low + high * (3 - order_low)
-        inner = window - span * (1 - low + high)
-        group = jnp.zeros_like(window)
-        for g in range(1, groups):
-            group += (inner >= g * leaves).astype(jnp.int32)
-        relative = group ^ me
-        core = relative & 1
-        column = core * (3 * half) + order * half + lax.shift_right_logical(relative, 1)
-        return column * leaves + inner - group * leaves
-
-    near_slots[...] = slot_of(near[...])
+    low = (window < span).astype(jnp.int32)
+    high = (window >= 2 * span).astype(jnp.int32)
+    order = low * order_low + high * (3 - order_low)
+    inner = window - span * (1 - low + high)
+    group = jnp.zeros_like(window)
+    for g in range(1, groups):
+        group += (inner >= g * leaves).astype(jnp.int32)
+    relative = group ^ me
+    column = (relative & 1) * (3 * half) + order * half + lax.shift_right_logical(relative, 1)
+    return column * leaves + inner - group * leaves
+
+
+def tally_kernel(groups, leaves, first, after, place, far, offset, hits, slots, classes):
+    held, padded, wide = hits.shape
     count = far.shape[1]
+    entries = slots.shape[1]
+    rows = pl.ds(first, held)
     slots[...] = jnp.full(slots.shape, -1, jnp.int32)
-    slots[:, 0:count] = slot_of(far[...])
+    slots[:, 0:count] = slot_of(far[rows, :], groups, leaves, place[0], place[1])
     classes[...] = jnp.full(classes.shape, -1, jnp.int32)
-    classes[:, 0:count] = offset[...]
-
+    classes[:, 0:count] = offset[rows, :]
+
+    def body(leaf):
+        slot = slots[pl.ds(leaf, 1), :]
+        of_class = classes[pl.ds(leaf, 1), :]
+        by_slot = lax.broadcasted_iota(jnp.int32, (wide, entries), 0) == slot
+        by_class = lax.broadcasted_iota(jnp.int32, (padded, entries), 0) == of_class
+        hits[leaf] = lax.dot_general(
+            by_class.astype(f32).astype(bf16),
+            by_slot.astype(f32).astype(bf16),
+            across,
+            preferred_element_type=f32,
+        ).astype(bf16)
+
+    repeat(held, 4, body)
+
+
+def plan_kernel(groups, counts, place, basis, near, near_slots, gram):
+    krylov, leaves, panels = basis.shape
+    near_slots[...] = slot_of(near[...], groups, leaves, place[0], place[1])
     live = live_rows(counts, (leaves, panels))
     masked = [basis[j] * live for j in range(krylov)]
     lane = lax.broadcasted_iota(jnp.int32, (krylov, panels), 1)
@@ -91,22 +108,27 @@
     return first, second, value - first - second
 
 
-pairs = ((0, 0), (0, 1), (1, 0), (1, 1), (0, 2), (2, 0))
-
-
-def main_kernel(
-    counts, near, here, there, slots, classes, m2l_hbm, l2p, basis, gram,
-    image_out, tile_out,
-    m2l, source32, source16, target32, target16, charge, poles32, sums, totals, found, sem,
-):
+pairs = ((0, 0), (0, 1), (1, 0))
+
+
+def main_kernel(pieces, tallies, *refs):
+    counts, near = refs[0:2]
+    blocks = refs[2 : 2 + pieces]
+    hits_hbm = refs[2 + pieces : 2 + pieces + tallies]
+    m2l_hbm, l2p, basis, gram, image_out, tile_out = refs[2 + pieces + tallies : 8 + pieces + tallies]
+    hits, m2l, source32, source16, target32, target16 = refs[8 + pieces + tallies : 14 + pieces + tallies]
+    charge, poles32, sums, totals, found, sems = refs[14 + pieces + tallies :]
     krylov, leaves, panels = basis.shape
-    blocks = here.shape[0]
     terms = l2p.shape[0]
     offsets = m2l.shape[1]
-    padded = found.shape[1]
-    entries = slots.shape[1]
-    copy = pltpu.make_async_copy(m2l_hbm, m2l, sem)
-    copy.start()
+    held = leaves // tallies
+    copies = [
+        pltpu.make_async_copy(hits_hbm[i], hits.at[pl.ds(i * held, held)], sems.at[i])
+        for i in range(tallies)
+    ]
+    copies.append(pltpu.make_async_copy(m2l_hbm, m2l, sems.at[tallies]))
+    for copy in copies:
+        copy.start()
 
     ones = jnp.ones((leaves, panels), f32)
     zeros = jnp.zeros((leaves, panels), f32)
@@ -117,24 +139,26 @@
             ref[pl.ds(base * WIDTH + k, leaves, stride=WIDTH), :] = value
 
     poles32[...] = jnp.zeros_like(poles32)
-    for b in range(2 * blocks):
-        got = here if b < blocks else there
-        at = b % blocks
-        point = [got[at, c] for c in range(3)]
-        area = got[at, 3]
+    for b in range(pieces):
+        got = blocks[b]
+        point = [got[c] - CENTRE for c in range(3)]
+        area = got[3]
         area = jnp.where(area > 0.0, area, 1.0)
-        split = [thirds(p) for p in point]
+        split = [thirds(p)[0:2] for p in point]
         square = point[0] * point[0] + point[1] * point[1] + point[2] * point[2]
         rows = [split[c][q] for c in range(3) for (_, q) in pairs]
         place(source32, b * leaves, rows + list(thirds(square + area)) + [ones] * 3)
         if b == 0:
             rows = [split[c][p] * (-2.0) for c in range(3) for (p, _) in pairs]
             place(target32, 0, rows + [ones] * 3 + list(thirds(square)))
-        charge[pl.ds(b * leaves, leaves), :] = got[at, 4]
-        poles32[pl.ds(b * leaves, leaves), :] = got[at, 5]
+        charge[pl.ds(b * leaves, leaves), :] = got[4]
+        poles32[pl.ds(b * leaves, leaves), :] = got[5]
     source16[...] = source32[...].astype(bf16)
     for leaf in range(leaves):
         target16[leaf] = target32[leaf * WIDTH : (leaf + 1) * WIDTH, :].T.astype(bf16)
+    pole = poles32[...]
+    high = pole.astype(bf16)
+    poles16 = jnp.concatenate([high, (pole - high.astype(f32)).astype(bf16)], axis=1)
 
     neighbours = near.shape[1]
 
@@ -149,32 +173,18 @@
                 total += inverse[:, e * panels : (e + 1) * panels] * charge[pl.ds(s, 1), :]
         totals[leaf] = total
 
-    repeat(leaves, 4, near_body)
+    def leaf_body(leaf):
+        near_body(leaf)
+        both = jnp.dot(hits[leaf], poles16, preferred_element_type=f32)
+        found[leaf] = both[:, 0:panels] + both[:, panels : 2 * panels]
+
+    for copy in copies[:tallies]:
+        copy.wait()
+    repeat(leaves, 4, leaf_body)
     nearby = jnp.concatenate(
         [jnp.sum(totals[leaf].T, axis=0, keepdims=True) for leaf in range(leaves)], axis=0
     )
-
-    pole = poles32[...].T
-    high = pole.astype(bf16)
-    poles16 = jnp.concatenate([high, (pole - high.astype(f32)).astype(bf16)], axis=0)
-    window = poles16.shape[1]
-
-    def class_body(leaf):
-        slot = slots[pl.ds(leaf, 1), :]
-        offset = classes[pl.ds(leaf, 1), :]
-        by_slot = lax.broadcasted_iota(jnp.int32, (window, entries), 0) == slot
-        by_class = lax.broadcasted_iota(jnp.int32, (padded, entries), 0) == offset
-        taken = jnp.dot(poles16, by_slot.astype(f32).astype(bf16), preferred_element_type=f32)
-        both = lax.dot_general(
-            by_class.astype(f32).astype(bf16),
-            taken.astype(bf16),
-            across,
-            preferred_element_type=f32,
-        )
-        found[leaf] = both[:, 0:panels] + both[:, panels : 2 * panels]
-
-    repeat(leaves, 4, class_body)
-    copy.wait()
+    copies[tallies].wait()
 
     group = 8
     filler = jnp.zeros((terms * group, panels - terms), bf16)
@@ -248,9 +258,9 @@
     lax.fori_loop(0, count // batch, several, 0)
 
 
-def final_kernel(counts, basis, image, tile, vector, column):
+def final_kernel(counts, basis, image, tile, other, vector, column):
     krylov, leaves, panels = basis.shape
-    sums = tile[...]
+    sums = tile[...] + other[...]
     population = sums[0:1, 2:3]
     energy = sums[0:1, 1:2]
     products = sums[:, 0:1]
@@ -270,7 +280,8 @@
         residue = residue - coefficients[j : j + 1, 0:1] * (basis[j] * live)
     vector[...] = residue / scale
     placed = jnp.sum(jnp.where(lane == row, coefficients, 0.0), axis=0, keepdims=True)
-    column[...] = jnp.where(lane[0:1] == krylov, scale, placed)
+    placed = jnp.where(lane[0:1] == krylov, scale, placed)
+    column[...] = placed.reshape(panels)[0 : krylov + 1]
 
 
 def swap(value, axis, bit):
@@ -309,19 +320,19 @@
     wide = window + -window % 128
     entries = far_list.shape[1] + -far_list.shape[1] % 128
     padded = offsets + -offsets % 16
-    near_slots, slots, classes, gram = pl.pallas_call(
-        functools.partial(plan_kernel, groups),
-        out_shape=(
-            jax.ShapeDtypeStruct(near_list.shape, jnp.int32),
-            jax.ShapeDtypeStruct((leaves, entries), jnp.int32),
-            jax.ShapeDtypeStruct((leaves, entries), jnp.int32),
-            jax.ShapeDtypeStruct((krylov, panels), f32),
-        ),
-        in_specs=smem(2) + vmem(4),
-        out_specs=tuple(vmem(4)),
-        compiler_params=params,
-        name="plan",
-    )(counts, position, basis, near_list, far_list, far_offset)
+    tallies = 3 if leaves % 3 == 0 else 1
+    held = leaves // tallies
+
+    def tally(index, after):
+        return pl.pallas_call(
+            functools.partial(tally_kernel, groups, leaves, index * held),
+            out_shape=jax.ShapeDtypeStruct((held, padded, wide), bf16),
+            in_specs=[pl.BlockSpec(memory_space=pl.ANY)] + smem(1) + vmem(2),
+            out_specs=pl.BlockSpec(memory_space=pltpu.VMEM),
+            scratch_shapes=[pltpu.VMEM((held, entries), jnp.int32)] * 2,
+            compiler_params=params,
+            name="tally",
+        )(after, position, far_list, far_offset)
 
     def spread(value):
         whole = [value]
@@ -333,19 +344,40 @@
 
     beside = swap(block, "seg", 1)
     own = spread(block)
+    hits = [tally(0, block)]
+    beside, hits[0] = lax.optimization_barrier((beside, hits[0]))
     beyond = hop(beside, "seg")
-    here = jnp.stack(own + spread(beside) + spread(beyond))
-    there = swap(here, "grp", 1)
+    if tallies > 1:
+        hits.append(tally(1, beside))
+        beyond, hits[1] = lax.optimization_barrier((beyond, hits[1]))
+        hits.append(tally(2, beyond))
+    near_slots, gram = pl.pallas_call(
+        functools.partial(plan_kernel, groups),
+        out_shape=(
+            jax.ShapeDtypeStruct(near_list.shape, jnp.int32),
+            jax.ShapeDtypeStruct((krylov, panels), f32),
+        ),
+        in_specs=smem(2) + vmem(2),
+        out_specs=tuple(vmem(2)),
+        compiler_params=params,
+        name="plan",
+    )(counts, position, basis, near_list)
+    here = own + spread(beside) + spread(beyond)
+    blocks = here + [swap(v, "grp", 1) for v in here]
 
     image, tile = pl.pallas_call(
-        main_kernel,
+        functools.partial(main_kernel, len(blocks), tallies),
         out_shape=(
             jax.ShapeDtypeStruct((leaves, panels), f32),
             jax.ShapeDtypeStruct((krylov, panels), f32),
         ),
-        in_specs=smem(2) + vmem(4) + [pl.BlockSpec(memory_space=pl.ANY)] + vmem(3),
+        in_specs=smem(2)
+        + vmem(len(blocks))
+        + [pl.BlockSpec(memory_space=pl.ANY)] * (tallies + 1)
+        + vmem(3),
         out_specs=tuple(vmem(2)),
         scratch_shapes=[
+            pltpu.VMEM((leaves, padded, wide), bf16),
             pltpu.VMEM(m2l.shape, bf16),
             pltpu.VMEM((window * WIDTH, panels), f32),
             pltpu.VMEM((window * WIDTH, panels), bf16),
@@ -356,30 +388,32 @@
             pltpu.VMEM((terms * 8, leaves * 8), f32),
             pltpu.VMEM((leaves, panels, panels), f32),
             pltpu.VMEM((leaves, padded, panels), f32),
-            pltpu.SemaphoreType.DMA,
+            pltpu.SemaphoreType.DMA((tallies + 1,)),
         ],
         compiler_params=params,
         name="main",
-    )(counts, near_slots, here, there, slots, classes, m2l, l2p, basis, gram)
-
-    for axis in ("grp", "seg"):
-        bit = 1
-        while bit < lax.axis_size(axis):
-            tile = tile + swap(tile, axis, bit)
-            bit *= 2
-
-    vector, column = pl.pallas_call(
+    )(counts, near_slots, *blocks, *hits, m2l, l2p, basis, gram)
+
+    stages = [
+        (axis, 1 << power)
+        for axis in ("grp", "seg")
+        for power in range((lax.axis_size(axis) - 1).bit_length())
+    ]
+    for axis, bit in stages[:-1]:
+        tile = tile + swap(tile, axis, bit)
+    other = swap(tile, *stages[-1])
+
+    return pl.pallas_call(
         final_kernel,
         out_shape=(
             jax.ShapeDtypeStruct((leaves, panels), f32),
-            jax.ShapeDtypeStruct((1, panels), f32),
+            jax.ShapeDtypeStruct((krylov + 1,), f32),
         ),
-        in_specs=smem(1) + vmem(3),
+        in_specs=smem(1) + vmem(4),
         out_specs=tuple(vmem(2)),
         compiler_params=params,
         name="final",
-    )(counts, basis, image, tile)
-    return vector, column[0, : krylov + 1]
+    )(counts, basis, image, tile, other)
 
 
 def solution(mesh):

time: 76.7 us -> 71.9 us (0.937)
  starting transfers between devices: 19.5 us -> 17.2 us
  waiting for transfers between devices: 14.8 us -> 12.6 us
  Pallas kernels: 35.9 us -> 37.5 us
  local copies, waits for them, and re-layouts: 2.84 us -> 1.25 us
    ppermute x1, waiting for transfers between devices: 1.92 us -> 0.01 us  [hop(): lax.ppermute(value, axis, [(i, k) for i, k in moves if 0 <= k < count])]
    ppermute x10 -> x15, starting transfers between devices: 15.6 us -> 13.8 us  [swap(): return lax.ppermute(value, axis, [(i, i ^ bit) for i in range(count)])]
    pallas_call x1 -> x4, Pallas kernels: 30.1 us -> 31.7 us  [the longest x1 22.2 us: on_device(): pl.pallas_call(functools.partial(main_kernel, len(blocks), tallies), out_...]
    squeeze x1 -> x0, local copies, waits for them, and re-layouts: 1.13 us -> none  [on_device(): return (vector, column[0, :krylov + 1])]
    unnamed x9 -> x28, local copies, waits for them, and re-layouts: 1.7 us -> 1.25 us
    ppermute x10 -> x15, waiting for transfers between devices: 12.9 us -> 12.6 us  [swap(): return lax.ppermute(value, axis, [(i, i ^ bit) for i in range(count)])]
  transfers between devices with their start and end apart: 11 -> 16, of which waited for: 8 -> 6; matrix products, arithmetic and copies ran while one was open for 2% -> 1% of each run, Pallas kernels for 2% -> 16%
where the time goes in v3:
time: 71.9 us; the launch traced here: 71.4 us
  Pallas kernels  37.5 us (52%)
  starting transfers between devices  17.2 us (24%)
  waiting for transfers between devices  12.6 us (18%)
  between operations  1.43 us (2%)
  other arithmetic  1.34 us (2%)
  local copies, waits for them, and re-layouts  1.25 us (2%)
    pallas_call x1, Pallas kernels, on_device(): pl.pallas_call(functools.partial(main_kernel, len(blocks), tallies), out_...  22.2 us
    ppermute x15, starting transfers between devices, swap(): return lax.ppermute(value, axis, [(i, i ^ bit) for i in range(count)])  13.8 us
    ppermute x15, waiting for transfers between devices, swap(): return lax.ppermute(value, axis, [(i, i ^ bit) for i in range(count)])  12.6 us
    pallas_call x3, Pallas kernels, tally(): pl.pallas_call(functools.partial(tally_kernel, groups, leaves, index * he...  9.45 us
    ppermute x1, starting transfers between devices, hop(): lax.ppermute(value, axis, [(i, k) for i, k in moves if 0 <= k < count])  3.47 us
    pallas_call x1, Pallas kernels, on_device(): pl.pallas_call(prep_kernel, out_shape=jax.ShapeDtypeStruct((6, leaves, pa...  2.3 us
    pallas_call x1, Pallas kernels, on_device(): pl.pallas_call(final_kernel, out_shape=(jax.ShapeDtypeStruct((leaves, pan...  1.86 us
    pallas_call x1, Pallas kernels, on_device(): pl.pallas_call(functools.partial(plan_kernel, groups), out_shape=(jax.Sha...  1.66 us
  transfers between devices with their start and end apart: 16, of which 6 were waited for; matrix products, arithmetic and copies ran while one was open for 1% of the time, Pallas kernels for 16%

profile of v3, /device:TPU:0, one launch (start us, length us, event | category | flops | bytes accessed | tf_op | source)
XLA Modules:
  0.0 71.4 jit_solution(9646038918842121178)
XLA Ops:
  1.3 2.3 %prep.1.after.refs_2_ = f32[6,24,128]{2,1,0:T(8,128)} custom-call(s32[1]{0:T(128)S(6)} %copy.12.counts.refs_0_, f32[8,24,128]{2,1,0:T(8,128)} %basis.5, f32[3,24,128]{2,1,0:T(8,128)} %bitcast.9, f32[24,128]{1,0:T(8,128)} %areas.1, bf16[121,24,128]{2,1,0:T(8,128)(2,1)} %bitcast.7), custom_call_target="tpu_custom_call" | custom-call | tf_op jit(solution)/shard_map/prep/pallas_call | solution.py:310
  3.6 3.0 %collective-permute-start.1 = (f32[6,24,128]{2,1,0:T(8,128)}, f32[6,24,128]{2,1,0:T(8,128)S(1)}, u32[]{:S(2)}, u32[]{:S(2)}) collective-permute-start(f32[6,24,128]{2,1,0:T(8,128)} %prep.1.after.refs_2_), channel_id=1, source_target_pairs={{0,4},{4,0},{8,12},{12,8},{16,20},{20,16},{24,28},{28,24},{1,5},{5... | collective-permute-start | bytes 221192 | tf_op jit(solution)/shard_map/ppermute | solution.py:289
  6.6 0.6 pad_add_fusion.place
  7.2 3.2 %tally.3.refs_14_ = bf16[8,320,384]{2,1,0:T(8,128)(2,1)} custom-call(f32[6,24,128]{2,1,0:T(8,128)} %prep.1.after.refs_2_, s32[2]{0:T(128)} %pad_add_fusion.place, s32[24,189]{1,0:T(8,128)} %far.5, s32[24,189]{1,0:T(8,128)} %offset.5), custom_call_target="tpu_custom_call" | custom-call | tf_op jit(solution)/shard_map/tally/pallas_call | solution.py:327
  10.4 3.5 %collective-permute-start.3 = (f32[6,24,128]{2,1,0:T(8,128)S(1)}, f32[6,24,128]{2,1,0:T(8,128)S(1)}, u32[]{:S(2)}, u32[]{:S(2)}) collective-permute-start(f32[6,24,128]{2,1,0:T(8,128)S(1)} %collective-permute-done.1.after.refs_4_), channel_id=1, source_target_pairs={{0,8},{8,16},{12,4},{16,24},{20,12},{28,20},{1,9},{9,17},{13,5},{1... | collective-permute-start | bytes 221192 | tf_op jit(solution)/shard_map/ppermute | solution.py:295
  13.8 0.1 collective-permute-start.5
  13.9 1.6 %collective-permute-start = (f32[6,24,128]{2,1,0:T(8,128)S(1)}, f32[6,24,128]{2,1,0:T(8,128)S(1)}, u32[]{:S(2)}, u32[]{:S(2)}) collective-permute-start(f32[6,24,128]{2,1,0:T(8,128)S(1)} %copy-done), channel_id=1, source_target_pairs={{0,2},{1,3},{2,0},{3,1},{4,6},{5,7},{6,4},{7,5},{8,10},{9,11},{10,... | collective-permute-start | bytes 221192 | tf_op jit(solution)/shard_map/ppermute | solution.py:289
  15.5 0.5 collective-permute-start.2
  16.0 3.1 %tally.4.refs_15_ = bf16[8,320,384]{2,1,0:T(8,128)(2,1)} custom-call(f32[6,24,128]{2,1,0:T(8,128)} %copy-done.1, s32[2]{0:T(128)} %pad_add_fusion.place, s32[24,189]{1,0:T(8,128)} %far.5, s32[24,189]{1,0:T(8,128)} %offset.5), custom_call_target="tpu_custom_call" | custom-call | tf_op jit(solution)/shard_map/tally/pallas_call | solution.py:327
  19.2 1.5 %collective-permute-start.4 = (f32[6,24,128]{2,1,0:T(8,128)S(1)}, f32[6,24,128]{2,1,0:T(8,128)S(1)}, u32[]{:S(2)}, u32[]{:S(2)}) collective-permute-start(f32[6,24,128]{2,1,0:T(8,128)S(1)} %collective-permute-done.3.after.refs_6_), channel_id=1, source_target_pairs={{0,2},{1,3},{2,0},{3,1},{4,6},{5,7},{6,4},{7,5},{8,10},{9,11},{10,... | collective-permute-start | bytes 221192 | tf_op jit(solution)/shard_map/ppermute | solution.py:289
  20.7 0.5 collective-permute-start.6
  21.2 0.1 collective-permute-start.9
  21.3 0.4 collective-permute-start.8
  21.7 1.8 %collective-permute-done.4.refs_7_ = f32[6,24,128]{2,1,0:T(8,128)S(1)} collective-permute-done((f32[6,24,128]{2,1,0:T(8,128)S(1)}, f32[6,24,128]{2,1,0:T(8,128)S(1)}, u32[]{:S(2)}, u32[]{:S(2)}) %collective-permute-start.4) | collective-permute-done | bytes 73760 | tf_op jit(solution)/shard_map/ppermute | solution.py:289
  23.5 1.7 %plan.1 = (s32[24,27]{1,0:T(8,128)}, f32[8,128]{1,0:T(8,128)}) custom-call(s32[1]{0:T(128)S(6)} %copy.12.counts.refs_0_, s32[2]{0:T(128)} %pad_add_fusion.place, f32[8,24,128]{2,1,0:T(8,128)} %basis.5, s32[24,27]{1,0:T(8,128)} %near.1), custom_call_target="tpu_custom_call" | custom-call | tf_op jit(solution)/shard_map/plan/pallas_call | solution.py:354
  25.2 3.2 %tally.5.refs_16_ = bf16[8,320,384]{2,1,0:T(8,128)(2,1)} custom-call(f32[6,24,128]{2,1,0:T(8,128)} %copy-done.2, s32[2]{0:T(128)} %pad_add_fusion.place, s32[24,189]{1,0:T(8,128)} %far.5, s32[24,189]{1,0:T(8,128)} %offset.5), custom_call_target="tpu_custom_call" | custom-call | tf_op jit(solution)/shard_map/tally/pallas_call | solution.py:327
  28.5 0.5 copy-done.8
  29.0 0.0 copy-done.10
  29.0 0.1 copy-done.9
  29.1 22.2 %main.1 = (f32[24,128]{1,0:T(8,128)}, f32[8,128]{1,0:T(8,128)}) custom-call(s32[1]{0:T(128)S(6)} %copy.12.counts.refs_0_, s32[24,27]{1,0:T(8,128)} %get-tuple-element.10.refs_1_, f32[6,24,128]{2,1,0:T(8,128)} %prep.1.after.refs_2_, f32[6,24,128]{2,1,0:T(8,128)} %copy-done.4, f32[6,24,128]{2,1,0:T(8,128)} %copy-done.1, f32[6,24,128]{2,1,0:T(8,128)} %copy-done.5, ...), custom_call_target="tpu_custom_call" | custom-call | tf_op jit(solution)/shard_map/main/pallas_call | solution.py:368
  51.4 0.5 collective-permute-start.11
  51.9 1.0 %collective-permute-done.11 = f32[8,128]{1,0:T(8,128)S(1)} collective-permute-done((f32[8,128]{1,0:T(8,128)}, f32[8,128]{1,0:T(8,128)S(1)}, u32[]{:S(2)}, u32[]{:S(2)}) %collective-permute-start.11) | collective-permute-done | bytes 4128 | tf_op jit(solution)/shard_map/ppermute | solution.py:289
  52.9 0.7 add.22
  53.6 1.5 %collective-permute-start.12 = (f32[8,128]{1,0:T(8,128)S(1)}, f32[8,128]{1,0:T(8,128)S(1)}, u32[]{:S(2)}, u32[]{:S(2)}) collective-permute-start(f32[8,128]{1,0:T(8,128)S(1)} %add.22), channel_id=1, source_target_pairs={{0,2},{1,3},{2,0},{3,1},{4,6},{5,7},{6,4},{7,5},{8,10},{9,11},{10,... | collective-permute-start | bytes 12296 | tf_op jit(solution)/shard_map/ppermute | solution.py:289
  55.1 2.1 %collective-permute-done.12 = f32[8,128]{1,0:T(8,128)S(1)} collective-permute-done((f32[8,128]{1,0:T(8,128)S(1)}, f32[8,128]{1,0:T(8,128)S(1)}, u32[]{:S(2)}, u32[]{:S(2)}) %collective-permute-start.12) | collective-permute-done | bytes 4128 | tf_op jit(solution)/shard_map/ppermute | solution.py:289
  57.2 3.6 %collective-permute-done.13 = f32[8,128]{1,0:T(8,128)S(1)} collective-permute-done((f32[8,128]{1,0:T(8,128)S(1)}, f32[8,128]{1,0:T(8,128)S(1)}, u32[]{:S(2)}, u32[]{:S(2)}) %collective-permute-start.13) | collective-permute-done | bytes 4128 | tf_op jit(solution)/shard_map/ppermute | solution.py:289
  60.8 1.6 %collective-permute-start.14 = (f32[8,128]{1,0:T(8,128)S(1)}, f32[8,128]{1,0:T(8,128)S(1)}, u32[]{:S(2)}, u32[]{:S(2)}) collective-permute-start(f32[8,128]{1,0:T(8,128)S(1)} %add.24), channel_id=1, source_target_pairs={{0,8},{4,12},{8,0},{12,4},{16,24},{20,28},{24,16},{28,20},{1,9},{5... | collective-permute-start | bytes 12296 | tf_op jit(solution)/shard_map/ppermute | solution.py:289
  62.4 2.1 %collective-permute-done.14 = f32[8,128]{1,0:T(8,128)S(1)} collective-permute-done((f32[8,128]{1,0:T(8,128)S(1)}, f32[8,128]{1,0:T(8,128)S(1)}, u32[]{:S(2)}, u32[]{:S(2)}) %collective-permute-start.14) | collective-permute-done | bytes 4128 | tf_op jit(solution)/shard_map/ppermute | solution.py:289
  64.5 2.6 %collective-permute-start.15 = (f32[8,128]{1,0:T(8,128)S(1)}, f32[8,128]{1,0:T(8,128)S(1)}, u32[]{:S(2)}, u32[]{:S(2)}) collective-permute-start(f32[8,128]{1,0:T(8,128)S(1)} %add.25.tile), channel_id=1, source_target_pairs={{0,16},{4,20},{8,24},{12,28},{16,0},{20,4},{24,8},{28,12},{1,17},{... | collective-permute-start | bytes 12296 | tf_op jit(solution)/shard_map/ppermute | solution.py:289
  67.0 1.9 %collective-permute-done.15.other = f32[8,128]{1,0:T(8,128)S(1)} collective-permute-done((f32[8,128]{1,0:T(8,128)S(1)}, f32[8,128]{1,0:T(8,128)S(1)}, u32[]{:S(2)}, u32[]{:S(2)}) %collective-permute-start.15) | collective-permute-done | bytes 4128 | tf_op jit(solution)/shard_map/ppermute | solution.py:289
  69.0 0.6 copy-done.13
  69.5 1.9 %final.1 = (f32[24,128]{1,0:T(8,128)}, f32[9]{0:T(128)}) custom-call(s32[1]{0:T(128)S(6)} %copy.12.counts.refs_0_, f32[8,24,128]{2,1,0:T(8,128)} %basis.5, f32[24,128]{1,0:T(8,128)} %get-tuple-element.16.image, f32[8,128]{1,0:T(8,128)} %copy-done.12, f32[8,128]{1,0:T(8,128)} %copy-done.13), custom_call_target="tpu_custom_call" | custom-call | tf_op jit(solution)/shard_map/final/pallas_call | solution.py:406
  (40 shorter events, 0.1 us)
Async XLA Ops:
  3.6 10.3 %copy-start = (f32[6,24,128]{2,1,0:T(8,128)S(1)}, f32[6,24,128]{2,1,0:T(8,128)}, u32[]{:S(2)}) copy-start(f32[6,24,128]{2,1,0:T(8,128)} %prep.1.after.refs_2_) | copy-start | bytes 221188
  3.6 6.8 %collective-permute-start.1 = (f32[6,24,128]{2,1,0:T(8,128)}, f32[6,24,128]{2,1,0:T(8,128)S(1)}, u32[]{:S(2)}, u32[]{:S(2)}) collective-permute-start(f32[6,24,128]{2,1,0:T(8,128)} %prep.1.after.refs_2_), channel_id=1, source_target_pairs={{0,4},{4,0},{8,12},{12,8},{16,20},{20,16},{24,28},{28,24},{1,5},{5... | collective-permute-start | bytes 221192 | tf_op jit(solution)/shard_map/ppermute | solution.py:289
  10.4 5.7 %copy-start.1 = (f32[6,24,128]{2,1,0:T(8,128)}, f32[6,24,128]{2,1,0:T(8,128)S(1)}, u32[]{:S(2)}) copy-start(f32[6,24,128]{2,1,0:T(8,128)S(1)} %collective-permute-done.1.after.refs_4_) | copy-start | bytes 221188
  10.4 8.8 %collective-permute-start.3 = (f32[6,24,128]{2,1,0:T(8,128)S(1)}, f32[6,24,128]{2,1,0:T(8,128)S(1)}, u32[]{:S(2)}, u32[]{:S(2)}) collective-permute-start(f32[6,24,128]{2,1,0:T(8,128)S(1)} %collective-permute-done.1.after.refs_4_), channel_id=1, source_target_pairs={{0,8},{8,16},{12,4},{16,24},{20,12},{28,20},{1,9},{9,17},{13,5},{1... | collective-permute-start | bytes 221192 | tf_op jit(solution)/shard_map/ppermute | solution.py:295
  13.8 7.3 %collective-permute-start.5 = (f32[6,24,128]{2,1,0:T(8,128)S(1)}, f32[6,24,128]{2,1,0:T(8,128)S(1)}, u32[]{:S(2)}, u32[]{:S(2)}) collective-permute-start(f32[6,24,128]{2,1,0:T(8,128)S(1)} %copy-done), channel_id=1, source_target_pairs={{0,1},{1,0},{2,3},{3,2},{4,5},{5,4},{6,7},{7,6},{8,9},{9,8},{10,11... | collective-permute-start | bytes 221192 | tf_op jit(solution)/shard_map/ppermute | solution.py:289
  13.9 6.7 %collective-permute-start = (f32[6,24,128]{2,1,0:T(8,128)S(1)}, f32[6,24,128]{2,1,0:T(8,128)S(1)}, u32[]{:S(2)}, u32[]{:S(2)}) collective-permute-start(f32[6,24,128]{2,1,0:T(8,128)S(1)} %copy-done), channel_id=1, source_target_pairs={{0,2},{1,3},{2,0},{3,1},{4,6},{5,7},{6,4},{7,5},{8,10},{9,11},{10,... | collective-permute-start | bytes 221192 | tf_op jit(solution)/shard_map/ppermute | solution.py:289
  15.5 5.8 %collective-permute-start.2 = (f32[6,24,128]{2,1,0:T(8,128)S(1)}, f32[6,24,128]{2,1,0:T(8,128)S(1)}, u32[]{:S(2)}, u32[]{:S(2)}) collective-permute-start(f32[6,24,128]{2,1,0:T(8,128)S(1)} %collective-permute-done.1.after.refs_4_), channel_id=1, source_target_pairs={{0,2},{1,3},{2,0},{3,1},{4,6},{5,7},{6,4},{7,5},{8,10},{9,11},{10,... | collective-permute-start | bytes 221192 | tf_op jit(solution)/shard_map/ppermute | solution.py:289
  19.2 6.0 %copy-start.2 = (f32[6,24,128]{2,1,0:T(8,128)}, f32[6,24,128]{2,1,0:T(8,128)S(1)}, u32[]{:S(2)}) copy-start(f32[6,24,128]{2,1,0:T(8,128)S(1)} %collective-permute-done.3.after.refs_6_) | copy-start | bytes 221188
  19.2 4.4 %collective-permute-start.4 = (f32[6,24,128]{2,1,0:T(8,128)S(1)}, f32[6,24,128]{2,1,0:T(8,128)S(1)}, u32[]{:S(2)}, u32[]{:S(2)}) collective-permute-start(f32[6,24,128]{2,1,0:T(8,128)S(1)} %collective-permute-done.3.after.refs_6_), channel_id=1, source_target_pairs={{0,2},{1,3},{2,0},{3,1},{4,6},{5,7},{6,4},{7,5},{8,10},{9,11},{10,... | collective-permute-start | bytes 221192 | tf_op jit(solution)/shard_map/ppermute | solution.py:289
  20.7 7.7 %collective-permute-start.7 = (f32[6,24,128]{2,1,0:T(8,128)}, f32[6,24,128]{2,1,0:T(8,128)S(1)}, u32[]{:S(2)}, u32[]{:S(2)}) collective-permute-start(f32[6,24,128]{2,1,0:T(8,128)} %copy-done.1), channel_id=1, source_target_pairs={{0,1},{1,0},{2,3},{3,2},{4,5},{5,4},{6,7},{7,6},{8,9},{9,8},{10,11... | collective-permute-start | bytes 221192 | tf_op jit(solution)/shard_map/ppermute | solution.py:289
  20.7 7.8 %copy-start.4 = (f32[6,24,128]{2,1,0:T(8,128)}, f32[6,24,128]{2,1,0:T(8,128)S(1)}, u32[]{:S(2)}) copy-start(f32[6,24,128]{2,1,0:T(8,128)S(1)} %collective-permute-done.refs_3_) | copy-start | bytes 221188
  20.7 7.7 %collective-permute-start.6 = (f32[6,24,128]{2,1,0:T(8,128)S(1)}, f32[6,24,128]{2,1,0:T(8,128)S(1)}, u32[]{:S(2)}, u32[]{:S(2)}) collective-permute-start(f32[6,24,128]{2,1,0:T(8,128)S(1)} %collective-permute-done.refs_3_), channel_id=1, source_target_pairs={{0,1},{1,0},{2,3},{3,2},{4,5},{5,4},{6,7},{7,6},{8,9},{9,8},{10,11... | collective-permute-start | bytes 221192 | tf_op jit(solution)/shard_map/ppermute | solution.py:289
  21.2 7.3 %copy-start.3 = (f32[6,24,128]{2,1,0:T(8,128)}, f32[6,24,128]{2,1,0:T(8,128)S(1)}, u32[]{:S(2)}) copy-start(f32[6,24,128]{2,1,0:T(8,128)S(1)} %collective-permute-done.5.refs_8_) | copy-start | bytes 221188
  21.2 7.2 %collective-permute-start.9 = (f32[6,24,128]{2,1,0:T(8,128)S(1)}, f32[6,24,128]{2,1,0:T(8,128)S(1)}, u32[]{:S(2)}, u32[]{:S(2)}) collective-permute-start(f32[6,24,128]{2,1,0:T(8,128)S(1)} %collective-permute-done.3.after.refs_6_), channel_id=1, source_target_pairs={{0,1},{1,0},{2,3},{3,2},{4,5},{5,4},{6,7},{7,6},{8,9},{9,8},{10,11... | collective-permute-start | bytes 221192 | tf_op jit(solution)/shard_map/ppermute | solution.py:289
  21.3 7.2 %copy-start.5 = (f32[6,24,128]{2,1,0:T(8,128)}, f32[6,24,128]{2,1,0:T(8,128)S(1)}, u32[]{:S(2)}) copy-start(f32[6,24,128]{2,1,0:T(8,128)S(1)} %collective-permute-done.2.refs_5_) | copy-start | bytes 221188
  21.3 7.1 %collective-permute-start.8 = (f32[6,24,128]{2,1,0:T(8,128)S(1)}, f32[6,24,128]{2,1,0:T(8,128)S(1)}, u32[]{:S(2)}, u32[]{:S(2)}) collective-permute-start(f32[6,24,128]{2,1,0:T(8,128)S(1)} %collective-permute-done.2.refs_5_), channel_id=1, source_target_pairs={{0,1},{1,0},{2,3},{3,2},{4,5},{5,4},{6,7},{7,6},{8,9},{9,8},{10,11... | collective-permute-start | bytes 221192 | tf_op jit(solution)/shard_map/ppermute | solution.py:289
  23.5 4.9 %copy-start.6 = (f32[6,24,128]{2,1,0:T(8,128)}, f32[6,24,128]{2,1,0:T(8,128)S(1)}, u32[]{:S(2)}) copy-start(f32[6,24,128]{2,1,0:T(8,128)S(1)} %collective-permute-done.4.refs_7_) | copy-start | bytes 221188
  23.5 4.9 %collective-permute-start.10 = (f32[6,24,128]{2,1,0:T(8,128)S(1)}, f32[6,24,128]{2,1,0:T(8,128)S(1)}, u32[]{:S(2)}, u32[]{:S(2)}) collective-permute-start(f32[6,24,128]{2,1,0:T(8,128)S(1)} %collective-permute-done.4.refs_7_), channel_id=1, source_target_pairs={{0,1},{1,0},{2,3},{3,2},{4,5},{5,4},{6,7},{7,6},{8,9},{9,8},{10,11... | collective-permute-start | bytes 221192 | tf_op jit(solution)/shard_map/ppermute | solution.py:289
  28.3 0.6 copy-start.8
  28.4 0.6 copy-start.7
  28.4 0.7 copy-start.10
  28.4 0.7 copy-start.9
  28.4 0.7 copy-start.11
  51.4 1.6 %collective-permute-start.11 = (f32[8,128]{1,0:T(8,128)}, f32[8,128]{1,0:T(8,128)S(1)}, u32[]{:S(2)}, u32[]{:S(2)}) collective-permute-start(f32[8,128]{1,0:T(8,128)} %get-tuple-element.17), channel_id=1, source_target_pairs={{0,1},{1,0},{2,3},{3,2},{4,5},{5,4},{6,7},{7,6},{8,9},{9,8},{10,11... | collective-permute-start | bytes 12296 | tf_op jit(solution)/shard_map/ppermute | solution.py:289
  53.6 3.6 %collective-permute-start.12 = (f32[8,128]{1,0:T(8,128)S(1)}, f32[8,128]{1,0:T(8,128)S(1)}, u32[]{:S(2)}, u32[]{:S(2)}) collective-permute-start(f32[8,128]{1,0:T(8,128)S(1)} %add.22), channel_id=1, source_target_pairs={{0,2},{1,3},{2,0},{3,1},{4,6},{5,7},{6,4},{7,5},{8,10},{9,11},{10,... | collective-permute-start | bytes 12296 | tf_op jit(solution)/shard_map/ppermute | solution.py:289
  57.2 3.6 %collective-permute-start.13 = (f32[8,128]{1,0:T(8,128)S(1)}, f32[8,128]{1,0:T(8,128)S(1)}, u32[]{:S(2)}, u32[]{:S(2)}) collective-permute-start(f32[8,128]{1,0:T(8,128)S(1)} %add.23), channel_id=1, source_target_pairs={{0,4},{4,0},{8,12},{12,8},{16,20},{20,16},{24,28},{28,24},{1,5},{5... | collective-permute-start | bytes 12296 | tf_op jit(solution)/shard_map/ppermute | solution.py:289
  60.8 3.6 %collective-permute-start.14 = (f32[8,128]{1,0:T(8,128)S(1)}, f32[8,128]{1,0:T(8,128)S(1)}, u32[]{:S(2)}, u32[]{:S(2)}) collective-permute-start(f32[8,128]{1,0:T(8,128)S(1)} %add.24), channel_id=1, source_target_pairs={{0,8},{4,12},{8,0},{12,4},{16,24},{20,28},{24,16},{28,20},{1,9},{5... | collective-permute-start | bytes 12296 | tf_op jit(solution)/shard_map/ppermute | solution.py:289
  64.5 4.5 %copy-start.12 = (f32[8,128]{1,0:T(8,128)}, f32[8,128]{1,0:T(8,128)S(1)}, u32[]{:S(2)}) copy-start(f32[8,128]{1,0:T(8,128)S(1)} %add.25.tile) | copy-start | bytes 12292
  64.5 4.5 %collective-permute-start.15 = (f32[8,128]{1,0:T(8,128)S(1)}, f32[8,128]{1,0:T(8,128)S(1)}, u32[]{:S(2)}, u32[]{:S(2)}) collective-permute-start(f32[8,128]{1,0:T(8,128)S(1)} %add.25.tile), channel_id=1, source_target_pairs={{0,16},{4,20},{8,24},{12,28},{16,0},{20,4},{24,8},{28,12},{1,17},{... | collective-permute-start | bytes 12296 | tf_op jit(solution)/shard_map/ppermute | solution.py:289
  69.0 0.6 copy-start.13

commit v4 on v3

--- a/solution.py
+++ b/solution.py
@@ -13,6 +13,7 @@
 f32 = jnp.float32
 WIDTH = 16
 CENTRE = 2.0
+UNROLL = 4
 LIMIT = 56 * 1024 * 1024
 
 across = (((1,), (1,)), ((), ()))
@@ -47,8 +48,8 @@
     block[5] = poles
 
 
-def slot_of(window, groups, leaves, me, order_low):
-    half = groups // 2
+def slot_of(window, table, leaves, me, order_low):
+    groups = len(table[0])
     span = groups * leaves
     low = (window < span).astype(jnp.int32)
     high = (window >= 2 * span).astype(jnp.int32)
@@ -57,39 +58,18 @@
     group = jnp.zeros_like(window)
     for g in range(1, groups):
         group += (inner >= g * leaves).astype(jnp.int32)
-    relative = group ^ me
-    column = (relative & 1) * (3 * half) + order * half + lax.shift_right_logical(relative, 1)
+    key = order * groups + (group ^ me)
+    column = jnp.zeros_like(window)
+    for i, line in enumerate(table):
+        for j, at in enumerate(line):
+            column = jnp.where(key == i * groups + j, at, column)
     return column * leaves + inner - group * leaves
 
 
-def tally_kernel(groups, leaves, first, after, place, far, offset, hits, slots, classes):
-    held, padded, wide = hits.shape
-    count = far.shape[1]
-    entries = slots.shape[1]
-    rows = pl.ds(first, held)
-    slots[...] = jnp.full(slots.shape, -1, jnp.int32)
-    slots[:, 0:count] = slot_of(far[rows, :], groups, leaves, place[0], place[1])
-    classes[...] = jnp.full(classes.shape, -1, jnp.int32)
-    classes[:, 0:count] = offset[rows, :]
-
-    def body(leaf):
-        slot = slots[pl.ds(leaf, 1), :]
-        of_class = classes[pl.ds(leaf, 1), :]
-        by_slot = lax.broadcasted_iota(jnp.int32, (wide, entries), 0) == slot
-        by_class = lax.broadcasted_iota(jnp.int32, (padded, entries), 0) == of_class
-        hits[leaf] = lax.dot_general(
-            by_class.astype(f32).astype(bf16),
-            by_slot.astype(f32).astype(bf16),
-            across,
-            preferred_element_type=f32,
-        ).astype(bf16)
-
-    repeat(held, 4, body)
-
-
-def plan_kernel(groups, counts, place, basis, near, near_slots, gram):
+def plan_kernel(table, counts, place, basis, near, far, near_slots, far_slots, gram):
     krylov, leaves, panels = basis.shape
-    near_slots[...] = slot_of(near[...], groups, leaves, place[0], place[1])
+    near_slots[...] = slot_of(near[...], table, leaves, place[0], place[1])
+    far_slots[...] = slot_of(far[...], table, leaves, place[0], place[1])
     live = live_rows(counts, (leaves, panels))
     masked = [basis[j] * live for j in range(krylov)]
     lane = lax.broadcasted_iota(jnp.int32, (krylov, panels), 1)
@@ -111,34 +91,28 @@
 pairs = ((0, 0), (0, 1), (1, 0))
 
 
-def main_kernel(pieces, tallies, *refs):
-    counts, near = refs[0:2]
-    blocks = refs[2 : 2 + pieces]
-    hits_hbm = refs[2 + pieces : 2 + pieces + tallies]
-    m2l_hbm, l2p, basis, gram, image_out, tile_out = refs[2 + pieces + tallies : 8 + pieces + tallies]
-    hits, m2l, source32, source16, target32, target16 = refs[8 + pieces + tallies : 14 + pieces + tallies]
-    charge, poles32, sums, totals, found, sems = refs[14 + pieces + tallies :]
+def main_kernel(orders, *refs):
+    pieces = len(orders)
+    counts, place, near, far = refs[0:4]
+    blocks = refs[4 : 4 + pieces]
+    classes, m2l_hbm, l2p, basis, gram, image_out, tile_out = refs[4 + pieces : 11 + pieces]
+    m2l, source32, source16, target32, target16 = refs[11 + pieces : 16 + pieces]
+    charge, poles32, taken, sums, totals, found, sem = refs[16 + pieces :]
     krylov, leaves, panels = basis.shape
     terms = l2p.shape[0]
     offsets = m2l.shape[1]
-    held = leaves // tallies
-    copies = [
-        pltpu.make_async_copy(hits_hbm[i], hits.at[pl.ds(i * held, held)], sems.at[i])
-        for i in range(tallies)
-    ]
-    copies.append(pltpu.make_async_copy(m2l_hbm, m2l, sems.at[tallies]))
-    for copy in copies:
-        copy.start()
+    copy = pltpu.make_async_copy(m2l_hbm, m2l, sem)
+    copy.start()
+    inside = place[2].astype(f32)
 
     ones = jnp.ones((leaves, panels), f32)
     zeros = jnp.zeros((leaves, panels), f32)
 
-    def place(ref, base, rows):
+    def lay(ref, base, rows):
         for k in range(WIDTH):
             value = rows[k] if k < len(rows) else zeros
             ref[pl.ds(base * WIDTH + k, leaves, stride=WIDTH), :] = value
 
-    poles32[...] = jnp.zeros_like(poles32)
     for b in range(pieces):
         got = blocks[b]
         point = [got[c] - CENTRE for c in range(3)]
@@ -147,22 +121,26 @@
         split = [thirds(p)[0:2] for p in point]
         square = point[0] * point[0] + point[1] * point[1] + point[2] * point[2]
         rows = [split[c][q] for c in range(3) for (_, q) in pairs]
-        place(source32, b * leaves, rows + list(thirds(square + area)) + [ones] * 3)
+        lay(source32, b * leaves, rows + list(thirds(square + area)) + [ones] * 3)
         if b == 0:
             rows = [split[c][p] * (-2.0) for c in range(3) for (p, _) in pairs]
-            place(target32, 0, rows + [ones] * 3 + list(thirds(square)))
-        charge[pl.ds(b * leaves, leaves), :] = got[4]
-        poles32[pl.ds(b * leaves, leaves), :] = got[5]
+            lay(target32, 0, rows + [ones] * 3 + list(thirds(square)))
+        known = inside if orders[b] == 2 else 1.0
+        charge[pl.ds(b * leaves, leaves), :] = got[4] * known
+        poles32[pl.ds(b * leaves, leaves), :] = got[5] * known
     source16[...] = source32[...].astype(bf16)
     for leaf in range(leaves):
         target16[leaf] = target32[leaf * WIDTH : (leaf + 1) * WIDTH, :].T.astype(bf16)
-    pole = poles32[...]
-    high = pole.astype(bf16)
-    poles16 = jnp.concatenate([high, (pole - high.astype(f32)).astype(bf16)], axis=1)
-
     neighbours = near.shape[1]
 
-    def near_body(leaf):
+    entries = far.shape[1]
+    padded = found.shape[1]
+    depth = taken.shape[1]
+    taken[:, entries:, :] = jnp.zeros((taken.shape[0], depth - entries, panels), f32)
+
+    def leaf_body(leaf, i):
+        for e in range(entries):
+            taken[i, e : e + 1, :] = poles32[pl.ds(far[leaf, e], 1), :]
         total = jnp.zeros((panels, panels), f32)
         for start in range(0, neighbours, 2):
             ids = [near[leaf, e] for e in range(start, min(start + 2, neighbours))]
@@ -172,19 +150,22 @@
             for e, s in enumerate(ids):
                 total += inverse[:, e * panels : (e + 1) * panels] * charge[pl.ds(s, 1), :]
         totals[leaf] = total
-
-    def leaf_body(leaf):
-        near_body(leaf)
-        both = jnp.dot(hits[leaf], poles16, preferred_element_type=f32)
+        pole = taken[i]
+        high = pole.astype(bf16)
+        pole = jnp.concatenate([high, (pole - high.astype(f32)).astype(bf16)], axis=1)
+        offset = classes[pl.ds(leaf, 1), :]
+        by_class = lax.broadcasted_iota(jnp.int32, (padded, entries), 0) == offset
+        by_class = jnp.concatenate(
+            [by_class.astype(f32), jnp.zeros((padded, depth - entries), f32)], axis=1
+        ).astype(bf16)
+        both = jnp.dot(by_class, pole, preferred_element_type=f32)
         found[leaf] = both[:, 0:panels] + both[:, panels : 2 * panels]
 
-    for copy in copies[:tallies]:
-        copy.wait()
-    repeat(leaves, 4, leaf_body)
+    repeat(leaves, UNROLL, leaf_body)
     nearby = jnp.concatenate(
         [jnp.sum(totals[leaf].T, axis=0, keepdims=True) for leaf in range(leaves)], axis=0
     )
-    copies[tallies].wait()
+    copy.wait()
 
     group = 8
     filler = jnp.zeros((terms * group, panels - terms), bf16)
@@ -252,7 +233,7 @@
 
     def several(step, carry):
         for i in range(batch):
-            body(step * batch + i)
+            body(step * batch + i, i)
         return carry
 
     lax.fori_loop(0, count // batch, several, 0)
@@ -284,15 +265,28 @@
     column[...] = placed.reshape(panels)[0 : krylov + 1]
 
 
-def swap(value, axis, bit):
-    count = lax.axis_size(axis)
-    return lax.ppermute(value, axis, [(i, i ^ bit) for i in range(count)])
-
-
-def hop(value, axis):
-    count = lax.axis_size(axis)
-    moves = [(i, i + 2 if i % 2 == 0 else i - 2) for i in range(count)]
-    return lax.ppermute(value, axis, [(i, k) for i, k in moves if 0 <= k < count])
+def move(value, step):
+    segments, groups = lax.axis_size("seg"), lax.axis_size("grp")
+    moves = []
+    for segment in range(segments):
+        for group in range(groups):
+            to = step(segment, group)
+            moves.append((segment * groups + group, to[0] * groups + to[1]))
+    return lax.ppermute(value, ("seg", "grp"), moves)
+
+
+def swap(value, segment_bit, group_bit):
+    return move(value, lambda s, g: (s ^ segment_bit, g ^ group_bit))
+
+
+def hop(value):
+    segments = lax.axis_size("seg")
+
+    def step(s, g):
+        to = s + 2 if s % 2 == 0 else s - 2
+        return (to if 0 <= to < segments else s ^ 1, g ^ 1)
+
+    return move(value, step)
 
 
 def on_device(basis, coords, areas, p2m, l2p, m2l, counts, near_list, far_list, far_offset):
@@ -304,8 +298,11 @@
     terms, offsets = m2l.shape[:2]
     groups = lax.axis_size("grp")
     params = pltpu.CompilerParams(vmem_limit_bytes=LIMIT)
-    even = 1 - lax.axis_index("seg") % 2
-    position = jnp.stack([lax.axis_index("grp"), 1 + even]).astype(jnp.int32)
+    here = lax.axis_index("seg")
+    odd = here % 2
+    order_low = 2 - odd
+    inside = jnp.where(odd == 0, here >= 2, here < lax.axis_size("seg") - 2)
+    position = jnp.stack([lax.axis_index("grp"), order_low, inside]).astype(jnp.int32)
 
     block = pl.pallas_call(
         prep_kernel,
@@ -317,90 +314,78 @@
     )(counts, basis, coords, areas, p2m)
 
     window = 3 * groups * leaves
-    wide = window + -window % 128
-    entries = far_list.shape[1] + -far_list.shape[1] % 128
+    entries = far_list.shape[1]
     padded = offsets + -offsets % 16
-    tallies = 3 if leaves % 3 == 0 else 1
-    held = leaves // tallies
-
-    def tally(index, after):
-        return pl.pallas_call(
-            functools.partial(tally_kernel, groups, leaves, index * held),
-            out_shape=jax.ShapeDtypeStruct((held, padded, wide), bf16),
-            in_specs=[pl.BlockSpec(memory_space=pl.ANY)] + smem(1) + vmem(2),
-            out_specs=pl.BlockSpec(memory_space=pltpu.VMEM),
-            scratch_shapes=[pltpu.VMEM((held, entries), jnp.int32)] * 2,
-            compiler_params=params,
-            name="tally",
-        )(after, position, far_list, far_offset)
-
-    def spread(value):
-        whole = [value]
+
+    def spread(pieces):
         bit = 2
         while bit < groups:
-            whole = whole + [swap(v, "grp", bit) for v in whole]
+            mask = bit | 1
+            pieces = pieces + [(swap(v, 0, mask), order, rel ^ mask) for v, order, rel in pieces]
             bit *= 2
-        return whole
-
-    beside = swap(block, "seg", 1)
-    own = spread(block)
-    hits = [tally(0, block)]
-    beside, hits[0] = lax.optimization_barrier((beside, hits[0]))
-    beyond = hop(beside, "seg")
-    if tallies > 1:
-        hits.append(tally(1, beside))
-        beyond, hits[1] = lax.optimization_barrier((beyond, hits[1]))
-        hits.append(tally(2, beyond))
-    near_slots, gram = pl.pallas_call(
-        functools.partial(plan_kernel, groups),
+        return pieces
+
+    beside = swap(block, 1, 1)
+    own = spread([(block, 0, 0)])
+    beyond = hop(beside)
+    pieces = own + [(beside, 1, 1)] + [(swap(v, 1, 1), 1, rel ^ 1) for v, _, rel in own[1:]]
+    pieces = pieces + spread([(beyond, 2, 0)])
+    pieces = pieces + [(swap(v, 0, 1), order, rel ^ 1) for v, order, rel in pieces]
+    table = [[0] * groups for _ in range(3)]
+    for at, (_, order, rel) in enumerate(pieces):
+        table[order][rel] = at
+    near_slots, far_slots, gram = pl.pallas_call(
+        functools.partial(plan_kernel, table),
         out_shape=(
             jax.ShapeDtypeStruct(near_list.shape, jnp.int32),
+            jax.ShapeDtypeStruct(far_list.shape, jnp.int32),
             jax.ShapeDtypeStruct((krylov, panels), f32),
         ),
-        in_specs=smem(2) + vmem(2),
-        out_specs=tuple(vmem(2)),
+        in_specs=smem(2) + vmem(3),
+        out_specs=tuple(vmem(3)),
         compiler_params=params,
         name="plan",
-    )(counts, position, basis, near_list)
-    here = own + spread(beside) + spread(beyond)
-    blocks = here + [swap(v, "grp", 1) for v in here]
+    )(counts, position, basis, near_list, far_list)
 
     image, tile = pl.pallas_call(
-        functools.partial(main_kernel, len(blocks), tallies),
+        functools.partial(main_kernel, [order for _, order, _ in pieces]),
         out_shape=(
             jax.ShapeDtypeStruct((leaves, panels), f32),
             jax.ShapeDtypeStruct((krylov, panels), f32),
         ),
-        in_specs=smem(2)
-        + vmem(len(blocks))
-        + [pl.BlockSpec(memory_space=pl.ANY)] * (tallies + 1)
+        in_specs=smem(4)
+        + vmem(len(pieces) + 1)
+        + [pl.BlockSpec(memory_space=pl.ANY)]
         + vmem(3),
         out_specs=tuple(vmem(2)),
         scratch_shapes=[
-            pltpu.VMEM((leaves, padded, wide), bf16),
             pltpu.VMEM(m2l.shape, bf16),
             pltpu.VMEM((window * WIDTH, panels), f32),
             pltpu.VMEM((window * WIDTH, panels), bf16),
             pltpu.VMEM((leaves * WIDTH, panels), f32),
             pltpu.VMEM((leaves, panels, WIDTH), bf16),
             pltpu.VMEM((window, panels), f32),
-            pltpu.VMEM((wide, panels), f32),
+            pltpu.VMEM((window, panels), f32),
+            pltpu.VMEM((UNROLL, entries + -entries % 64, panels), f32),
             pltpu.VMEM((terms * 8, leaves * 8), f32),
             pltpu.VMEM((leaves, panels, panels), f32),
             pltpu.VMEM((leaves, padded, panels), f32),
-            pltpu.SemaphoreType.DMA((tallies + 1,)),
+            pltpu.SemaphoreType.DMA,
         ],
         compiler_params=params,
         name="main",
-    )(counts, near_slots, *blocks, *hits, m2l, l2p, basis, gram)
-
-    stages = [
-        (axis, 1 << power)
-        for axis in ("grp", "seg")
-        for power in range((lax.axis_size(axis) - 1).bit_length())
-    ]
-    for axis, bit in stages[:-1]:
-        tile = tile + swap(tile, axis, bit)
+    )(
+        counts, position, near_slots, far_slots,
+        *[v for v, _, _ in pieces], far_offset, m2l, l2p, basis, gram,
+    )
+
+    def masks(axis):
+        return [1 << power for power in range((lax.axis_size(axis) - 1).bit_length())]
+
+    stages = [(0, bit if bit == 1 else bit | 1) for bit in masks("grp")]
+    stages += [(bit, 1) for bit in masks("seg")]
+    for stage in stages[:-1]:
+        tile = tile + swap(tile, *stage)
     other = swap(tile, *stages[-1])
 
     return pl.pallas_call(

time: 71.9 us -> 62.1 us (0.86)
  Pallas kernels: 37.5 us -> 28.5 us
  waiting for transfers between devices: 12.6 us -> 11 us
  starting transfers between devices: 17.2 us -> 18.3 us
    pallas_call x5 -> x2, Pallas kernels: 33.4 us -> 24.4 us  [the longest x1 22.7 us: on_device(): pl.pallas_call(functools.partial(main_kernel, [order for _, order, _ in p...]
    ppermute x16, waiting for transfers between devices: 12.6 us -> 11 us  [move(): return lax.ppermute(value, ('seg', 'grp'), moves)]
    ppermute x16, starting transfers between devices: 17.2 us -> 18.3 us  [move(): return lax.ppermute(value, ('seg', 'grp'), moves)]
  transfers between devices with their start and end apart: 16 -> 16, of which waited for: 6 -> 8; matrix products, arithmetic and copies ran while one was open for 1% -> 1% of each run, Pallas kernels for 16% -> 3%
where the time goes in v4:
time: 62.1 us; the launch traced here: 61.8 us
  Pallas kernels  28.5 us (46%)
  starting transfers between devices  18.3 us (29%)
  waiting for transfers between devices  11 us (18%)
  between operations  1.42 us (2%)
  other arithmetic  1.31 us (2%)
  local copies, waits for them, and re-layouts  1.25 us (2%)
    pallas_call x1, Pallas kernels, on_device(): pl.pallas_call(functools.partial(main_kernel, [order for _, order, _ in p...  22.7 us
    ppermute x16, starting transfers between devices, move(): return lax.ppermute(value, ('seg', 'grp'), moves)  18.3 us
    ppermute x16, waiting for transfers between devices, move(): return lax.ppermute(value, ('seg', 'grp'), moves)  11 us
    pallas_call x1, Pallas kernels, on_device(): pl.pallas_call(prep_kernel, out_shape=jax.ShapeDtypeStruct((6, leaves, pa...  2.3 us
    pallas_call x1, Pallas kernels, on_device(): pl.pallas_call(final_kernel, out_shape=(jax.ShapeDtypeStruct((leaves, pan...  1.86 us
    pallas_call x1, Pallas kernels, on_device(): pl.pallas_call(functools.partial(plan_kernel, table), out_shape=(jax.Shap...  1.66 us
    unnamed x26, local copies, waits for them, and re-layouts  1.25 us
  transfers between devices with their start and end apart: 16, of which 8 were waited for; matrix products, arithmetic and copies ran while one was open for 1% of the time, Pallas kernels for 3%

profile of v4, /device:TPU:0, one launch (start us, length us, event | category | flops | bytes accessed | tf_op | source)
XLA Modules:
  0.0 61.8 jit_solution(17748354361815427175)
XLA Ops:
  1.3 2.3 %prep.1.refs_4_ = f32[6,24,128]{2,1,0:T(8,128)} custom-call(s32[1]{0:T(128)S(6)} %copy.12.counts.refs_0_, f32[8,24,128]{2,1,0:T(8,128)} %basis.5, f32[3,24,128]{2,1,0:T(8,128)} %bitcast.10, f32[24,128]{1,0:T(8,128)} %areas.1, bf16[121,24,128]{2,1,0:T(8,128)(2,1)} %bitcast.8), custom_call_target="tpu_custom_call" | custom-call | tf_op jit(solution)/shard_map/prep/pallas_call | solution.py:307
  3.6 2.4 %collective-permute-start.1 = (f32[6,24,128]{2,1,0:T(8,128)}, f32[6,24,128]{2,1,0:T(8,128)S(1)}, u32[]{:S(2)}, u32[]{:S(2)}) collective-permute-start(f32[6,24,128]{2,1,0:T(8,128)} %prep.1.refs_4_), channel_id=1, source_target_pairs={{0,5},{1,4},{2,7},{3,6},{4,1},{5,0},{6,3},{7,2},{8,13},{9,12},{10,... | collective-permute-start | bytes 221192 | tf_op jit(solution)/shard_map/ppermute | solution.py:275
  6.0 1.8 %collective-permute-start = (f32[6,24,128]{2,1,0:T(8,128)}, f32[6,24,128]{2,1,0:T(8,128)S(1)}, u32[]{:S(2)}, u32[]{:S(2)}) collective-permute-start(f32[6,24,128]{2,1,0:T(8,128)} %prep.1.refs_4_), channel_id=1, source_target_pairs={{0,3},{1,2},{2,1},{3,0},{4,7},{5,6},{6,5},{7,4},{8,11},{9,10},{10,... | collective-permute-start | bytes 221192 | tf_op jit(solution)/shard_map/ppermute | solution.py:275
  7.8 1.2 %collective-permute-done.1.refs_6_ = f32[6,24,128]{2,1,0:T(8,128)S(1)} collective-permute-done((f32[6,24,128]{2,1,0:T(8,128)}, f32[6,24,128]{2,1,0:T(8,128)S(1)}, u32[]{:S(2)}, u32[]{:S(2)}) %collective-permute-start.1) | collective-permute-done | bytes 73760 | tf_op jit(solution)/shard_map/ppermute | solution.py:275
  9.0 2.2 %collective-permute-start.3 = (f32[6,24,128]{2,1,0:T(8,128)S(1)}, f32[6,24,128]{2,1,0:T(8,128)S(1)}, u32[]{:S(2)}, u32[]{:S(2)}) collective-permute-start(f32[6,24,128]{2,1,0:T(8,128)S(1)} %collective-permute-done.1.refs_6_), channel_id=1, source_target_pairs={{0,9},{1,8},{2,11},{3,10},{4,1},{5,0},{6,3},{7,2},{8,17},{9,16},{1... | collective-permute-start | bytes 221192 | tf_op jit(solution)/shard_map/ppermute | solution.py:275
  11.1 0.3 collective-permute-start.5
  11.4 2.0 %collective-permute-done.3.refs_8_ = f32[6,24,128]{2,1,0:T(8,128)S(1)} collective-permute-done((f32[6,24,128]{2,1,0:T(8,128)S(1)}, f32[6,24,128]{2,1,0:T(8,128)S(1)}, u32[]{:S(2)}, u32[]{:S(2)}) %collective-permute-start.3) | collective-permute-done | bytes 73760 | tf_op jit(solution)/shard_map/ppermute | solution.py:275
  13.4 1.8 %collective-permute-start.4 = (f32[6,24,128]{2,1,0:T(8,128)S(1)}, f32[6,24,128]{2,1,0:T(8,128)S(1)}, u32[]{:S(2)}, u32[]{:S(2)}) collective-permute-start(f32[6,24,128]{2,1,0:T(8,128)S(1)} %collective-permute-done.3.refs_8_), channel_id=1, source_target_pairs={{0,3},{1,2},{2,1},{3,0},{4,7},{5,6},{6,5},{7,4},{8,11},{9,10},{10,... | collective-permute-start | bytes 221192 | tf_op jit(solution)/shard_map/ppermute | solution.py:275
  15.2 0.4 collective-permute-start.7
  15.6 0.1 collective-permute-start.6
  15.8 0.4 collective-permute-start.9
  16.2 0.1 collective-permute-start.8
  16.3 1.3 %collective-permute-done.4.refs_9_ = f32[6,24,128]{2,1,0:T(8,128)S(1)} collective-permute-done((f32[6,24,128]{2,1,0:T(8,128)S(1)}, f32[6,24,128]{2,1,0:T(8,128)S(1)}, u32[]{:S(2)}, u32[]{:S(2)}) %collective-permute-start.4) | collective-permute-done | bytes 73760 | tf_op jit(solution)/shard_map/ppermute | solution.py:275
  17.6 0.3 collective-permute-start.10
  17.9 0.6 pad_add_fusion.place.refs_1_
  18.5 1.7 %plan.1 = (s32[24,27]{1,0:T(8,128)}, s32[24,189]{1,0:T(8,128)}, f32[8,128]{1,0:T(8,128)}) custom-call(s32[1]{0:T(128)S(6)} %copy.12.counts.refs_0_, s32[3]{0:T(128)} %pad_add_fusion.place.refs_1_, f32[8,24,128]{2,1,0:T(8,128)} %basis.5, s32[24,27]{1,0:T(8,128)} %near.1, s32[24,189]{1,0:T(8,128)} %far.1), custom_call_target="tpu_custom_call" | custom-call | tf_op jit(solution)/shard_map/plan/pallas_call | solution.py:337
  20.3 0.5 copy-done.6
  20.9 0.0 copy-done.10
  20.9 22.7 %main.1 = (f32[24,128]{1,0:T(8,128)}, f32[8,128]{1,0:T(8,128)}) custom-call(s32[1]{0:T(128)S(6)} %copy.12.counts.refs_0_, s32[3]{0:T(128)} %pad_add_fusion.place.refs_1_, s32[24,27]{1,0:T(8,128)} %get-tuple-element.7.refs_2_, s32[24,189]{1,0:T(8,128)} %get-tuple-element.8.refs_3_, f32[6,24,128]{2,1,0:T(8,128)} %prep.1.refs_4_, f32[6,24,128]{2,1,0:T(8,128)} %copy-done.1, ...), custom_call_target="tpu_custom_call" | custom-call | tf_op jit(solution)/shard_map/main/pallas_call | solution.py:350
  43.6 0.3 collective-permute-start.11
  43.9 1.2 %collective-permute-done.11 = f32[8,128]{1,0:T(8,128)S(1)} collective-permute-done((f32[8,128]{1,0:T(8,128)}, f32[8,128]{1,0:T(8,128)S(1)}, u32[]{:S(2)}, u32[]{:S(2)}) %collective-permute-start.11) | collective-permute-done | bytes 4128 | tf_op jit(solution)/shard_map/ppermute | solution.py:275
  45.1 0.7 %add.17 = f32[8,128]{1,0:T(8,128)S(1)} add(f32[8,128]{1,0:T(8,128)} %get-tuple-element.11, f32[8,128]{1,0:T(8,128)S(1)} %collective-permute-done.11) | non-fusion elementwise | flops 1024 | bytes 12288 | tf_op jit(solution)/shard_map/add | solution.py:388
  45.8 2.0 %collective-permute-start.12 = (f32[8,128]{1,0:T(8,128)S(1)}, f32[8,128]{1,0:T(8,128)S(1)}, u32[]{:S(2)}, u32[]{:S(2)}) collective-permute-start(f32[8,128]{1,0:T(8,128)S(1)} %add.17), channel_id=1, source_target_pairs={{0,3},{1,2},{2,1},{3,0},{4,7},{5,6},{6,5},{7,4},{8,11},{9,10},{10,... | collective-permute-start | bytes 12296 | tf_op jit(solution)/shard_map/ppermute | solution.py:275
  47.8 1.3 %collective-permute-done.12 = f32[8,128]{1,0:T(8,128)S(1)} collective-permute-done((f32[8,128]{1,0:T(8,128)S(1)}, f32[8,128]{1,0:T(8,128)S(1)}, u32[]{:S(2)}, u32[]{:S(2)}) %collective-permute-start.12) | collective-permute-done | bytes 4128 | tf_op jit(solution)/shard_map/ppermute | solution.py:275
  49.1 1.8 %collective-permute-start.13 = (f32[8,128]{1,0:T(8,128)S(1)}, f32[8,128]{1,0:T(8,128)S(1)}, u32[]{:S(2)}, u32[]{:S(2)}) collective-permute-start(f32[8,128]{1,0:T(8,128)S(1)} %add.18), channel_id=1, source_target_pairs={{0,5},{1,4},{2,7},{3,6},{4,1},{5,0},{6,3},{7,2},{8,13},{9,12},{10,... | collective-permute-start | bytes 12296 | tf_op jit(solution)/shard_map/ppermute | solution.py:275
  50.9 1.3 %collective-permute-done.13 = f32[8,128]{1,0:T(8,128)S(1)} collective-permute-done((f32[8,128]{1,0:T(8,128)S(1)}, f32[8,128]{1,0:T(8,128)S(1)}, u32[]{:S(2)}, u32[]{:S(2)}) %collective-permute-start.13) | collective-permute-done | bytes 4128 | tf_op jit(solution)/shard_map/ppermute | solution.py:275
  52.2 1.7 %collective-permute-start.14 = (f32[8,128]{1,0:T(8,128)S(1)}, f32[8,128]{1,0:T(8,128)S(1)}, u32[]{:S(2)}, u32[]{:S(2)}) collective-permute-start(f32[8,128]{1,0:T(8,128)S(1)} %add.19), channel_id=1, source_target_pairs={{0,9},{1,8},{2,11},{3,10},{4,13},{5,12},{6,15},{7,14},{8,1},{9,0},... | collective-permute-start | bytes 12296 | tf_op jit(solution)/shard_map/ppermute | solution.py:275
  53.9 1.3 %collective-permute-done.14 = f32[8,128]{1,0:T(8,128)S(1)} collective-permute-done((f32[8,128]{1,0:T(8,128)S(1)}, f32[8,128]{1,0:T(8,128)S(1)}, u32[]{:S(2)}, u32[]{:S(2)}) %collective-permute-start.14) | collective-permute-done | bytes 4128 | tf_op jit(solution)/shard_map/ppermute | solution.py:275
  55.3 2.7 %collective-permute-start.15 = (f32[8,128]{1,0:T(8,128)S(1)}, f32[8,128]{1,0:T(8,128)S(1)}, u32[]{:S(2)}, u32[]{:S(2)}) collective-permute-start(f32[8,128]{1,0:T(8,128)S(1)} %add.20.tile), channel_id=1, source_target_pairs={{0,17},{1,16},{2,19},{3,18},{4,21},{5,20},{6,23},{7,22},{8,25},{9,... | collective-permute-start | bytes 12296 | tf_op jit(solution)/shard_map/ppermute | solution.py:275
  58.0 1.3 %collective-permute-done.15.other = f32[8,128]{1,0:T(8,128)S(1)} collective-permute-done((f32[8,128]{1,0:T(8,128)S(1)}, f32[8,128]{1,0:T(8,128)S(1)}, u32[]{:S(2)}, u32[]{:S(2)}) %collective-permute-start.15) | collective-permute-done | bytes 4128 | tf_op jit(solution)/shard_map/ppermute | solution.py:275
  59.3 0.6 copy-done.12
  59.9 1.9 %final.1 = (f32[24,128]{1,0:T(8,128)}, f32[9]{0:T(128)}) custom-call(s32[1]{0:T(128)S(6)} %copy.12.counts.refs_0_, f32[8,24,128]{2,1,0:T(8,128)} %basis.5, f32[24,128]{1,0:T(8,128)} %get-tuple-element.10.image, f32[8,128]{1,0:T(8,128)} %copy-done.11, f32[8,128]{1,0:T(8,128)} %copy-done.12), custom_call_target="tpu_custom_call" | custom-call | tf_op jit(solution)/shard_map/final/pallas_call | solution.py:391
  (35 shorter events, 0.2 us)
Async XLA Ops:
  3.6 5.4 %collective-permute-start.1 = (f32[6,24,128]{2,1,0:T(8,128)}, f32[6,24,128]{2,1,0:T(8,128)S(1)}, u32[]{:S(2)}, u32[]{:S(2)}) collective-permute-start(f32[6,24,128]{2,1,0:T(8,128)} %prep.1.refs_4_), channel_id=1, source_target_pairs={{0,5},{1,4},{2,7},{3,6},{4,1},{5,0},{6,3},{7,2},{8,13},{9,12},{10,... | collective-permute-start | bytes 221192 | tf_op jit(solution)/shard_map/ppermute | solution.py:275
  6.0 5.4 %collective-permute-start = (f32[6,24,128]{2,1,0:T(8,128)}, f32[6,24,128]{2,1,0:T(8,128)S(1)}, u32[]{:S(2)}, u32[]{:S(2)}) collective-permute-start(f32[6,24,128]{2,1,0:T(8,128)} %prep.1.refs_4_), channel_id=1, source_target_pairs={{0,3},{1,2},{2,1},{3,0},{4,7},{5,6},{6,5},{7,4},{8,11},{9,10},{10,... | collective-permute-start | bytes 221192 | tf_op jit(solution)/shard_map/ppermute | solution.py:275
  9.0 11.3 %copy-start = (f32[6,24,128]{2,1,0:T(8,128)}, f32[6,24,128]{2,1,0:T(8,128)S(1)}, u32[]{:S(2)}) copy-start(f32[6,24,128]{2,1,0:T(8,128)S(1)} %collective-permute-done.1.refs_6_) | copy-start | bytes 221188
  9.0 4.4 %collective-permute-start.3 = (f32[6,24,128]{2,1,0:T(8,128)S(1)}, f32[6,24,128]{2,1,0:T(8,128)S(1)}, u32[]{:S(2)}, u32[]{:S(2)}) collective-permute-start(f32[6,24,128]{2,1,0:T(8,128)S(1)} %collective-permute-done.1.refs_6_), channel_id=1, source_target_pairs={{0,9},{1,8},{2,11},{3,10},{4,1},{5,0},{6,3},{7,2},{8,17},{9,16},{1... | collective-permute-start | bytes 221192 | tf_op jit(solution)/shard_map/ppermute | solution.py:275
  11.1 4.7 %collective-permute-start.5 = (f32[6,24,128]{2,1,0:T(8,128)}, f32[6,24,128]{2,1,0:T(8,128)S(1)}, u32[]{:S(2)}, u32[]{:S(2)}) collective-permute-start(f32[6,24,128]{2,1,0:T(8,128)} %prep.1.refs_4_), channel_id=1, source_target_pairs={{0,1},{1,0},{2,3},{3,2},{4,5},{5,4},{6,7},{7,6},{8,9},{9,8},{10,11... | collective-permute-start | bytes 221192 | tf_op jit(solution)/shard_map/ppermute | solution.py:275
  11.4 8.8 %copy-start.1 = (f32[6,24,128]{2,1,0:T(8,128)}, f32[6,24,128]{2,1,0:T(8,128)S(1)}, u32[]{:S(2)}) copy-start(f32[6,24,128]{2,1,0:T(8,128)S(1)} %collective-permute-done.refs_5_) | copy-start | bytes 221188
  11.4 4.7 %collective-permute-start.2 = (f32[6,24,128]{2,1,0:T(8,128)S(1)}, f32[6,24,128]{2,1,0:T(8,128)S(1)}, u32[]{:S(2)}, u32[]{:S(2)}) collective-permute-start(f32[6,24,128]{2,1,0:T(8,128)S(1)} %collective-permute-done.refs_5_), channel_id=1, source_target_pairs={{0,5},{1,4},{2,7},{3,6},{4,1},{5,0},{6,3},{7,2},{8,13},{9,12},{10,... | collective-permute-start | bytes 221192 | tf_op jit(solution)/shard_map/ppermute | solution.py:275
  13.4 6.9 %copy-start.2 = (f32[6,24,128]{2,1,0:T(8,128)}, f32[6,24,128]{2,1,0:T(8,128)S(1)}, u32[]{:S(2)}) copy-start(f32[6,24,128]{2,1,0:T(8,128)S(1)} %collective-permute-done.3.refs_8_) | copy-start | bytes 221188
  13.4 4.2 %collective-permute-start.4 = (f32[6,24,128]{2,1,0:T(8,128)S(1)}, f32[6,24,128]{2,1,0:T(8,128)S(1)}, u32[]{:S(2)}, u32[]{:S(2)}) collective-permute-start(f32[6,24,128]{2,1,0:T(8,128)S(1)} %collective-permute-done.3.refs_8_), channel_id=1, source_target_pairs={{0,3},{1,2},{2,1},{3,0},{4,7},{5,6},{6,5},{7,4},{8,11},{9,10},{10,... | collective-permute-start | bytes 221192 | tf_op jit(solution)/shard_map/ppermute | solution.py:275
  15.2 4.9 %collective-permute-start.7 = (f32[6,24,128]{2,1,0:T(8,128)S(1)}, f32[6,24,128]{2,1,0:T(8,128)S(1)}, u32[]{:S(2)}, u32[]{:S(2)}) collective-permute-start(f32[6,24,128]{2,1,0:T(8,128)S(1)} %collective-permute-done.1.refs_6_), channel_id=1, source_target_pairs={{0,1},{1,0},{2,3},{3,2},{4,5},{5,4},{6,7},{7,6},{8,9},{9,8},{10,11... | collective-permute-start | bytes 221192 | tf_op jit(solution)/shard_map/ppermute | solution.py:275
  15.6 4.5 %collective-permute-start.6 = (f32[6,24,128]{2,1,0:T(8,128)S(1)}, f32[6,24,128]{2,1,0:T(8,128)S(1)}, u32[]{:S(2)}, u32[]{:S(2)}) collective-permute-start(f32[6,24,128]{2,1,0:T(8,128)S(1)} %collective-permute-done.refs_5_), channel_id=1, source_target_pairs={{0,1},{1,0},{2,3},{3,2},{4,5},{5,4},{6,7},{7,6},{8,9},{9,8},{10,11... | collective-permute-start | bytes 221192 | tf_op jit(solution)/shard_map/ppermute | solution.py:275
  15.8 4.5 %copy-start.3 = (f32[6,24,128]{2,1,0:T(8,128)}, f32[6,24,128]{2,1,0:T(8,128)S(1)}, u32[]{:S(2)}) copy-start(f32[6,24,128]{2,1,0:T(8,128)S(1)} %collective-permute-done.5.refs_10_) | copy-start | bytes 221188
  15.8 4.4 %collective-permute-start.9 = (f32[6,24,128]{2,1,0:T(8,128)S(1)}, f32[6,24,128]{2,1,0:T(8,128)S(1)}, u32[]{:S(2)}, u32[]{:S(2)}) collective-permute-start(f32[6,24,128]{2,1,0:T(8,128)S(1)} %collective-permute-done.3.refs_8_), channel_id=1, source_target_pairs={{0,1},{1,0},{2,3},{3,2},{4,5},{5,4},{6,7},{7,6},{8,9},{9,8},{10,11... | collective-permute-start | bytes 221192 | tf_op jit(solution)/shard_map/ppermute | solution.py:275
  16.2 4.1 %copy-start.4 = (f32[6,24,128]{2,1,0:T(8,128)}, f32[6,24,128]{2,1,0:T(8,128)S(1)}, u32[]{:S(2)}) copy-start(f32[6,24,128]{2,1,0:T(8,128)S(1)} %collective-permute-done.2.refs_7_) | copy-start | bytes 221188
  16.2 4.0 %collective-permute-start.8 = (f32[6,24,128]{2,1,0:T(8,128)S(1)}, f32[6,24,128]{2,1,0:T(8,128)S(1)}, u32[]{:S(2)}, u32[]{:S(2)}) collective-permute-start(f32[6,24,128]{2,1,0:T(8,128)S(1)} %collective-permute-done.2.refs_7_), channel_id=1, source_target_pairs={{0,1},{1,0},{2,3},{3,2},{4,5},{5,4},{6,7},{7,6},{8,9},{9,8},{10,11... | collective-permute-start | bytes 221192 | tf_op jit(solution)/shard_map/ppermute | solution.py:275
  17.6 2.7 %copy-start.5 = (f32[6,24,128]{2,1,0:T(8,128)}, f32[6,24,128]{2,1,0:T(8,128)S(1)}, u32[]{:S(2)}) copy-start(f32[6,24,128]{2,1,0:T(8,128)S(1)} %collective-permute-done.4.refs_9_) | copy-start | bytes 221188
  17.6 2.6 %collective-permute-start.10 = (f32[6,24,128]{2,1,0:T(8,128)S(1)}, f32[6,24,128]{2,1,0:T(8,128)S(1)}, u32[]{:S(2)}, u32[]{:S(2)}) collective-permute-start(f32[6,24,128]{2,1,0:T(8,128)S(1)} %collective-permute-done.4.refs_9_), channel_id=1, source_target_pairs={{0,1},{1,0},{2,3},{3,2},{4,5},{5,4},{6,7},{7,6},{8,9},{9,8},{10,11... | collective-permute-start | bytes 221192 | tf_op jit(solution)/shard_map/ppermute | solution.py:275
  20.2 0.6 %copy-start.6 = (f32[6,24,128]{2,1,0:T(8,128)}, f32[6,24,128]{2,1,0:T(8,128)S(1)}, u32[]{:S(2)}) copy-start(f32[6,24,128]{2,1,0:T(8,128)S(1)} %collective-permute-done.7.refs_12_) | copy-start | bytes 221188
  20.2 0.7 %copy-start.7 = (f32[6,24,128]{2,1,0:T(8,128)}, f32[6,24,128]{2,1,0:T(8,128)S(1)}, u32[]{:S(2)}) copy-start(f32[6,24,128]{2,1,0:T(8,128)S(1)} %collective-permute-done.6.refs_11_) | copy-start | bytes 221188
  20.2 0.7 %copy-start.8 = (f32[6,24,128]{2,1,0:T(8,128)}, f32[6,24,128]{2,1,0:T(8,128)S(1)}, u32[]{:S(2)}) copy-start(f32[6,24,128]{2,1,0:T(8,128)S(1)} %collective-permute-done.9.refs_14_) | copy-start | bytes 221188
  20.2 0.7 %copy-start.9 = (f32[6,24,128]{2,1,0:T(8,128)}, f32[6,24,128]{2,1,0:T(8,128)S(1)}, u32[]{:S(2)}) copy-start(f32[6,24,128]{2,1,0:T(8,128)S(1)} %collective-permute-done.8.refs_13_) | copy-start | bytes 221188
  20.2 0.7 %copy-start.10 = (f32[6,24,128]{2,1,0:T(8,128)}, f32[6,24,128]{2,1,0:T(8,128)S(1)}, u32[]{:S(2)}) copy-start(f32[6,24,128]{2,1,0:T(8,128)S(1)} %collective-permute-done.10.refs_15_) | copy-start | bytes 221188
  43.6 1.4 %collective-permute-start.11 = (f32[8,128]{1,0:T(8,128)}, f32[8,128]{1,0:T(8,128)S(1)}, u32[]{:S(2)}, u32[]{:S(2)}) collective-permute-start(f32[8,128]{1,0:T(8,128)} %get-tuple-element.11), channel_id=1, source_target_pairs={{0,1},{1,0},{2,3},{3,2},{4,5},{5,4},{6,7},{7,6},{8,9},{9,8},{10,11... | collective-permute-start | bytes 12296 | tf_op jit(solution)/shard_map/ppermute | solution.py:275
  45.8 3.3 %collective-permute-start.12 = (f32[8,128]{1,0:T(8,128)S(1)}, f32[8,128]{1,0:T(8,128)S(1)}, u32[]{:S(2)}, u32[]{:S(2)}) collective-permute-start(f32[8,128]{1,0:T(8,128)S(1)} %add.17), channel_id=1, source_target_pairs={{0,3},{1,2},{2,1},{3,0},{4,7},{5,6},{6,5},{7,4},{8,11},{9,10},{10,... | collective-permute-start | bytes 12296 | tf_op jit(solution)/shard_map/ppermute | solution.py:275
  49.1 3.1 %collective-permute-start.13 = (f32[8,128]{1,0:T(8,128)S(1)}, f32[8,128]{1,0:T(8,128)S(1)}, u32[]{:S(2)}, u32[]{:S(2)}) collective-permute-start(f32[8,128]{1,0:T(8,128)S(1)} %add.18), channel_id=1, source_target_pairs={{0,5},{1,4},{2,7},{3,6},{4,1},{5,0},{6,3},{7,2},{8,13},{9,12},{10,... | collective-permute-start | bytes 12296 | tf_op jit(solution)/shard_map/ppermute | solution.py:275
  52.2 3.0 %collective-permute-start.14 = (f32[8,128]{1,0:T(8,128)S(1)}, f32[8,128]{1,0:T(8,128)S(1)}, u32[]{:S(2)}, u32[]{:S(2)}) collective-permute-start(f32[8,128]{1,0:T(8,128)S(1)} %add.19), channel_id=1, source_target_pairs={{0,9},{1,8},{2,11},{3,10},{4,13},{5,12},{6,15},{7,14},{8,1},{9,0},... | collective-permute-start | bytes 12296 | tf_op jit(solution)/shard_map/ppermute | solution.py:275
  55.3 4.0 %copy-start.11 = (f32[8,128]{1,0:T(8,128)}, f32[8,128]{1,0:T(8,128)S(1)}, u32[]{:S(2)}) copy-start(f32[8,128]{1,0:T(8,128)S(1)} %add.20.tile) | copy-start | bytes 12292
  55.3 4.0 %collective-permute-start.15 = (f32[8,128]{1,0:T(8,128)S(1)}, f32[8,128]{1,0:T(8,128)S(1)}, u32[]{:S(2)}, u32[]{:S(2)}) collective-permute-start(f32[8,128]{1,0:T(8,128)S(1)} %add.20.tile), channel_id=1, source_target_pairs={{0,17},{1,16},{2,19},{3,18},{4,21},{5,20},{6,23},{7,22},{8,25},{9,... | collective-permute-start | bytes 12296 | tf_op jit(solution)/shard_map/ppermute | solution.py:275
  59.3 0.6 copy-start.12

commit v5 on v4

--- a/solution.py
+++ b/solution.py
@@ -13,7 +13,7 @@
 f32 = jnp.float32
 WIDTH = 16
 CENTRE = 2.0
-UNROLL = 4
+UNROLL = 8
 LIMIT = 56 * 1024 * 1024
 
 across = (((1,), (1,)), ((), ()))
@@ -21,6 +21,10 @@
 
 def vmem(count):
     return [pl.BlockSpec(memory_space=pltpu.VMEM)] * count
+
+
+def anywhere(count):
+    return [pl.BlockSpec(memory_space=pl.ANY)] * count
 
 
 def smem(count):
@@ -138,9 +142,7 @@
     depth = taken.shape[1]
     taken[:, entries:, :] = jnp.zeros((taken.shape[0], depth - entries, panels), f32)
 
-    def leaf_body(leaf, i):
-        for e in range(entries):
-            taken[i, e : e + 1, :] = poles32[pl.ds(far[leaf, e], 1), :]
+    def near_body(leaf, i):
         total = jnp.zeros((panels, panels), f32)
         for start in range(0, neighbours, 2):
             ids = [near[leaf, e] for e in range(start, min(start + 2, neighbours))]
@@ -150,6 +152,10 @@
             for e, s in enumerate(ids):
                 total += inverse[:, e * panels : (e + 1) * panels] * charge[pl.ds(s, 1), :]
         totals[leaf] = total
+
+    def far_gather(leaf, i):
+        for e in range(entries):
+            taken[i, e : e + 1, :] = poles32[pl.ds(far[leaf, e], 1), :]
         pole = taken[i]
         high = pole.astype(bf16)
         pole = jnp.concatenate([high, (pole - high.astype(f32)).astype(bf16)], axis=1)
@@ -161,7 +167,8 @@
         both = jnp.dot(by_class, pole, preferred_element_type=f32)
         found[leaf] = both[:, 0:panels] + both[:, panels : 2 * panels]
 
-    repeat(leaves, UNROLL, leaf_body)
+    repeat(leaves, 12, near_body)
+    repeat(leaves, UNROLL, far_gather)
     nearby = jnp.concatenate(
         [jnp.sum(totals[leaf].T, axis=0, keepdims=True) for leaf in range(leaves)], axis=0
     )
@@ -189,7 +196,7 @@
         tail = m2l[:, full * group : offsets, :].astype(f32)
         tail = jnp.concatenate([tail, jnp.zeros((terms, group - rest, terms), f32)], axis=1)
         sums[...] = translate(tail.reshape(terms * group, terms).astype(bf16), full * group)
-    batch = next(n for n in range(min(13, full), 0, -1) if full % n == 0)
+    batch = next(n for n in range(min(39, full), 0, -1) if full % n == 0)
 
     def far_body(step, carry):
         value = None
@@ -239,7 +246,15 @@
     lax.fori_loop(0, count // batch, several, 0)
 
 
-def final_kernel(counts, basis, image, tile, other, vector, column):
+def final_kernel(counts, *refs):
+    vector, column = refs[4:6]
+    basis, image, tile, other = refs[6:10]
+    sems = refs[10]
+    copies = [pltpu.make_async_copy(refs[i], refs[6 + i], sems.at[i]) for i in range(4)]
+    for copy in copies:
+        copy.start()
+    for copy in copies:
+        copy.wait()
     krylov, leaves, panels = basis.shape
     sums = tile[...] + other[...]
     population = sums[0:1, 2:3]
@@ -298,6 +313,7 @@
     terms, offsets = m2l.shape[:2]
     groups = lax.axis_size("grp")
     params = pltpu.CompilerParams(vmem_limit_bytes=LIMIT)
+    small = pltpu.CompilerParams(vmem_limit_bytes=LIMIT // 8)
     here = lax.axis_index("seg")
     odd = here % 2
     order_low = 2 - odd
@@ -320,20 +336,20 @@
     def spread(pieces):
         bit = 2
         while bit < groups:
-            mask = bit | 1
-            pieces = pieces + [(swap(v, 0, mask), order, rel ^ mask) for v, order, rel in pieces]
+            pieces = pieces + [swap(v, 0, bit | 1) for v in pieces]
             bit *= 2
         return pieces
 
     beside = swap(block, 1, 1)
-    own = spread([(block, 0, 0)])
-    beyond = hop(beside)
-    pieces = own + [(beside, 1, 1)] + [(swap(v, 1, 1), 1, rel ^ 1) for v, _, rel in own[1:]]
-    pieces = pieces + spread([(beyond, 2, 0)])
-    pieces = pieces + [(swap(v, 0, 1), order, rel ^ 1) for v, order, rel in pieces]
-    table = [[0] * groups for _ in range(3)]
-    for at, (_, order, rel) in enumerate(pieces):
-        table[order][rel] = at
+    own = spread([block])
+    rels = [0]
+    bit = 2
+    while bit < groups:
+        rels = rels + [rel ^ bit ^ 1 for rel in rels]
+        bit *= 2
+    keys = [(0, rel) for rel in rels] + [(1, rel ^ 1) for rel in rels] + [(2, rel) for rel in rels]
+    keys = keys + [(order, rel ^ 1) for order, rel in keys]
+    table = [[keys.index((order, rel)) for rel in range(groups)] for order in range(3)]
     near_slots, far_slots, gram = pl.pallas_call(
         functools.partial(plan_kernel, table),
         out_shape=(
@@ -347,16 +363,18 @@
         name="plan",
     )(counts, position, basis, near_list, far_list)
 
+    beside, near_slots = lax.optimization_barrier((beside, near_slots))
+    beyond = hop(beside)
+    pieces = own + [beside] + [swap(v, 1, 1) for v in own[1:]] + spread([beyond])
+    pieces = pieces + [swap(v, 0, 1) for v in pieces]
+
     image, tile = pl.pallas_call(
-        functools.partial(main_kernel, [order for _, order, _ in pieces]),
+        functools.partial(main_kernel, [order for order, _ in keys]),
         out_shape=(
             jax.ShapeDtypeStruct((leaves, panels), f32),
             jax.ShapeDtypeStruct((krylov, panels), f32),
         ),
-        in_specs=smem(4)
-        + vmem(len(pieces) + 1)
-        + [pl.BlockSpec(memory_space=pl.ANY)]
-        + vmem(3),
+        in_specs=smem(4) + vmem(len(pieces) + 1) + anywhere(1) + vmem(3),
         out_specs=tuple(vmem(2)),
         scratch_shapes=[
             pltpu.VMEM(m2l.shape, bf16),
@@ -376,7 +394,7 @@
         name="main",
     )(
         counts, position, near_slots, far_slots,
-        *[v for v, _, _ in pieces], far_offset, m2l, l2p, basis, gram,
+        *pieces, far_offset, m2l, l2p, basis, gram,
     )
 
     def masks(axis):
@@ -394,9 +412,11 @@
             jax.ShapeDtypeStruct((leaves, panels), f32),
             jax.ShapeDtypeStruct((krylov + 1,), f32),
         ),
-        in_specs=smem(1) + vmem(4),
+        in_specs=smem(1) + anywhere(4),
         out_specs=tuple(vmem(2)),
-        compiler_params=params,
+        scratch_shapes=[pltpu.VMEM(a.shape, f32) for a in (basis, image, tile, other)]
+        + [pltpu.SemaphoreType.DMA((4,))],
+        compiler_params=small,
         name="final",
     )(counts, basis, image, tile, other)
 

time: 62.1 us -> 60.6 us (0.976)
  starting transfers between devices: 18.3 us -> 17 us
    ppermute x16, starting transfers between devices: 18.3 us -> 17 us  [move(): return lax.ppermute(value, ('seg', 'grp'), moves)]
    pallas_call x1, Pallas kernels: 1.86 us -> 1.11 us  [on_device(): pl.pallas_call(final_kernel, out_shape=(jax.ShapeDtypeStruct((leaves, pan...]
  transfers between devices with their start and end apart: 16 -> 16, of which waited for: 8 -> 9; matrix products, arithmetic and copies ran while one was open for 1% -> 1% of each run, Pallas kernels for 3% -> 3%
where the time goes in v5:
time: 60.6 us; the launch traced here: 60.3 us
  Pallas kernels  28 us (46%)
  starting transfers between devices  17 us (28%)
  waiting for transfers between devices  11 us (18%)
  between operations  1.62 us (3%)
  local copies, waits for them, and re-layouts  1.31 us (2%)
  other arithmetic  1.31 us (2%)
    pallas_call x1, Pallas kernels, on_device(): pl.pallas_call(functools.partial(main_kernel, [order for order, _ in keys...  22.9 us
    ppermute x16, starting transfers between devices, move(): return lax.ppermute(value, ('seg', 'grp'), moves)  17 us
    ppermute x16, waiting for transfers between devices, move(): return lax.ppermute(value, ('seg', 'grp'), moves)  11 us
    pallas_call x1, Pallas kernels, on_device(): pl.pallas_call(prep_kernel, out_shape=jax.ShapeDtypeStruct((6, leaves, pa...  2.3 us
    pallas_call x1, Pallas kernels, on_device(): pl.pallas_call(functools.partial(plan_kernel, table), out_shape=(jax.Shap...  1.66 us
    unnamed x26, local copies, waits for them, and re-layouts  1.31 us
  transfers between devices with their start and end apart: 16, of which 9 were waited for; matrix products, arithmetic and copies ran while one was open for 1% of the time, Pallas kernels for 3%

profile of v5, /device:TPU:0, one launch (start us, length us, event | category | flops | bytes accessed | tf_op | source)
XLA Modules:
  0.0 60.3 jit_solution(1166664614110891883)
XLA Ops:
  0.6 0.0 copy-start
  1.3 2.3 %prep.1.refs_4_ = f32[6,24,128]{2,1,0:T(8,128)} custom-call(s32[1]{0:T(128)S(6)} %copy.12.counts.refs_0_, f32[8,24,128]{2,1,0:T(8,128)} %refs_0_.2, f32[3,24,128]{2,1,0:T(8,128)} %bitcast.10, f32[24,128]{1,0:T(8,128)} %areas.1, bf16[121,24,128]{2,1,0:T(8,128)(2,1)} %bitcast.8), custom_call_target="tpu_custom_call" | custom-call | tf_op jit(solution)/shard_map/prep/pallas_call | solution.py:323
  3.6 2.4 %collective-permute-start.1 = (f32[6,24,128]{2,1,0:T(8,128)}, f32[6,24,128]{2,1,0:T(8,128)S(1)}, u32[]{:S(2)}, u32[]{:S(2)}) collective-permute-start(f32[6,24,128]{2,1,0:T(8,128)} %prep.1.refs_4_), channel_id=1, source_target_pairs={{0,3},{1,2},{2,1},{3,0},{4,7},{5,6},{6,5},{7,4},{8,11},{9,10},{10,... | collective-permute-start | bytes 221192 | tf_op jit(solution)/shard_map/ppermute | solution.py:290
  6.0 1.8 %collective-permute-start = (f32[6,24,128]{2,1,0:T(8,128)}, f32[6,24,128]{2,1,0:T(8,128)S(1)}, u32[]{:S(2)}, u32[]{:S(2)}) collective-permute-start(f32[6,24,128]{2,1,0:T(8,128)} %prep.1.refs_4_), channel_id=1, source_target_pairs={{0,5},{1,4},{2,7},{3,6},{4,1},{5,0},{6,3},{7,2},{8,13},{9,12},{10,... | collective-permute-start | bytes 221192 | tf_op jit(solution)/shard_map/ppermute | solution.py:290
  7.8 0.6 %pad_add_fusion.place.refs_1_ = s32[3]{0:T(128)} fusion(s32[1]{0:T(128)} %bitcast.2, s32[1]{0:T(128)} %bitcast.1, s32[1]{0:T(128)} %bitcast), kind=kLoop, calls=%fused_computation | loop fusion | flops 6 | bytes 24 | tf_op jit(solution)/shard_map/stack | solution.py:321
  8.4 1.7 %plan.1 = (s32[24,27]{1,0:T(8,128)}, s32[24,189]{1,0:T(8,128)}, f32[8,128]{1,0:T(8,128)}) custom-call(s32[1]{0:T(128)S(6)} %copy.12.counts.refs_0_, s32[3]{0:T(128)} %pad_add_fusion.place.refs_1_, f32[8,24,128]{2,1,0:T(8,128)} %refs_0_.2, s32[24,27]{1,0:T(8,128)} %near.1, s32[24,189]{1,0:T(8,128)} %far.1), custom_call_target="tpu_custom_call" | custom-call | tf_op jit(solution)/shard_map/plan/pallas_call | solution.py:353
  10.1 0.1 collective-permute-done.refs_6_
  10.1 1.7 %collective-permute-start.3 = (f32[6,24,128]{2,1,0:T(8,128)S(1)}, f32[6,24,128]{2,1,0:T(8,128)S(1)}, u32[]{:S(2)}, u32[]{:S(2)}) collective-permute-start(f32[6,24,128]{2,1,0:T(8,128)S(1)} %collective-permute-done.refs_6_), channel_id=1, source_target_pairs={{0,9},{1,8},{2,11},{3,10},{4,1},{5,0},{6,3},{7,2},{8,17},{9,16},{1... | collective-permute-start | bytes 221192 | tf_op jit(solution)/shard_map/ppermute | solution.py:290
  11.9 0.6 collective-permute-start.2
  12.4 1.6 %collective-permute-done.3.refs_8_ = f32[6,24,128]{2,1,0:T(8,128)S(1)} collective-permute-done((f32[6,24,128]{2,1,0:T(8,128)S(1)}, f32[6,24,128]{2,1,0:T(8,128)S(1)}, u32[]{:S(2)}, u32[]{:S(2)}) %collective-permute-start.3) | collective-permute-done | bytes 73760 | tf_op jit(solution)/shard_map/ppermute | solution.py:290
  14.0 1.9 %collective-permute-start.4 = (f32[6,24,128]{2,1,0:T(8,128)S(1)}, f32[6,24,128]{2,1,0:T(8,128)S(1)}, u32[]{:S(2)}, u32[]{:S(2)}) collective-permute-start(f32[6,24,128]{2,1,0:T(8,128)S(1)} %collective-permute-done.3.refs_8_), channel_id=1, source_target_pairs={{0,3},{1,2},{2,1},{3,0},{4,7},{5,6},{6,5},{7,4},{8,11},{9,10},{10,... | collective-permute-start | bytes 221192 | tf_op jit(solution)/shard_map/ppermute | solution.py:290
  15.9 0.5 collective-permute-start.6
  16.4 0.1 collective-permute-start.9
  16.5 0.4 collective-permute-start.8
  16.9 1.3 %collective-permute-done.4.refs_9_ = f32[6,24,128]{2,1,0:T(8,128)S(1)} collective-permute-done((f32[6,24,128]{2,1,0:T(8,128)S(1)}, f32[6,24,128]{2,1,0:T(8,128)S(1)}, u32[]{:S(2)}, u32[]{:S(2)}) %collective-permute-start.4) | collective-permute-done | bytes 73760 | tf_op jit(solution)/shard_map/ppermute | solution.py:290
  18.2 0.3 collective-permute-start.10
  18.6 0.9 %collective-permute-done.10.refs_15_ = f32[6,24,128]{2,1,0:T(8,128)S(1)} collective-permute-done((f32[6,24,128]{2,1,0:T(8,128)S(1)}, f32[6,24,128]{2,1,0:T(8,128)S(1)}, u32[]{:S(2)}, u32[]{:S(2)}) %collective-permute-start.10) | collective-permute-done | bytes 73760 | tf_op jit(solution)/shard_map/ppermute | solution.py:290
  19.6 0.6 copy-done.12
  20.1 22.9 %main.1 = (f32[24,128]{1,0:T(8,128)}, f32[8,128]{1,0:T(8,128)}) custom-call(s32[1]{0:T(128)S(6)} %copy.12.counts.refs_0_, s32[3]{0:T(128)} %pad_add_fusion.place.refs_1_, s32[24,27]{1,0:T(8,128)} %get-tuple-element.10.refs_2_, s32[24,189]{1,0:T(8,128)} %get-tuple-element.11.refs_3_, f32[6,24,128]{2,1,0:T(8,128)} %prep.1.refs_4_, f32[6,24,128]{2,1,0:T(8,128)} %copy-done.2, ...), custom_call_target="tpu_custom_call" | custom-call | tf_op jit(solution)/shard_map/main/pallas_call | solution.py:371
  43.1 0.4 collective-permute-start.11
  43.5 1.1 %collective-permute-done.11 = f32[8,128]{1,0:T(8,128)S(1)} collective-permute-done((f32[8,128]{1,0:T(8,128)}, f32[8,128]{1,0:T(8,128)S(1)}, u32[]{:S(2)}, u32[]{:S(2)}) %collective-permute-start.11) | collective-permute-done | bytes 4128 | tf_op jit(solution)/shard_map/ppermute | solution.py:290
  44.5 0.7 %add.17 = f32[8,128]{1,0:T(8,128)S(1)} add(f32[8,128]{1,0:T(8,128)} %get-tuple-element.15, f32[8,128]{1,0:T(8,128)S(1)} %collective-permute-done.11) | non-fusion elementwise | flops 1024 | bytes 12288 | tf_op jit(solution)/shard_map/add | solution.py:406
  45.2 1.5 %collective-permute-start.12 = (f32[8,128]{1,0:T(8,128)S(1)}, f32[8,128]{1,0:T(8,128)S(1)}, u32[]{:S(2)}, u32[]{:S(2)}) collective-permute-start(f32[8,128]{1,0:T(8,128)S(1)} %add.17), channel_id=1, source_target_pairs={{0,3},{1,2},{2,1},{3,0},{4,7},{5,6},{6,5},{7,4},{8,11},{9,10},{10,... | collective-permute-start | bytes 12296 | tf_op jit(solution)/shard_map/ppermute | solution.py:290
  46.7 1.6 %collective-permute-done.12 = f32[8,128]{1,0:T(8,128)S(1)} collective-permute-done((f32[8,128]{1,0:T(8,128)S(1)}, f32[8,128]{1,0:T(8,128)S(1)}, u32[]{:S(2)}, u32[]{:S(2)}) %collective-permute-start.12) | collective-permute-done | bytes 4128 | tf_op jit(solution)/shard_map/ppermute | solution.py:290
  48.2 1.5 %collective-permute-start.13 = (f32[8,128]{1,0:T(8,128)S(1)}, f32[8,128]{1,0:T(8,128)S(1)}, u32[]{:S(2)}, u32[]{:S(2)}) collective-permute-start(f32[8,128]{1,0:T(8,128)S(1)} %add.18), channel_id=1, source_target_pairs={{0,5},{1,4},{2,7},{3,6},{4,1},{5,0},{6,3},{7,2},{8,13},{9,12},{10,... | collective-permute-start | bytes 12296 | tf_op jit(solution)/shard_map/ppermute | solution.py:290
  49.7 1.6 %collective-permute-done.13 = f32[8,128]{1,0:T(8,128)S(1)} collective-permute-done((f32[8,128]{1,0:T(8,128)S(1)}, f32[8,128]{1,0:T(8,128)S(1)}, u32[]{:S(2)}, u32[]{:S(2)}) %collective-permute-start.13) | collective-permute-done | bytes 4128 | tf_op jit(solution)/shard_map/ppermute | solution.py:290
  51.3 1.4 %collective-permute-start.14 = (f32[8,128]{1,0:T(8,128)S(1)}, f32[8,128]{1,0:T(8,128)S(1)}, u32[]{:S(2)}, u32[]{:S(2)}) collective-permute-start(f32[8,128]{1,0:T(8,128)S(1)} %add.19), channel_id=1, source_target_pairs={{0,9},{1,8},{2,11},{3,10},{4,13},{5,12},{6,15},{7,14},{8,1},{9,0},... | collective-permute-start | bytes 12296 | tf_op jit(solution)/shard_map/ppermute | solution.py:290
  52.6 1.7 %collective-permute-done.14 = f32[8,128]{1,0:T(8,128)S(1)} collective-permute-done((f32[8,128]{1,0:T(8,128)S(1)}, f32[8,128]{1,0:T(8,128)S(1)}, u32[]{:S(2)}, u32[]{:S(2)}) %collective-permute-start.14) | collective-permute-done | bytes 4128 | tf_op jit(solution)/shard_map/ppermute | solution.py:290
  54.3 2.6 %collective-permute-start.15 = (f32[8,128]{1,0:T(8,128)S(1)}, f32[8,128]{1,0:T(8,128)S(1)}, u32[]{:S(2)}, u32[]{:S(2)}) collective-permute-start(f32[8,128]{1,0:T(8,128)S(1)} %add.20.refs_2_), channel_id=1, source_target_pairs={{0,17},{1,16},{2,19},{3,18},{4,21},{5,20},{6,23},{7,22},{8,25},{9,... | collective-permute-start | bytes 12296 | tf_op jit(solution)/shard_map/ppermute | solution.py:290
  56.9 1.3 %collective-permute-done.15.refs_3_ = f32[8,128]{1,0:T(8,128)S(1)} collective-permute-done((f32[8,128]{1,0:T(8,128)S(1)}, f32[8,128]{1,0:T(8,128)S(1)}, u32[]{:S(2)}, u32[]{:S(2)}) %collective-permute-start.15) | collective-permute-done | bytes 4128 | tf_op jit(solution)/shard_map/ppermute | solution.py:290
  58.3 0.7 %copy-done.1 = f32[24,128]{1,0:T(8,128)S(1)} copy-done((f32[24,128]{1,0:T(8,128)S(1)}, f32[24,128]{1,0:T(8,128)}, u32[]{:S(2)}) %copy-start.1) | copy-done | bytes 12312
  59.0 1.1 %final.1 = (f32[24,128]{1,0:T(8,128)}, f32[9]{0:T(128)}) custom-call(s32[1]{0:T(128)S(6)} %copy.12.counts.refs_0_, f32[8,24,128]{2,1,0:T(8,128)S(1)} %copy-done, f32[24,128]{1,0:T(8,128)S(1)} %copy-done.1, f32[8,128]{1,0:T(8,128)S(1)} %add.20.refs_2_, f32[8,128]{1,0:T(8,128)S(1)} %collective-permute-done.15.refs_3_), custom_call_target="tpu_custom_call" | custom-call | tf_op jit(solution)/shard_map/final/pallas_call | solution.py:409
  (35 shorter events, 0.1 us)
Async XLA Ops:
  0.6 57.6 %copy-start = (f32[8,24,128]{2,1,0:T(8,128)S(1)}, f32[8,24,128]{2,1,0:T(8,128)}, u32[]{:S(2)}) copy-start(f32[8,24,128]{2,1,0:T(8,128)} %refs_0_.2) | copy-start | bytes 294916
  3.6 8.3 %collective-permute-start.1 = (f32[6,24,128]{2,1,0:T(8,128)}, f32[6,24,128]{2,1,0:T(8,128)S(1)}, u32[]{:S(2)}, u32[]{:S(2)}) collective-permute-start(f32[6,24,128]{2,1,0:T(8,128)} %prep.1.refs_4_), channel_id=1, source_target_pairs={{0,3},{1,2},{2,1},{3,0},{4,7},{5,6},{6,5},{7,4},{8,11},{9,10},{10,... | collective-permute-start | bytes 221192 | tf_op jit(solution)/shard_map/ppermute | solution.py:290
  6.0 4.1 %collective-permute-start = (f32[6,24,128]{2,1,0:T(8,128)}, f32[6,24,128]{2,1,0:T(8,128)S(1)}, u32[]{:S(2)}, u32[]{:S(2)}) collective-permute-start(f32[6,24,128]{2,1,0:T(8,128)} %prep.1.refs_4_), channel_id=1, source_target_pairs={{0,5},{1,4},{2,7},{3,6},{4,1},{5,0},{6,3},{7,2},{8,13},{9,12},{10,... | collective-permute-start | bytes 221192 | tf_op jit(solution)/shard_map/ppermute | solution.py:290
  10.1 9.4 %copy-start.3 = (f32[6,24,128]{2,1,0:T(8,128)}, f32[6,24,128]{2,1,0:T(8,128)S(1)}, u32[]{:S(2)}) copy-start(f32[6,24,128]{2,1,0:T(8,128)S(1)} %collective-permute-done.refs_6_) | copy-start | bytes 221188
  10.1 3.9 %collective-permute-start.3 = (f32[6,24,128]{2,1,0:T(8,128)S(1)}, f32[6,24,128]{2,1,0:T(8,128)S(1)}, u32[]{:S(2)}, u32[]{:S(2)}) collective-permute-start(f32[6,24,128]{2,1,0:T(8,128)S(1)} %collective-permute-done.refs_6_), channel_id=1, source_target_pairs={{0,9},{1,8},{2,11},{3,10},{4,1},{5,0},{6,3},{7,2},{8,17},{9,16},{1... | collective-permute-start | bytes 221192 | tf_op jit(solution)/shard_map/ppermute | solution.py:290
  11.9 4.5 %collective-permute-start.5 = (f32[6,24,128]{2,1,0:T(8,128)}, f32[6,24,128]{2,1,0:T(8,128)S(1)}, u32[]{:S(2)}, u32[]{:S(2)}) collective-permute-start(f32[6,24,128]{2,1,0:T(8,128)} %prep.1.refs_4_), channel_id=1, source_target_pairs={{0,1},{1,0},{2,3},{3,2},{4,5},{5,4},{6,7},{7,6},{8,9},{9,8},{10,11... | collective-permute-start | bytes 221192 | tf_op jit(solution)/shard_map/ppermute | solution.py:290
  11.9 7.6 %copy-start.2 = (f32[6,24,128]{2,1,0:T(8,128)}, f32[6,24,128]{2,1,0:T(8,128)S(1)}, u32[]{:S(2)}) copy-start(f32[6,24,128]{2,1,0:T(8,128)S(1)} %collective-permute-done.1.refs_5_) | copy-start | bytes 221188
  11.9 4.6 %collective-permute-start.2 = (f32[6,24,128]{2,1,0:T(8,128)S(1)}, f32[6,24,128]{2,1,0:T(8,128)S(1)}, u32[]{:S(2)}, u32[]{:S(2)}) collective-permute-start(f32[6,24,128]{2,1,0:T(8,128)S(1)} %collective-permute-done.1.refs_5_), channel_id=1, source_target_pairs={{0,5},{1,4},{2,7},{3,6},{4,1},{5,0},{6,3},{7,2},{8,13},{9,12},{10,... | collective-permute-start | bytes 221192 | tf_op jit(solution)/shard_map/ppermute | solution.py:290
  14.0 5.5 %copy-start.4 = (f32[6,24,128]{2,1,0:T(8,128)}, f32[6,24,128]{2,1,0:T(8,128)S(1)}, u32[]{:S(2)}) copy-start(f32[6,24,128]{2,1,0:T(8,128)S(1)} %collective-permute-done.3.refs_8_) | copy-start | bytes 221188
  14.0 4.2 %collective-permute-start.4 = (f32[6,24,128]{2,1,0:T(8,128)S(1)}, f32[6,24,128]{2,1,0:T(8,128)S(1)}, u32[]{:S(2)}, u32[]{:S(2)}) collective-permute-start(f32[6,24,128]{2,1,0:T(8,128)S(1)} %collective-permute-done.3.refs_8_), channel_id=1, source_target_pairs={{0,3},{1,2},{2,1},{3,0},{4,7},{5,6},{6,5},{7,4},{8,11},{9,10},{10,... | collective-permute-start | bytes 221192 | tf_op jit(solution)/shard_map/ppermute | solution.py:290
  15.9 2.7 %collective-permute-start.7 = (f32[6,24,128]{2,1,0:T(8,128)S(1)}, f32[6,24,128]{2,1,0:T(8,128)S(1)}, u32[]{:S(2)}, u32[]{:S(2)}) collective-permute-start(f32[6,24,128]{2,1,0:T(8,128)S(1)} %collective-permute-done.refs_6_), channel_id=1, source_target_pairs={{0,1},{1,0},{2,3},{3,2},{4,5},{5,4},{6,7},{7,6},{8,9},{9,8},{10,11... | collective-permute-start | bytes 221192 | tf_op jit(solution)/shard_map/ppermute | solution.py:290
  15.9 2.6 %collective-permute-start.6 = (f32[6,24,128]{2,1,0:T(8,128)S(1)}, f32[6,24,128]{2,1,0:T(8,128)S(1)}, u32[]{:S(2)}, u32[]{:S(2)}) collective-permute-start(f32[6,24,128]{2,1,0:T(8,128)S(1)} %collective-permute-done.1.refs_5_), channel_id=1, source_target_pairs={{0,1},{1,0},{2,3},{3,2},{4,5},{5,4},{6,7},{7,6},{8,9},{9,8},{10,11... | collective-permute-start | bytes 221192 | tf_op jit(solution)/shard_map/ppermute | solution.py:290
  16.4 3.1 %copy-start.5 = (f32[6,24,128]{2,1,0:T(8,128)}, f32[6,24,128]{2,1,0:T(8,128)S(1)}, u32[]{:S(2)}) copy-start(f32[6,24,128]{2,1,0:T(8,128)S(1)} %collective-permute-done.5.refs_10_) | copy-start | bytes 221188
  16.4 2.2 %collective-permute-start.9 = (f32[6,24,128]{2,1,0:T(8,128)S(1)}, f32[6,24,128]{2,1,0:T(8,128)S(1)}, u32[]{:S(2)}, u32[]{:S(2)}) collective-permute-start(f32[6,24,128]{2,1,0:T(8,128)S(1)} %collective-permute-done.3.refs_8_), channel_id=1, source_target_pairs={{0,1},{1,0},{2,3},{3,2},{4,5},{5,4},{6,7},{7,6},{8,9},{9,8},{10,11... | collective-permute-start | bytes 221192 | tf_op jit(solution)/shard_map/ppermute | solution.py:290
  16.5 3.0 %copy-start.6 = (f32[6,24,128]{2,1,0:T(8,128)}, f32[6,24,128]{2,1,0:T(8,128)S(1)}, u32[]{:S(2)}) copy-start(f32[6,24,128]{2,1,0:T(8,128)S(1)} %collective-permute-done.2.refs_7_) | copy-start | bytes 221188
  16.5 2.1 %collective-permute-start.8 = (f32[6,24,128]{2,1,0:T(8,128)S(1)}, f32[6,24,128]{2,1,0:T(8,128)S(1)}, u32[]{:S(2)}, u32[]{:S(2)}) collective-permute-start(f32[6,24,128]{2,1,0:T(8,128)S(1)} %collective-permute-done.2.refs_7_), channel_id=1, source_target_pairs={{0,1},{1,0},{2,3},{3,2},{4,5},{5,4},{6,7},{7,6},{8,9},{9,8},{10,11... | collective-permute-start | bytes 221192 | tf_op jit(solution)/shard_map/ppermute | solution.py:290
  18.2 1.3 %copy-start.7 = (f32[6,24,128]{2,1,0:T(8,128)}, f32[6,24,128]{2,1,0:T(8,128)S(1)}, u32[]{:S(2)}) copy-start(f32[6,24,128]{2,1,0:T(8,128)S(1)} %collective-permute-done.4.refs_9_) | copy-start | bytes 221188
  18.2 1.3 %collective-permute-start.10 = (f32[6,24,128]{2,1,0:T(8,128)S(1)}, f32[6,24,128]{2,1,0:T(8,128)S(1)}, u32[]{:S(2)}, u32[]{:S(2)}) collective-permute-start(f32[6,24,128]{2,1,0:T(8,128)S(1)} %collective-permute-done.4.refs_9_), channel_id=1, source_target_pairs={{0,1},{1,0},{2,3},{3,2},{4,5},{5,4},{6,7},{7,6},{8,9},{9,8},{10,11... | collective-permute-start | bytes 221192 | tf_op jit(solution)/shard_map/ppermute | solution.py:290
  18.5 1.0 %copy-start.9 = (f32[6,24,128]{2,1,0:T(8,128)}, f32[6,24,128]{2,1,0:T(8,128)S(1)}, u32[]{:S(2)}) copy-start(f32[6,24,128]{2,1,0:T(8,128)S(1)} %collective-permute-done.6.refs_11_) | copy-start | bytes 221188
  18.6 1.0 %copy-start.8 = (f32[6,24,128]{2,1,0:T(8,128)}, f32[6,24,128]{2,1,0:T(8,128)S(1)}, u32[]{:S(2)}) copy-start(f32[6,24,128]{2,1,0:T(8,128)S(1)} %collective-permute-done.7.refs_12_) | copy-start | bytes 221188
  18.6 1.0 %copy-start.11 = (f32[6,24,128]{2,1,0:T(8,128)}, f32[6,24,128]{2,1,0:T(8,128)S(1)}, u32[]{:S(2)}) copy-start(f32[6,24,128]{2,1,0:T(8,128)S(1)} %collective-permute-done.8.refs_13_) | copy-start | bytes 221188
  18.6 1.0 %copy-start.10 = (f32[6,24,128]{2,1,0:T(8,128)}, f32[6,24,128]{2,1,0:T(8,128)S(1)}, u32[]{:S(2)}) copy-start(f32[6,24,128]{2,1,0:T(8,128)S(1)} %collective-permute-done.9.refs_14_) | copy-start | bytes 221188
  19.5 0.6 %copy-start.12 = (f32[6,24,128]{2,1,0:T(8,128)}, f32[6,24,128]{2,1,0:T(8,128)S(1)}, u32[]{:S(2)}) copy-start(f32[6,24,128]{2,1,0:T(8,128)S(1)} %collective-permute-done.10.refs_15_) | copy-start | bytes 221188
  43.1 1.4 %collective-permute-start.11 = (f32[8,128]{1,0:T(8,128)}, f32[8,128]{1,0:T(8,128)S(1)}, u32[]{:S(2)}, u32[]{:S(2)}) collective-permute-start(f32[8,128]{1,0:T(8,128)} %get-tuple-element.15), channel_id=1, source_target_pairs={{0,1},{1,0},{2,3},{3,2},{4,5},{5,4},{6,7},{7,6},{8,9},{9,8},{10,11... | collective-permute-start | bytes 12296 | tf_op jit(solution)/shard_map/ppermute | solution.py:290
  45.2 3.0 %collective-permute-start.12 = (f32[8,128]{1,0:T(8,128)S(1)}, f32[8,128]{1,0:T(8,128)S(1)}, u32[]{:S(2)}, u32[]{:S(2)}) collective-permute-start(f32[8,128]{1,0:T(8,128)S(1)} %add.17), channel_id=1, source_target_pairs={{0,3},{1,2},{2,1},{3,0},{4,7},{5,6},{6,5},{7,4},{8,11},{9,10},{10,... | collective-permute-start | bytes 12296 | tf_op jit(solution)/shard_map/ppermute | solution.py:290
  48.2 3.0 %collective-permute-start.13 = (f32[8,128]{1,0:T(8,128)S(1)}, f32[8,128]{1,0:T(8,128)S(1)}, u32[]{:S(2)}, u32[]{:S(2)}) collective-permute-start(f32[8,128]{1,0:T(8,128)S(1)} %add.18), channel_id=1, source_target_pairs={{0,5},{1,4},{2,7},{3,6},{4,1},{5,0},{6,3},{7,2},{8,13},{9,12},{10,... | collective-permute-start | bytes 12296 | tf_op jit(solution)/shard_map/ppermute | solution.py:290
  51.3 3.0 %collective-permute-start.14 = (f32[8,128]{1,0:T(8,128)S(1)}, f32[8,128]{1,0:T(8,128)S(1)}, u32[]{:S(2)}, u32[]{:S(2)}) collective-permute-start(f32[8,128]{1,0:T(8,128)S(1)} %add.19), channel_id=1, source_target_pairs={{0,9},{1,8},{2,11},{3,10},{4,13},{5,12},{6,15},{7,14},{8,1},{9,0},... | collective-permute-start | bytes 12296 | tf_op jit(solution)/shard_map/ppermute | solution.py:290
  54.3 4.0 %collective-permute-start.15 = (f32[8,128]{1,0:T(8,128)S(1)}, f32[8,128]{1,0:T(8,128)S(1)}, u32[]{:S(2)}, u32[]{:S(2)}) collective-permute-start(f32[8,128]{1,0:T(8,128)S(1)} %add.20.refs_2_), channel_id=1, source_target_pairs={{0,17},{1,16},{2,19},{3,18},{4,21},{5,20},{6,23},{7,22},{8,25},{9,... | collective-permute-start | bytes 12296 | tf_op jit(solution)/shard_map/ppermute | solution.py:290
  58.3 0.7 %copy-start.1 = (f32[24,128]{1,0:T(8,128)S(1)}, f32[24,128]{1,0:T(8,128)}, u32[]{:S(2)}) copy-start(f32[24,128]{1,0:T(8,128)} %get-tuple-element.14.refs_1_) | copy-start | bytes 36868

commit v6 on v5

--- a/solution.py
+++ b/solution.py
@@ -70,10 +70,12 @@
     return column * leaves + inner - group * leaves
 
 
-def plan_kernel(table, counts, place, basis, near, far, near_slots, far_slots, gram):
+def plan_kernel(table, counts, basis, near, far, near_slots, far_slots, gram):
     krylov, leaves, panels = basis.shape
-    near_slots[...] = slot_of(near[...], table, leaves, place[0], place[1])
-    far_slots[...] = slot_of(far[...], table, leaves, place[0], place[1])
+    me = lax.axis_index("grp")
+    order_low = 2 - lax.rem(lax.axis_index("seg"), 2)
+    near_slots[...] = slot_of(near[...], table, leaves, me, order_low)
+    far_slots[...] = slot_of(far[...], table, leaves, me, order_low)
     live = live_rows(counts, (leaves, panels))
     masked = [basis[j] * live for j in range(krylov)]
     lane = lax.broadcasted_iota(jnp.int32, (krylov, panels), 1)
@@ -95,19 +97,22 @@
 pairs = ((0, 0), (0, 1), (1, 0))
 
 
-def main_kernel(orders, *refs):
+def main_kernel(orders, segments, *refs):
     pieces = len(orders)
-    counts, place, near, far = refs[0:4]
-    blocks = refs[4 : 4 + pieces]
-    classes, m2l_hbm, l2p, basis, gram, image_out, tile_out = refs[4 + pieces : 11 + pieces]
-    m2l, source32, source16, target32, target16 = refs[11 + pieces : 16 + pieces]
-    charge, poles32, taken, sums, totals, found, sem = refs[16 + pieces :]
+    counts, near, far = refs[0:3]
+    blocks = refs[3 : 3 + pieces]
+    classes, m2l_hbm, l2p, basis, gram, image_out, tile_out = refs[3 + pieces : 10 + pieces]
+    m2l, source32, source16, target32, target16 = refs[10 + pieces : 15 + pieces]
+    charge, poles32, taken, sums, totals, found, sem = refs[15 + pieces :]
     krylov, leaves, panels = basis.shape
     terms = l2p.shape[0]
     offsets = m2l.shape[1]
     copy = pltpu.make_async_copy(m2l_hbm, m2l, sem)
     copy.start()
-    inside = place[2].astype(f32)
+    segment = lax.axis_index("seg")
+    low_end = jnp.where(segment >= 2, 1.0, 0.0)
+    high_end = jnp.where(segment < segments - 2, 1.0, 0.0)
+    inside = jnp.where(lax.rem(segment, 2) == 0, low_end, high_end)
 
     ones = jnp.ones((leaves, panels), f32)
     zeros = jnp.zeros((leaves, panels), f32)
@@ -167,7 +172,7 @@
         both = jnp.dot(by_class, pole, preferred_element_type=f32)
         found[leaf] = both[:, 0:panels] + both[:, panels : 2 * panels]
 
-    repeat(leaves, 12, near_body)
+    repeat(leaves, leaves, near_body)
     repeat(leaves, UNROLL, far_gather)
     nearby = jnp.concatenate(
         [jnp.sum(totals[leaf].T, axis=0, keepdims=True) for leaf in range(leaves)], axis=0
@@ -314,12 +319,6 @@
     groups = lax.axis_size("grp")
     params = pltpu.CompilerParams(vmem_limit_bytes=LIMIT)
     small = pltpu.CompilerParams(vmem_limit_bytes=LIMIT // 8)
-    here = lax.axis_index("seg")
-    odd = here % 2
-    order_low = 2 - odd
-    inside = jnp.where(odd == 0, here >= 2, here < lax.axis_size("seg") - 2)
-    position = jnp.stack([lax.axis_index("grp"), order_low, inside]).astype(jnp.int32)
-
     block = pl.pallas_call(
         prep_kernel,
         out_shape=jax.ShapeDtypeStruct((6, leaves, panels), f32),
@@ -357,11 +356,11 @@
             jax.ShapeDtypeStruct(far_list.shape, jnp.int32),
             jax.ShapeDtypeStruct((krylov, panels), f32),
         ),
-        in_specs=smem(2) + vmem(3),
+        in_specs=smem(1) + vmem(3),
         out_specs=tuple(vmem(3)),
         compiler_params=params,
         name="plan",
-    )(counts, position, basis, near_list, far_list)
+    )(counts, basis, near_list, far_list)
 
     beside, near_slots = lax.optimization_barrier((beside, near_slots))
     beyond = hop(beside)
@@ -369,12 +368,12 @@
     pieces = pieces + [swap(v, 0, 1) for v in pieces]
 
     image, tile = pl.pallas_call(
-        functools.partial(main_kernel, [order for order, _ in keys]),
+        functools.partial(main_kernel, [order for order, _ in keys], lax.axis_size("seg")),
         out_shape=(
             jax.ShapeDtypeStruct((leaves, panels), f32),
             jax.ShapeDtypeStruct((krylov, panels), f32),
         ),
-        in_specs=smem(4) + vmem(len(pieces) + 1) + anywhere(1) + vmem(3),
+        in_specs=smem(3) + vmem(len(pieces) + 1) + anywhere(1) + vmem(3),
         out_specs=tuple(vmem(2)),
         scratch_shapes=[
             pltpu.VMEM(m2l.shape, bf16),
@@ -393,7 +392,7 @@
         compiler_params=params,
         name="main",
     )(
-        counts, position, near_slots, far_slots,
+        counts, near_slots, far_slots,
         *pieces, far_offset, m2l, l2p, basis, gram,
     )
 

time: 60.6 us -> 60.1 us (level)
  waiting for transfers between devices: 11 us -> 11.8 us
  other arithmetic: 1.31 us -> 0.69 us
    ppermute x16, waiting for transfers between devices: 11 us -> 11.8 us  [move(): return lax.ppermute(value, ('seg', 'grp'), moves)]
    another operation x1 -> x0, other arithmetic: 0.61 us -> none  [on_device(): jnp.stack([lax.axis_index('grp'), order_low, inside]).astype(jnp.int32)]
  transfers between devices with their start and end apart: 16 -> 16, of which waited for: 9 -> 8; matrix products, arithmetic and copies ran while one was open for 1% -> 0% of each run, Pallas kernels for 3% -> 3%
where the time goes in v6:
time: 60.1 us; the launch traced here: 59.8 us
  Pallas kernels  27.7 us (46%)
  starting transfers between devices  16.6 us (28%)
  waiting for transfers between devices  11.8 us (20%)
  between operations  1.62 us (3%)
  local copies, waits for them, and re-layouts  1.31 us (2%)
  other arithmetic  0.69 us (1%)
    pallas_call x1, Pallas kernels, on_device(): pl.pallas_call(functools.partial(main_kernel, [order for order, _ in keys...  22.7 us
    ppermute x16, starting transfers between devices, move(): return lax.ppermute(value, ('seg', 'grp'), moves)  16.6 us
    ppermute x16, waiting for transfers between devices, move(): return lax.ppermute(value, ('seg', 'grp'), moves)  11.8 us
    pallas_call x1, Pallas kernels, on_device(): pl.pallas_call(prep_kernel, out_shape=jax.ShapeDtypeStruct((6, leaves, pa...  2.3 us
    pallas_call x1, Pallas kernels, on_device(): pl.pallas_call(functools.partial(plan_kernel, table), out_shape=(jax.Shap...  1.65 us
    unnamed x26, local copies, waits for them, and re-layouts  1.31 us
  transfers between devices with their start and end apart: 16, of which 8 were waited for; matrix products, arithmetic and copies ran while one was open for 0% of the time, Pallas kernels for 3%

profile of v6, /device:TPU:0, one launch (start us, length us, event | category | flops | bytes accessed | tf_op | source)
XLA Modules:
  0.0 59.8 jit_solution(15360273906133031499)
XLA Ops:
  0.6 0.0 copy-start
  1.3 2.3 %prep.1.refs_3_ = f32[6,24,128]{2,1,0:T(8,128)} custom-call(s32[1]{0:T(128)S(6)} %copy.12.counts.refs_0_, f32[8,24,128]{2,1,0:T(8,128)} %refs_0_.2, f32[3,24,128]{2,1,0:T(8,128)} %bitcast.7, f32[24,128]{1,0:T(8,128)} %areas.1, bf16[121,24,128]{2,1,0:T(8,128)(2,1)} %bitcast.5), custom_call_target="tpu_custom_call" | custom-call | tf_op jit(solution)/shard_map/prep/pallas_call | solution.py:322
  3.6 2.4 %collective-permute-start = (f32[6,24,128]{2,1,0:T(8,128)}, f32[6,24,128]{2,1,0:T(8,128)S(1)}, u32[]{:S(2)}, u32[]{:S(2)}) collective-permute-start(f32[6,24,128]{2,1,0:T(8,128)} %prep.1.refs_3_), channel_id=1, source_target_pairs={{0,5},{1,4},{2,7},{3,6},{4,1},{5,0},{6,3},{7,2},{8,13},{9,12},{10,... | collective-permute-start | bytes 221192 | tf_op jit(solution)/shard_map/ppermute | solution.py:295
  6.0 1.8 %collective-permute-start.1 = (f32[6,24,128]{2,1,0:T(8,128)}, f32[6,24,128]{2,1,0:T(8,128)S(1)}, u32[]{:S(2)}, u32[]{:S(2)}) collective-permute-start(f32[6,24,128]{2,1,0:T(8,128)} %prep.1.refs_3_), channel_id=1, source_target_pairs={{0,3},{1,2},{2,1},{3,0},{4,7},{5,6},{6,5},{7,4},{8,11},{9,10},{10,... | collective-permute-start | bytes 221192 | tf_op jit(solution)/shard_map/ppermute | solution.py:295
  7.8 1.6 %plan.1 = (s32[24,27]{1,0:T(8,128)}, s32[24,189]{1,0:T(8,128)}, f32[8,128]{1,0:T(8,128)}) custom-call(s32[1]{0:T(128)S(6)} %copy.12.counts.refs_0_, f32[8,24,128]{2,1,0:T(8,128)} %refs_0_.2, s32[24,27]{1,0:T(8,128)} %near.1, s32[24,189]{1,0:T(8,128)} %far.1), custom_call_target="tpu_custom_call" | custom-call | tf_op jit(solution)/shard_map/plan/pallas_call | solution.py:352
  9.5 0.0 collective-permute-done.refs_5_
  9.5 1.7 %collective-permute-start.3 = (f32[6,24,128]{2,1,0:T(8,128)S(1)}, f32[6,24,128]{2,1,0:T(8,128)S(1)}, u32[]{:S(2)}, u32[]{:S(2)}) collective-permute-start(f32[6,24,128]{2,1,0:T(8,128)S(1)} %collective-permute-done.refs_5_), channel_id=1, source_target_pairs={{0,9},{1,8},{2,11},{3,10},{4,1},{5,0},{6,3},{7,2},{8,17},{9,16},{1... | collective-permute-start | bytes 221192 | tf_op jit(solution)/shard_map/ppermute | solution.py:295
  11.2 0.3 collective-permute-start.5
  11.5 2.3 %collective-permute-done.3.refs_7_ = f32[6,24,128]{2,1,0:T(8,128)S(1)} collective-permute-done((f32[6,24,128]{2,1,0:T(8,128)S(1)}, f32[6,24,128]{2,1,0:T(8,128)S(1)}, u32[]{:S(2)}, u32[]{:S(2)}) %collective-permute-start.3) | collective-permute-done | bytes 73760 | tf_op jit(solution)/shard_map/ppermute | solution.py:295
  13.7 1.5 %collective-permute-start.4 = (f32[6,24,128]{2,1,0:T(8,128)S(1)}, f32[6,24,128]{2,1,0:T(8,128)S(1)}, u32[]{:S(2)}, u32[]{:S(2)}) collective-permute-start(f32[6,24,128]{2,1,0:T(8,128)S(1)} %collective-permute-done.3.refs_7_), channel_id=1, source_target_pairs={{0,3},{1,2},{2,1},{3,0},{4,7},{5,6},{6,5},{7,4},{8,11},{9,10},{10,... | collective-permute-start | bytes 221192 | tf_op jit(solution)/shard_map/ppermute | solution.py:295
  15.3 0.4 collective-permute-start.7
  15.7 0.1 collective-permute-start.6
  15.8 0.4 collective-permute-start.9
  16.2 0.1 collective-permute-start.8
  16.3 1.7 %collective-permute-done.4.refs_8_ = f32[6,24,128]{2,1,0:T(8,128)S(1)} collective-permute-done((f32[6,24,128]{2,1,0:T(8,128)S(1)}, f32[6,24,128]{2,1,0:T(8,128)S(1)}, u32[]{:S(2)}, u32[]{:S(2)}) %collective-permute-start.4) | collective-permute-done | bytes 73760 | tf_op jit(solution)/shard_map/ppermute | solution.py:295
  18.0 0.1 collective-permute-start.10
  18.2 1.1 %collective-permute-done.10.refs_14_ = f32[6,24,128]{2,1,0:T(8,128)S(1)} collective-permute-done((f32[6,24,128]{2,1,0:T(8,128)S(1)}, f32[6,24,128]{2,1,0:T(8,128)S(1)}, u32[]{:S(2)}, u32[]{:S(2)}) %collective-permute-start.10) | collective-permute-done | bytes 73760 | tf_op jit(solution)/shard_map/ppermute | solution.py:295
  19.4 0.6 copy-done.12
  19.9 22.7 %main.1 = (f32[24,128]{1,0:T(8,128)}, f32[8,128]{1,0:T(8,128)}) custom-call(s32[1]{0:T(128)S(6)} %copy.12.counts.refs_0_, s32[24,27]{1,0:T(8,128)} %get-tuple-element.10.refs_1_, s32[24,189]{1,0:T(8,128)} %get-tuple-element.11.refs_2_, f32[6,24,128]{2,1,0:T(8,128)} %prep.1.refs_3_, f32[6,24,128]{2,1,0:T(8,128)} %copy-done.3, f32[6,24,128]{2,1,0:T(8,128)} %copy-done.2, ...), custom_call_target="tpu_custom_call" | custom-call | tf_op jit(solution)/shard_map/main/pallas_call | solution.py:370
  42.6 0.2 collective-permute-start.11
  42.8 1.2 %collective-permute-done.11 = f32[8,128]{1,0:T(8,128)S(1)} collective-permute-done((f32[8,128]{1,0:T(8,128)}, f32[8,128]{1,0:T(8,128)S(1)}, u32[]{:S(2)}, u32[]{:S(2)}) %collective-permute-start.11) | collective-permute-done | bytes 4128 | tf_op jit(solution)/shard_map/ppermute | solution.py:295
  44.0 0.7 %add.12 = f32[8,128]{1,0:T(8,128)S(1)} add(f32[8,128]{1,0:T(8,128)} %get-tuple-element.15, f32[8,128]{1,0:T(8,128)S(1)} %collective-permute-done.11) | non-fusion elementwise | flops 1024 | bytes 12288 | tf_op jit(solution)/shard_map/add | solution.py:405
  44.7 1.6 %collective-permute-start.12 = (f32[8,128]{1,0:T(8,128)S(1)}, f32[8,128]{1,0:T(8,128)S(1)}, u32[]{:S(2)}, u32[]{:S(2)}) collective-permute-start(f32[8,128]{1,0:T(8,128)S(1)} %add.12), channel_id=1, source_target_pairs={{0,3},{1,2},{2,1},{3,0},{4,7},{5,6},{6,5},{7,4},{8,11},{9,10},{10,... | collective-permute-start | bytes 12296 | tf_op jit(solution)/shard_map/ppermute | solution.py:295
  46.3 1.5 %collective-permute-done.12 = f32[8,128]{1,0:T(8,128)S(1)} collective-permute-done((f32[8,128]{1,0:T(8,128)S(1)}, f32[8,128]{1,0:T(8,128)S(1)}, u32[]{:S(2)}, u32[]{:S(2)}) %collective-permute-start.12) | collective-permute-done | bytes 4128 | tf_op jit(solution)/shard_map/ppermute | solution.py:295
  47.8 1.6 %collective-permute-start.13 = (f32[8,128]{1,0:T(8,128)S(1)}, f32[8,128]{1,0:T(8,128)S(1)}, u32[]{:S(2)}, u32[]{:S(2)}) collective-permute-start(f32[8,128]{1,0:T(8,128)S(1)} %add.13), channel_id=1, source_target_pairs={{0,5},{1,4},{2,7},{3,6},{4,1},{5,0},{6,3},{7,2},{8,13},{9,12},{10,... | collective-permute-start | bytes 12296 | tf_op jit(solution)/shard_map/ppermute | solution.py:295
  49.4 1.4 %collective-permute-done.13 = f32[8,128]{1,0:T(8,128)S(1)} collective-permute-done((f32[8,128]{1,0:T(8,128)S(1)}, f32[8,128]{1,0:T(8,128)S(1)}, u32[]{:S(2)}, u32[]{:S(2)}) %collective-permute-start.13) | collective-permute-done | bytes 4128 | tf_op jit(solution)/shard_map/ppermute | solution.py:295
  50.8 1.7 %collective-permute-start.14 = (f32[8,128]{1,0:T(8,128)S(1)}, f32[8,128]{1,0:T(8,128)S(1)}, u32[]{:S(2)}, u32[]{:S(2)}) collective-permute-start(f32[8,128]{1,0:T(8,128)S(1)} %add.14), channel_id=1, source_target_pairs={{0,9},{1,8},{2,11},{3,10},{4,13},{5,12},{6,15},{7,14},{8,1},{9,0},... | collective-permute-start | bytes 12296 | tf_op jit(solution)/shard_map/ppermute | solution.py:295
  52.5 1.4 %collective-permute-done.14 = f32[8,128]{1,0:T(8,128)S(1)} collective-permute-done((f32[8,128]{1,0:T(8,128)S(1)}, f32[8,128]{1,0:T(8,128)S(1)}, u32[]{:S(2)}, u32[]{:S(2)}) %collective-permute-start.14) | collective-permute-done | bytes 4128 | tf_op jit(solution)/shard_map/ppermute | solution.py:295
  53.8 2.7 %collective-permute-start.15 = (f32[8,128]{1,0:T(8,128)S(1)}, f32[8,128]{1,0:T(8,128)S(1)}, u32[]{:S(2)}, u32[]{:S(2)}) collective-permute-start(f32[8,128]{1,0:T(8,128)S(1)} %add.15.refs_2_), channel_id=1, source_target_pairs={{0,17},{1,16},{2,19},{3,18},{4,21},{5,20},{6,23},{7,22},{8,25},{9,... | collective-permute-start | bytes 12296 | tf_op jit(solution)/shard_map/ppermute | solution.py:295
  56.5 1.3 %collective-permute-done.15.refs_3_ = f32[8,128]{1,0:T(8,128)S(1)} collective-permute-done((f32[8,128]{1,0:T(8,128)S(1)}, f32[8,128]{1,0:T(8,128)S(1)}, u32[]{:S(2)}, u32[]{:S(2)}) %collective-permute-start.15) | collective-permute-done | bytes 4128 | tf_op jit(solution)/shard_map/ppermute | solution.py:295
  57.9 0.7 %copy-done.1 = f32[24,128]{1,0:T(8,128)S(1)} copy-done((f32[24,128]{1,0:T(8,128)S(1)}, f32[24,128]{1,0:T(8,128)}, u32[]{:S(2)}) %copy-start.1) | copy-done | bytes 12312
  58.6 1.1 %final.1 = (f32[24,128]{1,0:T(8,128)}, f32[9]{0:T(128)}) custom-call(s32[1]{0:T(128)S(6)} %copy.12.counts.refs_0_, f32[8,24,128]{2,1,0:T(8,128)S(1)} %copy-done, f32[24,128]{1,0:T(8,128)S(1)} %copy-done.1, f32[8,128]{1,0:T(8,128)S(1)} %add.15.refs_2_, f32[8,128]{1,0:T(8,128)S(1)} %collective-permute-done.15.refs_3_), custom_call_target="tpu_custom_call" | custom-call | tf_op jit(solution)/shard_map/final/pallas_call | solution.py:408
  (34 shorter events, 0.1 us)
Async XLA Ops:
  0.6 57.2 %copy-start = (f32[8,24,128]{2,1,0:T(8,128)S(1)}, f32[8,24,128]{2,1,0:T(8,128)}, u32[]{:S(2)}) copy-start(f32[8,24,128]{2,1,0:T(8,128)} %refs_0_.2) | copy-start | bytes 294916
  3.6 5.8 %collective-permute-start = (f32[6,24,128]{2,1,0:T(8,128)}, f32[6,24,128]{2,1,0:T(8,128)S(1)}, u32[]{:S(2)}, u32[]{:S(2)}) collective-permute-start(f32[6,24,128]{2,1,0:T(8,128)} %prep.1.refs_3_), channel_id=1, source_target_pairs={{0,5},{1,4},{2,7},{3,6},{4,1},{5,0},{6,3},{7,2},{8,13},{9,12},{10,... | collective-permute-start | bytes 221192 | tf_op jit(solution)/shard_map/ppermute | solution.py:295
  6.0 5.4 %collective-permute-start.1 = (f32[6,24,128]{2,1,0:T(8,128)}, f32[6,24,128]{2,1,0:T(8,128)S(1)}, u32[]{:S(2)}, u32[]{:S(2)}) collective-permute-start(f32[6,24,128]{2,1,0:T(8,128)} %prep.1.refs_3_), channel_id=1, source_target_pairs={{0,3},{1,2},{2,1},{3,0},{4,7},{5,6},{6,5},{7,4},{8,11},{9,10},{10,... | collective-permute-start | bytes 221192 | tf_op jit(solution)/shard_map/ppermute | solution.py:295
  9.5 9.8 %copy-start.2 = (f32[6,24,128]{2,1,0:T(8,128)}, f32[6,24,128]{2,1,0:T(8,128)S(1)}, u32[]{:S(2)}) copy-start(f32[6,24,128]{2,1,0:T(8,128)S(1)} %collective-permute-done.refs_5_) | copy-start | bytes 221188
  9.5 4.3 %collective-permute-start.3 = (f32[6,24,128]{2,1,0:T(8,128)S(1)}, f32[6,24,128]{2,1,0:T(8,128)S(1)}, u32[]{:S(2)}, u32[]{:S(2)}) collective-permute-start(f32[6,24,128]{2,1,0:T(8,128)S(1)} %collective-permute-done.refs_5_), channel_id=1, source_target_pairs={{0,9},{1,8},{2,11},{3,10},{4,1},{5,0},{6,3},{7,2},{8,17},{9,16},{1... | collective-permute-start | bytes 221192 | tf_op jit(solution)/shard_map/ppermute | solution.py:295
  11.2 4.7 %collective-permute-start.5 = (f32[6,24,128]{2,1,0:T(8,128)}, f32[6,24,128]{2,1,0:T(8,128)S(1)}, u32[]{:S(2)}, u32[]{:S(2)}) collective-permute-start(f32[6,24,128]{2,1,0:T(8,128)} %prep.1.refs_3_), channel_id=1, source_target_pairs={{0,1},{1,0},{2,3},{3,2},{4,5},{5,4},{6,7},{7,6},{8,9},{9,8},{10,11... | collective-permute-start | bytes 221192 | tf_op jit(solution)/shard_map/ppermute | solution.py:295
  11.5 7.8 %copy-start.3 = (f32[6,24,128]{2,1,0:T(8,128)}, f32[6,24,128]{2,1,0:T(8,128)S(1)}, u32[]{:S(2)}) copy-start(f32[6,24,128]{2,1,0:T(8,128)S(1)} %collective-permute-done.1.refs_4_) | copy-start | bytes 221188
  11.5 4.7 %collective-permute-start.2 = (f32[6,24,128]{2,1,0:T(8,128)S(1)}, f32[6,24,128]{2,1,0:T(8,128)S(1)}, u32[]{:S(2)}, u32[]{:S(2)}) collective-permute-start(f32[6,24,128]{2,1,0:T(8,128)S(1)} %collective-permute-done.1.refs_4_), channel_id=1, source_target_pairs={{0,5},{1,4},{2,7},{3,6},{4,1},{5,0},{6,3},{7,2},{8,13},{9,12},{10,... | collective-permute-start | bytes 221192 | tf_op jit(solution)/shard_map/ppermute | solution.py:295
  13.7 5.6 %copy-start.4 = (f32[6,24,128]{2,1,0:T(8,128)}, f32[6,24,128]{2,1,0:T(8,128)S(1)}, u32[]{:S(2)}) copy-start(f32[6,24,128]{2,1,0:T(8,128)S(1)} %collective-permute-done.3.refs_7_) | copy-start | bytes 221188
  13.7 4.3 %collective-permute-start.4 = (f32[6,24,128]{2,1,0:T(8,128)S(1)}, f32[6,24,128]{2,1,0:T(8,128)S(1)}, u32[]{:S(2)}, u32[]{:S(2)}) collective-permute-start(f32[6,24,128]{2,1,0:T(8,128)S(1)} %collective-permute-done.3.refs_7_), channel_id=1, source_target_pairs={{0,3},{1,2},{2,1},{3,0},{4,7},{5,6},{6,5},{7,4},{8,11},{9,10},{10,... | collective-permute-start | bytes 221192 | tf_op jit(solution)/shard_map/ppermute | solution.py:295
  15.3 2.9 %collective-permute-start.7 = (f32[6,24,128]{2,1,0:T(8,128)S(1)}, f32[6,24,128]{2,1,0:T(8,128)S(1)}, u32[]{:S(2)}, u32[]{:S(2)}) collective-permute-start(f32[6,24,128]{2,1,0:T(8,128)S(1)} %collective-permute-done.refs_5_), channel_id=1, source_target_pairs={{0,1},{1,0},{2,3},{3,2},{4,5},{5,4},{6,7},{7,6},{8,9},{9,8},{10,11... | collective-permute-start | bytes 221192 | tf_op jit(solution)/shard_map/ppermute | solution.py:295
  15.7 2.5 %collective-permute-start.6 = (f32[6,24,128]{2,1,0:T(8,128)S(1)}, f32[6,24,128]{2,1,0:T(8,128)S(1)}, u32[]{:S(2)}, u32[]{:S(2)}) collective-permute-start(f32[6,24,128]{2,1,0:T(8,128)S(1)} %collective-permute-done.1.refs_4_), channel_id=1, source_target_pairs={{0,1},{1,0},{2,3},{3,2},{4,5},{5,4},{6,7},{7,6},{8,9},{9,8},{10,11... | collective-permute-start | bytes 221192 | tf_op jit(solution)/shard_map/ppermute | solution.py:295
  15.8 3.5 %copy-start.5 = (f32[6,24,128]{2,1,0:T(8,128)}, f32[6,24,128]{2,1,0:T(8,128)S(1)}, u32[]{:S(2)}) copy-start(f32[6,24,128]{2,1,0:T(8,128)S(1)} %collective-permute-done.5.refs_9_) | copy-start | bytes 221188
  15.8 2.4 %collective-permute-start.9 = (f32[6,24,128]{2,1,0:T(8,128)S(1)}, f32[6,24,128]{2,1,0:T(8,128)S(1)}, u32[]{:S(2)}, u32[]{:S(2)}) collective-permute-start(f32[6,24,128]{2,1,0:T(8,128)S(1)} %collective-permute-done.3.refs_7_), channel_id=1, source_target_pairs={{0,1},{1,0},{2,3},{3,2},{4,5},{5,4},{6,7},{7,6},{8,9},{9,8},{10,11... | collective-permute-start | bytes 221192 | tf_op jit(solution)/shard_map/ppermute | solution.py:295
  16.2 3.1 %copy-start.6 = (f32[6,24,128]{2,1,0:T(8,128)}, f32[6,24,128]{2,1,0:T(8,128)S(1)}, u32[]{:S(2)}) copy-start(f32[6,24,128]{2,1,0:T(8,128)S(1)} %collective-permute-done.2.refs_6_) | copy-start | bytes 221188
  16.2 2.0 %collective-permute-start.8 = (f32[6,24,128]{2,1,0:T(8,128)S(1)}, f32[6,24,128]{2,1,0:T(8,128)S(1)}, u32[]{:S(2)}, u32[]{:S(2)}) collective-permute-start(f32[6,24,128]{2,1,0:T(8,128)S(1)} %collective-permute-done.2.refs_6_), channel_id=1, source_target_pairs={{0,1},{1,0},{2,3},{3,2},{4,5},{5,4},{6,7},{7,6},{8,9},{9,8},{10,11... | collective-permute-start | bytes 221192 | tf_op jit(solution)/shard_map/ppermute | solution.py:295
  18.0 1.3 %copy-start.7 = (f32[6,24,128]{2,1,0:T(8,128)}, f32[6,24,128]{2,1,0:T(8,128)S(1)}, u32[]{:S(2)}) copy-start(f32[6,24,128]{2,1,0:T(8,128)S(1)} %collective-permute-done.4.refs_8_) | copy-start | bytes 221188
  18.0 1.3 %collective-permute-start.10 = (f32[6,24,128]{2,1,0:T(8,128)S(1)}, f32[6,24,128]{2,1,0:T(8,128)S(1)}, u32[]{:S(2)}, u32[]{:S(2)}) collective-permute-start(f32[6,24,128]{2,1,0:T(8,128)S(1)} %collective-permute-done.4.refs_8_), channel_id=1, source_target_pairs={{0,1},{1,0},{2,3},{3,2},{4,5},{5,4},{6,7},{7,6},{8,9},{9,8},{10,11... | collective-permute-start | bytes 221192 | tf_op jit(solution)/shard_map/ppermute | solution.py:295
  18.1 1.2 %copy-start.9 = (f32[6,24,128]{2,1,0:T(8,128)}, f32[6,24,128]{2,1,0:T(8,128)S(1)}, u32[]{:S(2)}) copy-start(f32[6,24,128]{2,1,0:T(8,128)S(1)} %collective-permute-done.6.refs_10_) | copy-start | bytes 221188
  18.2 1.2 %copy-start.8 = (f32[6,24,128]{2,1,0:T(8,128)}, f32[6,24,128]{2,1,0:T(8,128)S(1)}, u32[]{:S(2)}) copy-start(f32[6,24,128]{2,1,0:T(8,128)S(1)} %collective-permute-done.7.refs_11_) | copy-start | bytes 221188
  18.2 1.2 %copy-start.11 = (f32[6,24,128]{2,1,0:T(8,128)}, f32[6,24,128]{2,1,0:T(8,128)S(1)}, u32[]{:S(2)}) copy-start(f32[6,24,128]{2,1,0:T(8,128)S(1)} %collective-permute-done.8.refs_12_) | copy-start | bytes 221188
  18.2 1.2 %copy-start.10 = (f32[6,24,128]{2,1,0:T(8,128)}, f32[6,24,128]{2,1,0:T(8,128)S(1)}, u32[]{:S(2)}) copy-start(f32[6,24,128]{2,1,0:T(8,128)S(1)} %collective-permute-done.9.refs_13_) | copy-start | bytes 221188
  19.3 0.6 %copy-start.12 = (f32[6,24,128]{2,1,0:T(8,128)}, f32[6,24,128]{2,1,0:T(8,128)S(1)}, u32[]{:S(2)}) copy-start(f32[6,24,128]{2,1,0:T(8,128)S(1)} %collective-permute-done.10.refs_14_) | copy-start | bytes 221188
  42.6 1.4 %collective-permute-start.11 = (f32[8,128]{1,0:T(8,128)}, f32[8,128]{1,0:T(8,128)S(1)}, u32[]{:S(2)}, u32[]{:S(2)}) collective-permute-start(f32[8,128]{1,0:T(8,128)} %get-tuple-element.15), channel_id=1, source_target_pairs={{0,1},{1,0},{2,3},{3,2},{4,5},{5,4},{6,7},{7,6},{8,9},{9,8},{10,11... | collective-permute-start | bytes 12296 | tf_op jit(solution)/shard_map/ppermute | solution.py:295
  44.7 3.0 %collective-permute-start.12 = (f32[8,128]{1,0:T(8,128)S(1)}, f32[8,128]{1,0:T(8,128)S(1)}, u32[]{:S(2)}, u32[]{:S(2)}) collective-permute-start(f32[8,128]{1,0:T(8,128)S(1)} %add.12), channel_id=1, source_target_pairs={{0,3},{1,2},{2,1},{3,0},{4,7},{5,6},{6,5},{7,4},{8,11},{9,10},{10,... | collective-permute-start | bytes 12296 | tf_op jit(solution)/shard_map/ppermute | solution.py:295
  47.8 3.0 %collective-permute-start.13 = (f32[8,128]{1,0:T(8,128)S(1)}, f32[8,128]{1,0:T(8,128)S(1)}, u32[]{:S(2)}, u32[]{:S(2)}) collective-permute-start(f32[8,128]{1,0:T(8,128)S(1)} %add.13), channel_id=1, source_target_pairs={{0,5},{1,4},{2,7},{3,6},{4,1},{5,0},{6,3},{7,2},{8,13},{9,12},{10,... | collective-permute-start | bytes 12296 | tf_op jit(solution)/shard_map/ppermute | solution.py:295
  50.8 3.0 %collective-permute-start.14 = (f32[8,128]{1,0:T(8,128)S(1)}, f32[8,128]{1,0:T(8,128)S(1)}, u32[]{:S(2)}, u32[]{:S(2)}) collective-permute-start(f32[8,128]{1,0:T(8,128)S(1)} %add.14), channel_id=1, source_target_pairs={{0,9},{1,8},{2,11},{3,10},{4,13},{5,12},{6,15},{7,14},{8,1},{9,0},... | collective-permute-start | bytes 12296 | tf_op jit(solution)/shard_map/ppermute | solution.py:295
  53.8 4.0 %collective-permute-start.15 = (f32[8,128]{1,0:T(8,128)S(1)}, f32[8,128]{1,0:T(8,128)S(1)}, u32[]{:S(2)}, u32[]{:S(2)}) collective-permute-start(f32[8,128]{1,0:T(8,128)S(1)} %add.15.refs_2_), channel_id=1, source_target_pairs={{0,17},{1,16},{2,19},{3,18},{4,21},{5,20},{6,23},{7,22},{8,25},{9,... | collective-permute-start | bytes 12296 | tf_op jit(solution)/shard_map/ppermute | solution.py:295
  57.8 0.7 %copy-start.1 = (f32[24,128]{1,0:T(8,128)S(1)}, f32[24,128]{1,0:T(8,128)}, u32[]{:S(2)}) copy-start(f32[24,128]{1,0:T(8,128)} %get-tuple-element.14.refs_1_) | copy-start | bytes 36868
